TPU v7x, 32 devices: a whole 2x2x4 slice. The times are simulated.
32 devices in a mesh: row: 8 (over y, x, core), col: 4 (over z).
Axes of the slice: x: 2, y: 2, z: 4, core: 2. Of those that a mesh axis runs over, the one named last changes fastest.
Arguments:
- anc_inverse: float32 [4096, 4096], P('row', 'col')
- off_factor: float32 [2, 4096, 4096], P(None, 'row', 'col'), may hold values from -0.09375 to 0.09375
- diag_inverse: float32 [2, 4096, 4096], P(None, 'row', 'col')
- block_mask: int32 [2, 32], P(None, 'row'), may hold values 0 or 1
- edge_child: int32 [2, 8192], P(None, ('row', 'col')), may hold values from 0 to 4095, as said below
- edge_other: int32 [2, 8192], P(None, ('row', 'col')), may hold values from 0 to 8191, as said below
Outputs:
- off_inverse: float32 [2, 4096, 4096], P(None, 'row', 'col')
- diag_part: float32 [2, 4096, 4096], P(None, 'row', 'col')
- resist: float32 [2, 8192], P(None, ('row', 'col'))
Inputs may be any that keep to these rules, and one draw needn't show every extreme that they name: `edge_child`: edges come in runs of 256; run d, with c = d % 4, has u in [c * 4096 / 4, (c + 1) * 4096 / 4). `edge_other`: in run d of 256 edges, with r = d // 4, v lies in [r * 4096 / 8, (r + 1) * 4096 / 8) or in 4096 + [r * 4096 / 8, (r + 1) * 4096 / 8); v never equals u.
All inputs are finite; a program needn't handle non-finite values. No bound on the sum of `block_mask` on one device may be relied on, other than what follows from the above.
Results may differ from a plain program's by a relative error of at most 0.000073.
Values sent between devices are 32-bit elements; how exact they have to be, the bound alone decides.
No kernel may reach another device: no remote copies, remote signals or barrier semaphores. Data moves between devices by JAX's collectives and lax.ppermute only.
A program may use at most 128 MiB of HBM per device.

v0:
```python
import jax
import jax.numpy as jnp
from jax import lax
from jax.sharding import PartitionSpec as P


def scatter_form(off_rows, factor, diag_inverse):
    fronts, anc_rows, col_width = factor.shape
    diag_rows = diag_inverse.shape[1]
    highest = lax.Precision.HIGHEST
    product = jnp.einsum("kaj,kai->jki", off_rows, factor, precision=highest)
    summed = lax.psum_scatter(
        product.reshape(diag_rows * lax.axis_size("row"), fronts * col_width),
        "row",
        scatter_dimension=0,
        tiled=True,
    )
    return diag_inverse - jnp.transpose(summed.reshape(diag_rows, fronts, col_width), (1, 0, 2))


def per_device(anc_inverse, off_factor, diag_inverse, block_mask, edge_child, edge_other):
    fronts, anc_rows, col_width = off_factor.shape
    diag_rows = diag_inverse.shape[1]
    anc_cols = anc_inverse.shape[1]
    row_id = lax.axis_index("row")
    col_id = lax.axis_index("col")
    highest = lax.Precision.HIGHEST
    block_rows = anc_rows // block_mask.shape[1]
    keep = jnp.repeat(block_mask, block_rows, axis=1).astype(jnp.float32)
    factor = off_factor * keep[:, :, None]
    empty = jnp.zeros((fronts, anc_rows, col_width), jnp.float32)
    whole_rows = lax.all_gather(anc_inverse, "col", axis=1, tiled=True)
    off_inverse = empty - jnp.einsum(
        "ab,kbi->kai",
        whole_rows,
        lax.all_gather(factor, "row", axis=1, tiled=True),
        precision=highest,
    )
    supercols = col_width * lax.axis_size("col")
    ancestor = anc_cols * lax.axis_size("col")
    off_rows = lax.all_gather(off_inverse, "col", axis=2, tiled=True)
    diag_part = scatter_form(off_rows, factor, diag_inverse)
    row_global = row_id * diag_rows + jnp.arange(diag_rows, dtype=jnp.int32)
    col_global = col_id * col_width + jnp.arange(col_width, dtype=jnp.int32)
    hit = (row_global[:, None] == col_global[None, :]).astype(jnp.float32)
    cc_local = jnp.sum(diag_part * hit[None], axis=1)
    anc_row_global = row_id * anc_rows + jnp.arange(anc_rows, dtype=jnp.int32)
    anc_col_global = col_id * anc_cols + jnp.arange(anc_cols, dtype=jnp.int32)
    anc_hit = (anc_row_global[:, None] == anc_col_global[None, :]).astype(jnp.float32)
    z_local = jnp.sum(anc_inverse * anc_hit, axis=0)
    cc_place = lax.dynamic_update_slice_in_dim(
        jnp.zeros((fronts, supercols), jnp.float32), cc_local, col_id * col_width, 1
    )
    z_place = lax.dynamic_update_slice_in_dim(
        jnp.zeros((ancestor,), jnp.float32), z_local, col_id * anc_cols, 0
    )
    cc_diag, z_diag = lax.psum((cc_place, z_place), ("row", "col"))
    is_child = edge_other < supercols
    local_near = jnp.clip(edge_child - col_id * col_width, 0, col_width - 1)
    child_row = jnp.clip(edge_other - row_id * diag_rows, 0, diag_rows - 1)
    anc_row = jnp.clip(edge_other - supercols - row_id * anc_rows, 0, anc_rows - 1)
    flat_diag = diag_part.reshape(fronts, diag_rows * col_width)
    flat_off = off_inverse.reshape(fronts, anc_rows * col_width)
    mixed = jnp.where(
        is_child,
        jnp.take_along_axis(flat_diag, child_row * col_width + local_near, axis=1),
        jnp.take_along_axis(flat_off, anc_row * col_width + local_near, axis=1),
    )
    child_end = jnp.clip(edge_other, 0, supercols - 1)
    anc_end = jnp.clip(edge_other - supercols, 0, ancestor - 1)
    near = jnp.take_along_axis(cc_diag, edge_child, axis=1)
    far = jnp.where(is_child, jnp.take_along_axis(cc_diag, child_end, axis=1), z_diag[anc_end])
    resist = near + far - 2.0 * mixed
    return (off_inverse, diag_part, resist)


def solution(mesh):
    placed = (
        P("row", "col"),
        P(None, "row", "col"),
        P(None, "row", "col"),
        P(None, "row"),
        P(None, ("row", "col")),
        P(None, ("row", "col")),
    )
    return jax.shard_map(
        per_device,
        mesh=mesh,
        in_specs=placed,
        out_specs=(P(None, "row", "col"), P(None, "row", "col"), P(None, ("row", "col"))),
        check_vma=False,
    )
```

profile of v0, /device:TPU:0, one launch (start us, length us, event | category | flops | bytes accessed | tf_op | source)
XLA Modules:
  0.0 1020.2 jit_solution(2937164954265021883)
XLA Ops:
  7.2 0.0 all-gather.6.cloned.1.call-start
  7.2 0.7 all-gather.6.cloned.1.call-update
  7.9 0.0 all-gather.4.cloned.1.call-start
  8.0 5.4 copy.12
  13.3 0.1 broadcast_bitcast_fusion
  13.4 4.7 broadcast_multiply_fusion
  18.1 0.0 all-gather.4.cloned.1.call-update
  18.2 0.0 all-gather.8.cloned.1.call-start
  18.2 143.7 %all-gather.6.cloned.1.call-done = f32[512,4096]{1,0:T(8,128)} async-done(((f32[512,1024]{1,0:T(8,128)}), f32[512,4096]{1,0:T(8,128)}) %all-gather.6.cloned.1.call-update) | async-done | bytes 8388624 | tf_op jit(solution)/shard_map/all_gather | solution.py:32
  161.9 161.5 %all-gather.4.cloned.1.call-done = f32[2,4096,1024]{1,2,0:T(8,128)} async-done(((f32[2,512,1024]{1,2,0:T(8,128)}), f32[2,4096,1024]{1,2,0:T(8,128)}) %all-gather.4.cloned.1.call-update) | async-done | bytes 33554448 | tf_op jit(solution)/shard_map/all_gather | solution.py:36
  323.4 60.6 %subtract_bitcast_fusion = f32[2,512,1024]{1,2,0:T(8,128)} fusion(f32[2,4096,1024]{1,2,0:T(8,128)} %all-gather.4.cloned.1.call-done, f32[512,4096]{1,0:T(8,128)} %all-gather.6.cloned.1.call-done), kind=kOutput, calls=%fused_computation.8 | convolution fusion | flops 51540656128 | bytes 46137344 | tf_op jit(solution)/shard_map/ab,kbi->kai/dot_general | solution.py:33
  384.1 0.0 reduce-scatter.2.cloned.1.call-start
  384.1 286.9 %all-gather.8.cloned.1.call-done = f32[2,512,4096]{1,2,0:T(8,128)} async-done(((f32[2,512,1024]{1,2,0:T(8,128)}), f32[2,512,4096]{1,2,0:T(8,128)}) %all-gather.8.cloned.1.call-update) | async-done | bytes 16777232 | tf_op jit(solution)/shard_map/all_gather | solution.py:41
  671.0 59.7 %fusion.14 = f32[2,1024,4096]{2,1,0:T(8,128)} fusion(f32[2,512,1024]{1,2,0:T(8,128)} %broadcast_multiply_fusion, f32[2,512,4096]{1,2,0:T(8,128)} %all-gather.8.cloned.1.call-done), kind=kOutput, calls=%fused_computation.43 | convolution fusion | flops 51539607552 | bytes 54525952 | tf_op jit(solution)/shard_map/kaj,kai->jki/dot_general | solution.py:11
  730.7 1.5 compare_convert_fusion
  732.3 1.9 copy.15
  734.2 5.7 copy.14
  740.0 2.3 fusion.2
  742.4 0.3 dynamic_update_slice.7
  742.7 5.9 copy.18
  748.6 8.5 copy.27
  757.1 7.9 gather_fusion.4
  765.0 169.3 %reduce-scatter.2.cloned.1.call-done = f32[512,2048]{0,1:T(8,128)} async-done(((f32[4096,2048]{0,1:T(8,128)}), f32[512,2048]{0,1:T(8,128)}) %reduce-scatter.2.cloned.1.call-update) | async-done | bytes 4194320 | tf_op jit(solution)/shard_map/reduce_scatter | solution.py:12
  934.3 6.0 multiply_reduce_fusion
  940.3 40.0 %all-reduce = (f32[2,4096]{1,0:T(2,128)S(1)}, f32[4096]{0:T(1024)S(1)}) all-reduce(f32[2,4096]{1,0:T(2,128)S(1)} %constant_dynamic-update-slice_fusion, f32[4096]{0:T(1024)S(1)} %dynamic_update_slice.7), channel_id=1, replica_groups=mesh['row'=8,'col'=4] {'row','col'}, use_global_device_ids=true, to_apply=%region_2.0 | all-reduce | flops 12288 | bytes 98304 | tf_op jit(solution)/shard_map/psum | solution.py:57
  980.4 4.8 gather_fusion.1
  985.2 4.8 gather_fusion.2
  990.1 3.1 gather_fusion
  993.2 5.4 copy.19
  998.6 7.4 copy.25
  1006.0 7.0 gather_fusion.3
  1013.0 0.6 fusion.6
  (28 shorter events, 0.2 us)
Async XLA Ops:
  7.2 154.8 %all-gather.6.cloned.1.call-start = ((), (), s32[]{:S(2)}) async-start(), calls=%async_computation.2 | async-start | bytes 10485760 | tf_op jit(solution)/shard_map/all_gather | solution.py:32
  7.9 5.4 copy-start.2
  7.9 315.5 %all-gather.4.cloned.1.call-start = ((), (), s32[]{:S(2)}) async-start(), calls=%async_computation.1 | async-start | bytes 37748736 | tf_op jit(solution)/shard_map/all_gather | solution.py:36
  18.2 652.8 %all-gather.8.cloned.1.call-start = ((), (), s32[]{:S(2)}) async-start(), calls=%async_computation.3 | async-start | bytes 20971520 | tf_op jit(solution)/shard_map/all_gather | solution.py:41
  384.1 550.2 %reduce-scatter.2.cloned.1.call-start = ((), (), s32[]{:S(2)}) async-start(), calls=%async_computation.4 | async-start | bytes 37748736 | tf_op jit(solution)/shard_map/reduce_scatter | solution.py:12
  734.2 5.8 copy-start
  734.2 5.7 copy-start.1
Sparse Core Ops, SparseCore 0:
  9.6 152.3 all-gather.5
  164.4 158.9 all-gather.3
  384.2 286.7 all-gather.7
  730.8 203.4 reduce-scatter.1
where the time goes:
time: 1020 us
  waiting for transfers between devices  762 us (75%)
  matrix products  120 us (12%)
  local copies, waits for them, and re-layouts  68.4 us (7%)
  blocking collectives  40 us (4%)
  other arithmetic  15.2 us (1%)
  between operations  13.9 us (1%)
    all_gather x1, waiting for transfers between devices, per_device(): off_rows = lax.all_gather(off_inverse, 'col', axis=2, tiled=True)  287 us
    reduce_scatter x1, waiting for transfers between devices, scatter_form(): lax.psum_scatter(product.reshape(diag_rows * lax.axis_size('row'), fronts...  169 us
    all_gather x1, waiting for transfers between devices, per_device(): lax.all_gather(factor, 'row', axis=1, tiled=True)  161 us
    all_gather x1, waiting for transfers between devices, per_device(): whole_rows = lax.all_gather(anc_inverse, 'col', axis=1, tiled=True)  144 us
    dot_general x1, matrix products, per_device(): jnp.einsum('ab,kbi->kai', whole_rows, lax.all_gather(factor, 'row', axis=...  60.6 us
    dot_general x1, matrix products, scatter_form(): product = jnp.einsum('kaj,kai->jki', off_rows, factor, precision=highest)  59.7 us
    psum x1, blocking collectives, per_device(): cc_diag, z_diag = lax.psum((cc_place, z_place), ('row', 'col'))  40 us
    unnamed x19, local copies, waits for them, and re-layouts  38.3 us
  transfers between devices with their start and end apart: 4, of which 4 were waited for; matrix products, arithmetic and copies ran while one was open for 4% of the time, Pallas kernels for 0%

commit v1 on v0

v1 whole, which is shorter than its diff:
```python
import jax
import jax.numpy as jnp
from jax import lax
from jax.experimental import pallas as pl
from jax.experimental.pallas import tpu as pltpu
from jax.sharding import PartitionSpec as P


def assign_pairs(n_col, fronts):
    work = []
    for low in range(n_col):
        for high in range(low + 1, n_col):
            for front in range(fronts):
                middle = low + high - (n_col - 1)
                if high - low == 1:
                    middle = 0
                at_high = middle < 0 or (middle == 0 and front < fronts // 2)
                work.append((high, low, front) if at_high else (low, high, front))
    return work


def line_schedule(n_col, work, fronts, up):
    def fold(plane):
        return plane if up else n_col - 1 - plane

    wanted = {("z", src): n_col - 1 for src in range(n_col - 1)}
    for plane, partner, front in work:
        plane, partner = fold(plane), fold(partner)
        if partner < plane:
            wanted[(front, partner)] = max(wanted.get((front, partner), 0), plane)
    arrived = {key: {key[1]: 0} for key in wanted}
    rank = {"z": 0}
    for order, front in enumerate(range(fronts) if up else reversed(range(fronts))):
        rank[front] = 1 + order
    steps = []
    while True:
        sends = {}
        for plane in range(n_col - 1):
            ready = [
                key for key, last in wanted.items()
                if plane < last and plane in arrived[key] and plane + 1 not in arrived[key]
            ]
            if ready:
                sends[plane] = min(ready, key=lambda k: (k[0] != "z", -k[1] if k[0] == "z" else k[1], rank[k[0]]))
        if not sends:
            break
        steps.append(sends)
        for plane, key in sends.items():
            arrived[key][plane + 1] = len(steps)
    folded = [{fold(p): (k[0], fold(k[1])) for p, k in sends.items()} for sends in steps]
    where_at = {(k[0], fold(k[1])): {fold(p): s for p, s in at.items()} for k, at in arrived.items()}
    return folded, where_at


def color_slots(work, ready):
    slots = []
    load = [sum(it[0] == plane for it in work) for plane in range(1 + max(it[0] for it in work))]
    for item in sorted(work, key=lambda it: (ready[it], -load[it[0]], it)):
        for slot in slots:
            if all(other[0] != item[0] and other[1] != item[1] for other in slot):
                slot.append(item)
                break
        else:
            slots.append([item])
    return sorted(slots, key=lambda slot: max(ready[it] for it in slot))


def choose(index, options):
    groups = []
    for plane, array in options.items():
        for entry in groups:
            if entry[0] is array:
                entry[1].append(plane)
                break
        else:
            groups.append((array, [plane]))
    result = groups[0][0]
    for array, planes in groups[1:]:
        hit = index == planes[0]
        for plane in planes[1:]:
            hit = jnp.logical_or(hit, index == plane)
        result = jnp.where(hit, array, result)
    return result


def tie(value, after):
    return lax.optimization_barrier((value, after))[0]


def halve(part, axis, bit_axis, bit, n_row):
    mine = (lax.axis_index("row") >> bit_axis) & 1
    send = lax.dynamic_index_in_dim(part, 1 - mine, axis, keepdims=False)
    keep = lax.dynamic_index_in_dim(part, mine, axis, keepdims=False)
    return keep + lax.ppermute(send, "row", [(i, i ^ bit) for i in range(n_row)])


def reduce_scatter(part, n_row, groups):
    rows, width = part.shape
    bits = n_row.bit_length() - 1
    part = part.reshape((groups,) + (2,) * bits + (rows // groups // n_row, width))

    first = halve(part, bits, 0, 1, n_row)
    half = width // 2
    rest = list(range(1, bits))

    def run_rest(piece, order):
        left = list(reversed(rest))
        for bit in order:
            axis = 1 + left.index(bit)
            piece = halve(piece, axis, bit, 1 << bit, n_row)
            left.remove(bit)
        return piece

    one = run_rest(first[..., :half], rest)
    two = run_rest(first[..., half:], rest[::-1])
    return jnp.concatenate([one, two], axis=-1)


def per_device(anc_inverse, off_factor, diag_inverse, block_mask, edge_child, edge_other):
    fronts, anc_rows, col_width = off_factor.shape
    diag_rows = diag_inverse.shape[1]
    anc_cols = anc_inverse.shape[1]
    row_id = lax.axis_index("row")
    col_id = lax.axis_index("col")
    n_row, n_col = lax.axis_size("row"), lax.axis_size("col")
    groups = col_width // diag_rows
    supercols, ancestor = col_width * n_col, anc_cols * n_col
    high = lax.Precision.HIGH

    keep = jnp.repeat(block_mask, anc_rows // block_mask.shape[1], axis=1).astype(jnp.float32)
    factor = [off_factor[k] * keep[k][:, None] for k in range(fronts)]
    side_by_side = jnp.concatenate(factor, axis=1)
    columns = lax.all_gather(side_by_side, "row", axis=0, tiled=True)

    work = assign_pairs(n_col, fronts)
    plans = {up: line_schedule(n_col, work, fronts, up) for up in (True, False)}
    got = {up: {} for up in plans}
    spots = {up: plans[up][1] for up in plans}
    ready = {
        (plane, partner, front): spots[partner < plane][(front, partner)][plane] for plane, partner, front in work
    }

    def hop(number, after=()):
        earlier = tuple(got[up][number - 1] for up in got if number - 1 in got[up]) or (side_by_side,)
        for up, (steps, where_at) in plans.items():
            if number > len(steps):
                continue
            sends = steps[number - 1]
            options = {}
            for plane, (kind, src) in sends.items():
                if src == plane:
                    options[plane] = anc_inverse if kind == "z" else factor[kind]
                else:
                    options[plane] = got[up][where_at[(kind, src)][plane]]
            operand = choose(col_id, options)
            operand = tie(operand, earlier + tuple(after))
            step = 1 if up else -1
            got[up][number] = lax.ppermute(operand, "col", [(p, p + step) for p in sorted(sends)])

    for number in range(1, n_col):
        hop(number)
    whole_rows = jnp.zeros((anc_rows, ancestor), jnp.float32)
    whole_rows = lax.dynamic_update_slice_in_dim(whole_rows, anc_inverse, col_id * anc_cols, 1)
    for shift in range(1, n_col):
        options = {}
        for plane in range(n_col):
            src = (plane - shift) % n_col
            options[plane] = got[src < plane][spots[src < plane][("z", src)][plane]]
        block = choose(col_id, options)
        whole_rows = lax.dynamic_update_slice_in_dim(whole_rows, block, (col_id - shift) % n_col * anc_cols, 1)
    hop(n_col)
    off_cat = -jnp.dot(whole_rows, columns, precision=high)
    last = max(len(steps) for steps, where_at in plans.values())
    for number in range(n_col + 1, last + 1):
        hop(number, (off_cat,))
    off = [off_cat[:, k * col_width:(k + 1) * col_width] for k in range(fronts)]

    row_global = row_id * diag_rows + jnp.arange(diag_rows, dtype=jnp.int32)
    col_global = col_id * col_width + jnp.arange(col_width, dtype=jnp.int32)
    hit = row_global[:, None] == col_global[None, :]
    cc_part = jnp.stack([
        jnp.sum(jnp.where(hit, diag_inverse[k], 0.0), axis=0) - jnp.sum(off[k] * factor[k], axis=0)
        for k in range(fronts)
    ])
    cc_near = cc_part
    bit = 1
    while bit < n_row:
        cc_near = cc_near + lax.ppermute(cc_near, "row", [(i, i ^ bit) for i in range(n_row)])
        bit *= 2
    cc_rows = lax.dynamic_slice_in_dim(cc_near, row_id % groups * diag_rows, diag_rows, 1)
    cc_far = cc_rows
    for shift in range(1, n_col):
        pairs = []
        for row in range(n_row):
            owner = row // groups
            pairs.append((row * n_col + owner, row * n_col + (owner + shift) % n_col))
        came = lax.ppermute(cc_rows, ("row", "col"), pairs)
        cc_far = jnp.where((col_id - row_id // groups) % n_col == shift, came, cc_far)
    own = lax.dynamic_slice_in_dim(whole_rows, row_id * anc_rows, anc_rows, 1)
    eye = jnp.arange(anc_rows)[:, None] == jnp.arange(anc_rows)[None, :]
    z_far = jnp.sum(jnp.where(eye, own, 0.0), axis=0)

    off_inverse = jnp.stack(off)
    is_child = edge_other < supercols
    at_col = edge_child[:, :, None] == col_global
    at_row = edge_other[:, :, None] == row_global
    at_anc = edge_other[:, :, None] == supercols + row_id * anc_rows + jnp.arange(anc_rows, dtype=jnp.int32)

    def picked(at, values):
        return jnp.sum(jnp.where(at, values, 0.0), axis=-1)

    def mixed_of(at, block):
        rows = jnp.einsum("ker,krc->kec", at.astype(jnp.float32), block, precision=lax.Precision.HIGHEST)
        return picked(at_col, rows)

    ends = picked(at_col, cc_near[:, None, :]) + picked(at_row, cc_far[:, None, :]) + picked(at_anc, z_far)
    ends = ends - 2.0 * mixed_of(at_anc, off_inverse)

    def partial_sum(left, right):
        return lax.dot_general(left, right, (((0,), (0,)), ((), ())), precision=high)

    diag_piece = [reduce_scatter(partial_sum(factor[k], off[k]), n_row, groups) for k in range(fronts)]
    direct, turned = {}, {}
    done = list(diag_piece)
    slots = color_slots(work, ready)
    for place, slot in enumerate(slots):
        side = choose(col_id, {
            plane: got[partner < plane][spots[partner < plane][(front, partner)][plane]]
            for plane, partner, front in slot
        })
        mine = choose(col_id, {plane: off[front] for plane, partner, front in slot})
        if place == len(slots) - 1:
            side = tie(side, tuple(done[:-2]))
        piece = reduce_scatter(partial_sum(side, mine), n_row, groups)
        done.append(piece)
        sent = lax.ppermute(piece, "col", [(plane, partner) for plane, partner, front in slot])
        sent = jnp.stack([
            jnp.concatenate([sent[h][:, g * diag_rows:(g + 1) * diag_rows] for h in range(groups)], axis=1)
            for g in range(groups)
        ])
        for plane, partner, front in slot:
            direct[(plane, partner, front)] = piece
            turned[(partner, plane, front)] = sent

    block_id = row_id // groups
    parts = []
    for k in range(fronts):
        blocks = []
        for block in range(n_col):
            options = {}
            for plane in range(n_col):
                if plane == block:
                    options[plane] = diag_piece[k]
                elif (plane, block, k) in direct:
                    options[plane] = direct[(plane, block, k)]
                else:
                    options[plane] = turned[(plane, block, k)]
            blocks.append(choose(col_id, options))
        chunks = tie(jnp.stack(blocks), ends).reshape(n_row, -1, col_width)
        found = lax.all_to_all(chunks, "row", 0, 0, tiled=True).reshape(diag_rows, col_width)
        straight = jnp.zeros((), jnp.bool_)
        for plane in range(n_col):
            for block in range(n_col):
                if plane == block or (plane, block, k) in direct:
                    straight = jnp.logical_or(straight, jnp.logical_and(col_id == plane, block_id == block))
        parts.append(subtract_block(diag_inverse[k], found, straight))
    diag_part = jnp.stack(parts)
    resist = ends - 2.0 * mixed_of(at_row, diag_part)
    return (off_inverse, diag_part, resist)


def subtract_block(base, found, straight):
    rows, width = base.shape

    def kernel(flag, base_ref, found_ref, out_ref):
        @pl.when(flag[0] == 1)
        def _():
            out_ref[...] = base_ref[...] - found_ref[...]

        @pl.when(flag[0] == 0)
        def _():
            out_ref[...] = base_ref[...] - found_ref[...].T

    spec = pl.BlockSpec((rows, rows), lambda h, flag: (0, h))
    return pl.pallas_call(
        kernel,
        grid_spec=pltpu.PrefetchScalarGridSpec(
            num_scalar_prefetch=1, grid=(width // rows,), in_specs=[spec, spec], out_specs=spec
        ),
        out_shape=jax.ShapeDtypeStruct(base.shape, base.dtype),
        compiler_params=pltpu.CompilerParams(vmem_limit_bytes=32 * 1024 * 1024),
    )(straight.astype(jnp.int32).reshape(1), base, found)


def solution(mesh):
    placed = (
        P("row", "col"),
        P(None, "row", "col"),
        P(None, "row", "col"),
        P(None, "row"),
        P(None, ("row", "col")),
        P(None, ("row", "col")),
    )
    return jax.shard_map(
        per_device,
        mesh=mesh,
        in_specs=placed,
        out_specs=(P(None, "row", "col"), P(None, "row", "col"), P(None, ("row", "col"))),
        check_vma=False,
    )
```

time: 1020 us -> 572 us (0.56); the launches traced: 1020 us -> 561 us
  waiting for transfers between devices: 762 us -> 317 us
  starting transfers between devices: 0.16 us -> 86.4 us
  matrix products: 120 us -> 65.1 us
  blocking collectives: 40 us -> 0 us
  local copies, waits for them, and re-layouts: 68.4 us -> 34.8 us
  other arithmetic: 15.2 us -> 39.2 us
    all_gather x3 -> x1, waiting for transfers between devices: 592 us -> 0.01 us  [per_device(): columns = lax.all_gather(side_by_side, 'row', axis=0, tiled=True)]
    ppermute x0 -> x50, waiting for transfers between devices: none -> 273 us  [the longest x10 181 us: hop(): lax.ppermute(operand, 'col', [(p, p + step) for p in sorted(sends)])]
    reduce_scatter x1 -> x0, waiting for transfers between devices: 169 us -> none  [scatter_form(): lax.psum_scatter(product.reshape(diag_rows * lax.axis_size('row'), fronts...]
    ppermute x0 -> x50, starting transfers between devices: none -> 78.2 us  [the longest x30 34 us: halve(): lax.ppermute(send, 'row', [(i, i ^ bit) for i in range(n_row)])]
    dot_general x2 -> x9, matrix products: 120 us -> 65.1 us  [the longest x1 33 us: per_device(): off_cat = -jnp.dot(whole_rows, columns, precision=high)]
    all_to_all x0 -> x2, waiting for transfers between devices: none -> 44.3 us  [per_device(): lax.all_to_all(chunks, 'row', 0, 0, tiled=True)]
    psum x1 -> x0, blocking collectives: 40 us -> none  [per_device(): cc_diag, z_diag = lax.psum((cc_place, z_place), ('row', 'col'))]
    gather x10 -> x0, local copies, waits for them, and re-layouts: 27.8 us -> none  [the longest x2 7.9 us: per_device(): jnp.take_along_axis(flat_off, anc_row * col_width + local_near, axis=1)]
  transfers between devices with their start and end apart: 4 -> 53, of which waited for: 4 -> 33; matrix products, arithmetic and copies ran while one was open for 4% -> 20% of each run, Pallas kernels for 0% -> 0%
where the time goes in v1:
time: 572 us; the launch traced here: 561 us
  waiting for transfers between devices  317 us (55%)
  starting transfers between devices  86.4 us (15%)
  matrix products  65.1 us (11%)
  other arithmetic  39.2 us (7%)
  local copies, waits for them, and re-layouts  34.8 us (6%)
  between operations  15.8 us (3%)
    ppermute x10, waiting for transfers between devices, hop(): lax.ppermute(operand, 'col', [(p, p + step) for p in sorted(sends)])  181 us
    ppermute x30, waiting for transfers between devices, halve(): lax.ppermute(send, 'row', [(i, i ^ bit) for i in range(n_row)])  62.6 us
    all_to_all x2, waiting for transfers between devices, per_device(): lax.all_to_all(chunks, 'row', 0, 0, tiled=True)  44.3 us
    ppermute x30, starting transfers between devices, halve(): lax.ppermute(send, 'row', [(i, i ^ bit) for i in range(n_row)])  34 us
    dot_general x1, matrix products, per_device(): off_cat = -jnp.dot(whole_rows, columns, precision=high)  33 us
    dot_general x6, matrix products, partial_sum(): lax.dot_general(left, right, (((0,), (0,)), ((), ())), precision=high)  27.1 us
    ppermute x4, waiting for transfers between devices, per_device(): lax.ppermute(piece, 'col', [(plane, partner) for plane, partner, front in...  26.9 us
    ppermute x10, starting transfers between devices, hop(): lax.ppermute(operand, 'col', [(p, p + step) for p in sorted(sends)])  23.2 us
  transfers between devices with their start and end apart: 53, of which 33 were waited for; matrix products, arithmetic and copies ran while one was open for 20% of the time, Pallas kernels for 0%

profile of v1, /device:TPU:0, one launch (start us, length us, event | category | flops | bytes accessed | tf_op | source)
XLA Modules:
  0.0 561.5 jit_solution(17899729932367585686)
XLA Ops:
  14.3 6.2 %collective-permute-start = (f32[512,1024]{1,0:T(8,128)}, f32[512,1024]{1,0:T(8,128)}, u32[]{:S(2)}, u32[]{:S(2)}) collective-permute-start(f32[512,1024]{1,0:T(8,128)} %param.6), channel_id=1, source_target_pairs={{0,1},{1,2},{2,3},{4,5},{5,6},{6,7},{8,9},{9,10},{10,11},{12,13},{... | collective-permute-start | bytes 6291464 | tf_op jit(solution)/shard_map/ppermute | solution.py:158
  21.8 42.6 %collective-permute-done = f32[512,1024]{1,0:T(8,128)} collective-permute-done((f32[512,1024]{1,0:T(8,128)}, f32[512,1024]{1,0:T(8,128)}, u32[]{:S(2)}, u32[]{:S(2)}) %collective-permute-start) | collective-permute-done | bytes 2097184 | tf_op jit(solution)/shard_map/ppermute | solution.py:158
  64.8 5.0 collective-permute-done.1
  72.1 43.5 %collective-permute-done.3 = f32[512,1024]{1,0:T(8,128)S(1)} collective-permute-done((f32[512,1024]{1,0:T(8,128)S(1)}, f32[512,1024]{1,0:T(8,128)S(1)}, u32[]{:S(2)}, u32[]{:S(2)}) %collective-permute-start.3) | collective-permute-done | bytes 2097184 | tf_op jit(solution)/shard_map/ppermute | solution.py:158
  119.0 49.0 %collective-permute-done.2 = f32[512,1024]{1,0:T(8,128)S(1)} collective-permute-done((f32[512,1024]{1,0:T(8,128)S(1)}, f32[512,1024]{1,0:T(8,128)S(1)}, u32[]{:S(2)}, u32[]{:S(2)}) %collective-permute-start.2) | collective-permute-done | bytes 2097184 | tf_op jit(solution)/shard_map/ppermute | solution.py:158
  168.1 4.9 collective-permute-start.5
  185.1 28.9 %collective-permute-done.5 = f32[512,1024]{1,0:T(8,128)} collective-permute-done((f32[512,1024]{1,0:T(8,128)}, f32[512,1024]{1,0:T(8,128)}, u32[]{:S(2)}, u32[]{:S(2)}) %collective-permute-start.5) | collective-permute-done | bytes 2097184 | tf_op jit(solution)/shard_map/ppermute | solution.py:158
  214.1 7.1 %collective-permute-done.4 = f32[512,1024]{1,0:T(8,128)} collective-permute-done((f32[512,1024]{1,0:T(8,128)}, f32[512,1024]{1,0:T(8,128)}, u32[]{:S(2)}, u32[]{:S(2)}) %collective-permute-start.4) | collective-permute-done | bytes 2097184 | tf_op jit(solution)/shard_map/ppermute | solution.py:158
  232.7 33.0 %convolution_negate_fusion = f32[512,2048]{1,0:T(8,128)S(1)} fusion(f32[512,4096]{1,0:T(8,128)} %copy-done.15, f32[4096,2048]{1,0:T(8,128)} %all-gather.2.cloned.1.call-done), kind=kOutput, calls=%fused_computation.3 | convolution fusion | flops 25770852352 | bytes 46137344 | tf_op jit(solution)/shard_map/dot_general | solution.py:172
  265.7 5.3 fusion.19
  278.7 3.7 fusion.5
  282.4 3.7 fusion.7
  286.7 6.1 %fusion.9 = f32[1024,1024]{1,0:T(8,128)S(1)} fusion(f32[512,1024]{1,0:T(8,128)} %collective-permute-done.6, f32[512,1024]{1,0:T(8,128)} %collective-permute-done.7, f32[512,2048]{1,0:T(8,128)S(1)} %convolution_negate_fusion, pred[]{:T(512)S(6)} %eq.59), kind=kOutput, calls=%fused_computation.36 | convolution fusion | flops 3222274048 | bytes 12583936 | tf_op jit(solution)/shard_map/dot_general | solution.py:220
  307.2 7.7 %collective-permute-start.43 = (f32[2,512]{1,0:T(2,128)S(1)}, f32[2,512]{1,0:T(2,128)S(1)}, u32[]{:S(2)}, u32[]{:S(2)}) collective-permute-start(f32[2,512]{1,0:T(2,128)S(1)} %constant_dynamic-slice_fusion), channel_id=1, source_target_pairs={{0,2},{4,6},{9,11},{13,15},{18,16},{22,20},{27,25},{31,29}} | collective-permute-start | bytes 12296 | tf_op jit(solution)/shard_map/ppermute | solution.py:197
  321.8 4.4 collective-permute-done.9
  326.2 7.1 %collective-permute-start.11 = (f32[2,2,64,512]{3,2,1,0:T(8,128)}, f32[2,2,64,512]{3,2,1,0:T(8,128)S(1)}, u32[]{:S(2)}, u32[]{:S(2)}) collective-permute-start(f32[2,2,64,512]{3,2,1,0:T(8,128)} %dynamic-slice_bitcast_fusion.9), channel_id=1, source_target_pairs={{0,8},{4,12},{8,0},{12,4},{16,24},{20,28},{24,16},{28,20},{1,9},{5... | collective-permute-start | bytes 1572872 | tf_op jit(solution)/shard_map/ppermute | solution.py:94
  333.9 4.3 fusion.12
  360.4 4.5 collective-permute-done.33
  371.5 4.6 collective-permute-done.48
  382.6 4.8 collective-permute-done.28
  387.8 5.1 collective-permute-done.12
  395.1 4.0 fusion.17
  410.5 11.3 %collective-permute-done.38 = f32[2,64,1024]{2,1,0:T(8,128)S(1)} collective-permute-done((f32[2,64,1024]{2,1,0:T(8,128)S(1)}, f32[2,64,1024]{2,1,0:T(8,128)S(1)}, u32[]{:S(2)}, u32[]{:S(2)}) %collective-permute-start.38) | collective-permute-done | bytes 524320 | tf_op jit(solution)/shard_map/ppermute | solution.py:236
  422.0 8.8 %collective-permute-done.35 = f32[2,64,1024]{2,1,0:T(8,128)S(1)} collective-permute-done((f32[2,64,1024]{2,1,0:T(8,128)S(1)}, f32[2,64,1024]{2,1,0:T(8,128)S(1)}, u32[]{:S(2)}, u32[]{:S(2)}) %collective-permute-start.35) | collective-permute-done | bytes 524320 | tf_op jit(solution)/shard_map/ppermute | solution.py:236
  434.5 9.0 %collective-permute-done.21 = f32[2,2,64,512]{3,2,1,0:T(8,128)S(1)} collective-permute-done((f32[2,2,64,512]{3,2,1,0:T(8,128)S(1)}, f32[2,2,64,512]{3,2,1,0:T(8,128)S(1)}, u32[]{:S(2)}, u32[]{:S(2)}) %collective-permute-start.21) | collective-permute-done | bytes 524320 | tf_op jit(solution)/shard_map/ppermute | solution.py:94
  456.5 5.8 %collective-permute-done.16 = f32[2,2,64,512]{3,2,1,0:T(8,128)S(1)} collective-permute-done((f32[2,2,64,512]{3,2,1,0:T(8,128)S(1)}, f32[2,2,64,512]{3,2,1,0:T(8,128)S(1)}, u32[]{:S(2)}, u32[]{:S(2)}) %collective-permute-start.16) | collective-permute-done | bytes 524320 | tf_op jit(solution)/shard_map/ppermute | solution.py:94
  470.4 4.3 collective-permute-start.37
  475.3 6.7 %collective-permute-done.37 = f32[2,64,1024]{2,1,0:T(8,128)S(1)} collective-permute-done((f32[2,64,1024]{2,1,0:T(8,128)S(1)}, f32[2,64,1024]{2,1,0:T(8,128)S(1)}, u32[]{:S(2)}, u32[]{:S(2)}) %collective-permute-start.37) | collective-permute-done | bytes 524320 | tf_op jit(solution)/shard_map/ppermute | solution.py:236
  492.0 23.9 %all-to-all-done = f32[8,64,1024]{2,1,0:T(8,128)S(1)} async-done(((f32[8,64,1024]{2,1,0:T(8,128)}), f32[8,64,1024]{2,1,0:T(8,128)S(1)}, u32[]{:S(2)}, u32[]{:S(2)}) %all-to-all-start) | async-done | bytes 2097184 | tf_op jit(solution)/shard_map/all_to_all | solution.py:260
  515.9 4.6 all-to-all-start.1
  520.6 4.1 slice_bitcast_fusion.1
  526.7 20.4 %all-to-all-done.1 = f32[8,64,1024]{2,1,0:T(8,128)} async-done(((f32[8,64,1024]{2,1,0:T(8,128)}), f32[8,64,1024]{2,1,0:T(8,128)}, u32[]{:S(2)}, u32[]{:S(2)}) %all-to-all-start.1) | async-done | bytes 2097184 | tf_op jit(solution)/shard_map/all_to_all | solution.py:260
  (273 shorter events, 160.9 us)
Async XLA Ops:
  7.2 225.5 %all-gather.2.cloned.1.call-start = ((), (), s32[]{:S(2)}) async-start(), calls=%async_computation.2 | async-start | bytes 37748736 | tf_op jit(solution)/shard_map/all_gather | solution.py:133
  14.3 50.1 %collective-permute-start = (f32[512,1024]{1,0:T(8,128)}, f32[512,1024]{1,0:T(8,128)}, u32[]{:S(2)}, u32[]{:S(2)}) collective-permute-start(f32[512,1024]{1,0:T(8,128)} %param.6), channel_id=1, source_target_pairs={{0,1},{1,2},{2,3},{4,5},{5,6},{6,7},{8,9},{9,10},{10,11},{12,13},{... | collective-permute-start | bytes 6291464 | tf_op jit(solution)/shard_map/ppermute | solution.py:158
  20.5 49.3 %collective-permute-start.1 = (f32[512,1024]{1,0:T(8,128)}, f32[512,1024]{1,0:T(8,128)}, u32[]{:S(2)}, u32[]{:S(2)}) collective-permute-start(f32[512,1024]{1,0:T(8,128)} %param.6), channel_id=1, source_target_pairs={{1,0},{2,1},{3,2},{5,4},{6,5},{7,6},{9,8},{10,9},{11,10},{13,12},{... | collective-permute-start | bytes 6291464 | tf_op jit(solution)/shard_map/ppermute | solution.py:158
  69.8 45.9 %collective-permute-start.3 = (f32[512,1024]{1,0:T(8,128)S(1)}, f32[512,1024]{1,0:T(8,128)S(1)}, u32[]{:S(2)}, u32[]{:S(2)}) collective-permute-start(f32[512,1024]{1,0:T(8,128)S(1)} %broadcast_select_fusion.1), channel_id=1, source_target_pairs={{0,1},{1,2},{2,3},{4,5},{5,6},{6,7},{8,9},{9,10},{10,11},{12,13},{... | collective-permute-start | bytes 6291464 | tf_op jit(solution)/shard_map/ppermute | solution.py:158
  117.7 50.3 %collective-permute-start.2 = (f32[512,1024]{1,0:T(8,128)S(1)}, f32[512,1024]{1,0:T(8,128)S(1)}, u32[]{:S(2)}, u32[]{:S(2)}) collective-permute-start(f32[512,1024]{1,0:T(8,128)S(1)} %get-tuple-element.16), channel_id=1, source_target_pairs={{1,0},{2,1},{3,2},{5,4},{6,5},{7,6},{9,8},{10,9},{11,10},{13,12},{... | collective-permute-start | bytes 6291464 | tf_op jit(solution)/shard_map/ppermute | solution.py:158
  168.1 46.0 %collective-permute-start.5 = (f32[512,1024]{1,0:T(8,128)}, f32[512,1024]{1,0:T(8,128)}, u32[]{:S(2)}, u32[]{:S(2)}) collective-permute-start(f32[512,1024]{1,0:T(8,128)} %get-tuple-element.19), channel_id=1, source_target_pairs={{0,1},{1,2},{2,3},{4,5},{5,6},{6,7},{8,9},{9,10},{10,11},{12,13},{... | collective-permute-start | bytes 6291464 | tf_op jit(solution)/shard_map/ppermute | solution.py:158
  174.7 46.5 %collective-permute-start.4 = (f32[512,1024]{1,0:T(8,128)}, f32[512,1024]{1,0:T(8,128)}, u32[]{:S(2)}, u32[]{:S(2)}) collective-permute-start(f32[512,1024]{1,0:T(8,128)} %broadcast_select_fusion.2), channel_id=1, source_target_pairs={{1,0},{2,1},{3,2},{5,4},{6,5},{7,6},{9,8},{10,9},{11,10},{13,12},{... | collective-permute-start | bytes 6291464 | tf_op jit(solution)/shard_map/ppermute | solution.py:158
  221.2 55.0 %collective-permute-start.6 = (f32[512,1024]{1,0:T(8,128)}, f32[512,1024]{1,0:T(8,128)}, u32[]{:S(2)}, u32[]{:S(2)}) collective-permute-start(f32[512,1024]{1,0:T(8,128)} %collective-permute-done.5), channel_id=1, source_target_pairs={{1,2},{2,3},{5,6},{6,7},{9,10},{10,11},{13,14},{14,15},{17,18},{18... | collective-permute-start | bytes 6291464 | tf_op jit(solution)/shard_map/ppermute | solution.py:158
  223.2 53.1 %collective-permute-start.7 = (f32[512,1024]{1,0:T(8,128)}, f32[512,1024]{1,0:T(8,128)}, u32[]{:S(2)}, u32[]{:S(2)}) collective-permute-start(f32[512,1024]{1,0:T(8,128)} %collective-permute-done.4), channel_id=1, source_target_pairs={{1,0},{2,1},{5,4},{6,5},{9,8},{10,9},{13,12},{14,13},{17,16},{18,1... | collective-permute-start | bytes 6291464 | tf_op jit(solution)/shard_map/ppermute | solution.py:158
  273.1 44.9 %collective-permute-start.10 = (f32[2,2,2,64,1024]{4,3,1,0,2:T(8,128)}, f32[2,2,2,64,1024]{4,3,1,0,2:T(8,128)}, u32[]{:S(2)}, u32[]{:S(2)}) collective-permute-start(f32[2,2,2,64,1024]{4,3,1,0,2:T(8,128)} %bitcast.238), channel_id=1, source_target_pairs={{0,4},{4,0},{8,12},{12,8},{16,20},{20,16},{24,28},{28,24},{1,5},{5... | collective-permute-start | bytes 6291464 | tf_op jit(solution)/shard_map/ppermute | solution.py:94
  276.2 49.9 %collective-permute-start.9 = (f32[512,1024]{1,0:T(8,128)S(1)}, f32[512,1024]{1,0:T(8,128)S(1)}, u32[]{:S(2)}, u32[]{:S(2)}) collective-permute-start(f32[512,1024]{1,0:T(8,128)S(1)} %copy-done.5), channel_id=1, source_target_pairs={{1,0},{2,1},{5,4},{6,5},{9,8},{10,9},{13,12},{14,13},{17,16},{18,1... | collective-permute-start | bytes 6291464 | tf_op jit(solution)/shard_map/ppermute | solution.py:158
  277.5 55.7 %collective-permute-start.8 = (f32[512,1024]{1,0:T(8,128)S(1)}, f32[512,1024]{1,0:T(8,128)S(1)}, u32[]{:S(2)}, u32[]{:S(2)}) collective-permute-start(f32[512,1024]{1,0:T(8,128)S(1)} %get-tuple-element.22), channel_id=1, source_target_pairs={{1,2},{2,3},{5,6},{6,7},{9,10},{10,11},{13,14},{14,15},{17,18},{18... | collective-permute-start | bytes 6291464 | tf_op jit(solution)/shard_map/ppermute | solution.py:158
  316.8 22.3 %collective-permute-start.30 = (f32[2,2,2,64,1024]{4,3,1,0,2:T(8,128)}, f32[2,2,2,64,1024]{4,3,1,0,2:T(8,128)}, u32[]{:S(2)}, u32[]{:S(2)}) collective-permute-start(f32[2,2,2,64,1024]{4,3,1,0,2:T(8,128)} %bitcast.235), channel_id=1, source_target_pairs={{0,4},{4,0},{8,12},{12,8},{16,20},{20,16},{24,28},{28,24},{1,5},{5... | collective-permute-start | bytes 6291464 | tf_op jit(solution)/shard_map/ppermute | solution.py:94
  317.6 24.2 %collective-permute-start.45 = (f32[2,2,2,64,1024]{4,3,2,1,0:T(8,128)}, f32[2,2,2,64,1024]{4,3,2,1,0:T(8,128)}, u32[]{:S(2)}, u32[]{:S(2)}) collective-permute-start(f32[2,2,2,64,1024]{4,3,2,1,0:T(8,128)} %dynamic-slice_bitcast_fusion), channel_id=1, source_target_pairs={{0,4},{4,0},{8,12},{12,8},{16,20},{20,16},{24,28},{28,24},{1,5},{5... | collective-permute-start | bytes 6291464 | tf_op jit(solution)/shard_map/ppermute | solution.py:94
  318.0 32.1 %collective-permute-start.25 = (f32[2,2,2,64,1024]{4,3,2,1,0:T(8,128)}, f32[2,2,2,64,1024]{4,3,2,1,0:T(8,128)}, u32[]{:S(2)}, u32[]{:S(2)}) collective-permute-start(f32[2,2,2,64,1024]{4,3,2,1,0:T(8,128)} %dynamic-slice_bitcast_fusion.1), channel_id=1, source_target_pairs={{0,4},{4,0},{8,12},{12,8},{16,20},{20,16},{24,28},{28,24},{1,5},{5... | collective-permute-start | bytes 6291464 | tf_op jit(solution)/shard_map/ppermute | solution.py:94
  326.2 26.6 %collective-permute-start.11 = (f32[2,2,64,512]{3,2,1,0:T(8,128)}, f32[2,2,64,512]{3,2,1,0:T(8,128)S(1)}, u32[]{:S(2)}, u32[]{:S(2)}) collective-permute-start(f32[2,2,64,512]{3,2,1,0:T(8,128)} %dynamic-slice_bitcast_fusion.9), channel_id=1, source_target_pairs={{0,8},{4,12},{8,0},{12,4},{16,24},{20,28},{24,16},{28,20},{1,9},{5... | collective-permute-start | bytes 1572872 | tf_op jit(solution)/shard_map/ppermute | solution.py:94
  333.3 26.9 %collective-permute-start.13 = (f32[2,2,64,512]{3,2,1,0:T(8,128)S(1)}, f32[2,2,64,512]{3,2,1,0:T(8,128)S(1)}, u32[]{:S(2)}, u32[]{:S(2)}) collective-permute-start(f32[2,2,64,512]{3,2,1,0:T(8,128)S(1)} %bitcast.270), channel_id=1, source_target_pairs={{0,16},{4,20},{8,24},{12,28},{16,0},{20,4},{24,8},{28,12},{1,17},{... | collective-permute-start | bytes 1572872 | tf_op jit(solution)/shard_map/ppermute | solution.py:94
  339.1 91.7 %collective-permute-start.20 = (f32[2,2,2,64,1024]{4,3,1,0,2:T(8,128)S(1)}, f32[2,2,2,64,1024]{4,3,1,0,2:T(8,128)S(1)}, u32[]{:S(2)}, u32[]{:S(2)}) collective-permute-start(f32[2,2,2,64,1024]{4,3,1,0,2:T(8,128)S(1)} %bitcast.268), channel_id=1, source_target_pairs={{0,4},{4,0},{8,12},{12,8},{16,20},{20,16},{24,28},{28,24},{1,5},{5... | collective-permute-start | bytes 6291464 | tf_op jit(solution)/shard_map/ppermute | solution.py:94
  341.8 15.7 %collective-permute-start.31 = (f32[2,2,64,512]{3,2,1,0:T(8,128)S(1)}, f32[2,2,64,512]{3,2,1,0:T(8,128)S(1)}, u32[]{:S(2)}, u32[]{:S(2)}) collective-permute-start(f32[2,2,64,512]{3,2,1,0:T(8,128)S(1)} %dynamic-slice_bitcast_fusion.4), channel_id=1, source_target_pairs={{0,8},{4,12},{8,0},{12,4},{16,24},{20,28},{24,16},{28,20},{1,9},{5... | collective-permute-start | bytes 1572872 | tf_op jit(solution)/shard_map/ppermute | solution.py:94
  352.7 16.0 %collective-permute-start.46 = (f32[2,2,64,512]{3,2,1,0:T(8,128)}, f32[2,2,64,512]{3,2,1,0:T(8,128)S(1)}, u32[]{:S(2)}, u32[]{:S(2)}) collective-permute-start(f32[2,2,64,512]{3,2,1,0:T(8,128)} %dynamic-slice_bitcast_fusion.3), channel_id=1, source_target_pairs={{0,8},{4,12},{8,0},{12,4},{16,24},{20,28},{24,16},{28,20},{1,9},{5... | collective-permute-start | bytes 1572872 | tf_op jit(solution)/shard_map/ppermute | solution.py:94
  357.5 18.7 %collective-permute-start.48 = (f32[2,2,64,512]{3,2,1,0:T(8,128)S(1)}, f32[2,2,64,512]{3,2,1,0:T(8,128)S(1)}, u32[]{:S(2)}, u32[]{:S(2)}) collective-permute-start(f32[2,2,64,512]{3,2,1,0:T(8,128)S(1)} %copy-done.20), channel_id=1, source_target_pairs={{0,16},{4,20},{8,24},{12,28},{16,0},{20,4},{24,8},{28,12},{1,17},{... | collective-permute-start | bytes 1572872 | tf_op jit(solution)/shard_map/ppermute | solution.py:94
  360.1 19.8 %collective-permute-start.26 = (f32[2,2,64,512]{3,2,1,0:T(8,128)S(1)}, f32[2,2,64,512]{3,2,1,0:T(8,128)S(1)}, u32[]{:S(2)}, u32[]{:S(2)}) collective-permute-start(f32[2,2,64,512]{3,2,1,0:T(8,128)S(1)} %dynamic-slice_bitcast_fusion.6), channel_id=1, source_target_pairs={{0,8},{4,12},{8,0},{12,4},{16,24},{20,28},{24,16},{28,20},{1,9},{5... | collective-permute-start | bytes 1572872 | tf_op jit(solution)/shard_map/ppermute | solution.py:94
  364.9 22.5 %collective-permute-start.28 = (f32[2,2,64,512]{3,2,1,0:T(8,128)S(1)}, f32[2,2,64,512]{3,2,1,0:T(8,128)S(1)}, u32[]{:S(2)}, u32[]{:S(2)}) collective-permute-start(f32[2,2,64,512]{3,2,1,0:T(8,128)S(1)} %dynamic-slice_bitcast_fusion.5), channel_id=1, source_target_pairs={{0,16},{4,20},{8,24},{12,28},{16,0},{20,4},{24,8},{28,12},{1,17},{... | collective-permute-start | bytes 1572872 | tf_op jit(solution)/shard_map/ppermute | solution.py:94
  368.7 24.3 %collective-permute-start.12 = (f32[2,64,512]{2,1,0:T(8,128)S(1)}, f32[2,64,512]{2,1,0:T(8,128)S(1)}, u32[]{:S(2)}, u32[]{:S(2)}) collective-permute-start(f32[2,64,512]{2,1,0:T(8,128)S(1)} %dynamic-slice_bitcast_fusion.21), channel_id=1, source_target_pairs={{0,16},{4,20},{8,24},{12,28},{16,0},{20,4},{24,8},{28,12},{1,17},{... | collective-permute-start | bytes 786440 | tf_op jit(solution)/shard_map/ppermute | solution.py:94
  376.1 17.1 %collective-permute-start.14 = (f32[2,64,512]{2,1,0:T(8,128)S(1)}, f32[2,64,512]{2,1,0:T(8,128)S(1)}, u32[]{:S(2)}, u32[]{:S(2)}) collective-permute-start(f32[2,64,512]{2,1,0:T(8,128)S(1)} %dynamic-slice_bitcast_fusion.20), channel_id=1, source_target_pairs={{0,8},{4,12},{8,0},{12,4},{16,24},{20,28},{24,16},{28,20},{1,9},{5... | collective-permute-start | bytes 786440 | tf_op jit(solution)/shard_map/ppermute | solution.py:94
  379.9 19.2 %collective-permute-start.32 = (f32[2,64,512]{2,1,0:T(8,128)S(1)}, f32[2,64,512]{2,1,0:T(8,128)S(1)}, u32[]{:S(2)}, u32[]{:S(2)}) collective-permute-start(f32[2,64,512]{2,1,0:T(8,128)S(1)} %dynamic-slice_bitcast_fusion.13), channel_id=1, source_target_pairs={{0,16},{4,20},{8,24},{12,28},{16,0},{20,4},{24,8},{28,12},{1,17},{... | collective-permute-start | bytes 786440 | tf_op jit(solution)/shard_map/ppermute | solution.py:94
  404.2 17.6 %collective-permute-start.38 = (f32[2,64,1024]{2,1,0:T(8,128)S(1)}, f32[2,64,1024]{2,1,0:T(8,128)S(1)}, u32[]{:S(2)}, u32[]{:S(2)}) collective-permute-start(f32[2,64,1024]{2,1,0:T(8,128)S(1)} %pad_maximum_fusion.5), channel_id=1, source_target_pairs={{1,3},{2,0},{5,7},{6,4},{9,11},{10,8},{13,15},{14,12},{17,19},{18,... | collective-permute-start | bytes 1572872 | tf_op jit(solution)/shard_map/ppermute | solution.py:236
  405.6 41.1 %collective-permute-start.15 = (f32[2,2,2,64,1024]{4,3,1,0,2:T(8,128)S(1)}, f32[2,2,2,64,1024]{4,3,1,0,2:T(8,128)S(1)}, u32[]{:S(2)}, u32[]{:S(2)}) collective-permute-start(f32[2,2,2,64,1024]{4,3,1,0,2:T(8,128)S(1)} %bitcast.269), channel_id=1, source_target_pairs={{0,4},{4,0},{8,12},{12,8},{16,20},{20,16},{24,28},{28,24},{1,5},{5... | collective-permute-start | bytes 6291464 | tf_op jit(solution)/shard_map/ppermute | solution.py:94
  409.1 21.6 %collective-permute-start.35 = (f32[2,64,1024]{2,1,0:T(8,128)S(1)}, f32[2,64,1024]{2,1,0:T(8,128)S(1)}, u32[]{:S(2)}, u32[]{:S(2)}) collective-permute-start(f32[2,64,1024]{2,1,0:T(8,128)S(1)} %pad_maximum_fusion.10), channel_id=1, source_target_pairs={{1,3},{2,0},{5,7},{6,4},{9,11},{10,8},{13,15},{14,12},{17,19},{18,... | collective-permute-start | bytes 1572872 | tf_op jit(solution)/shard_map/ppermute | solution.py:236
  447.3 14.9 %collective-permute-start.16 = (f32[2,2,64,512]{3,2,1,0:T(8,128)S(1)}, f32[2,2,64,512]{3,2,1,0:T(8,128)S(1)}, u32[]{:S(2)}, u32[]{:S(2)}) collective-permute-start(f32[2,2,64,512]{3,2,1,0:T(8,128)S(1)} %dynamic-slice_bitcast_fusion.8), channel_id=1, source_target_pairs={{0,8},{4,12},{8,0},{12,4},{16,24},{20,28},{24,16},{28,20},{1,9},{5... | collective-permute-start | bytes 1572872 | tf_op jit(solution)/shard_map/ppermute | solution.py:94
  485.7 30.2 %all-to-all-start = ((f32[8,64,1024]{2,1,0:T(8,128)}), f32[8,64,1024]{2,1,0:T(8,128)S(1)}, u32[]{:S(2)}, u32[]{:S(2)}) async-start(f32[8,64,1024]{2,1,0:T(8,128)} %bitcast.253), calls=%async_computation | async-start | bytes 4194304 | tf_op jit(solution)/shard_map/all_to_all | solution.py:260
  515.9 31.3 %all-to-all-start.1 = ((f32[8,64,1024]{2,1,0:T(8,128)}), f32[8,64,1024]{2,1,0:T(8,128)}, u32[]{:S(2)}, u32[]{:S(2)}) async-start(f32[8,64,1024]{2,1,0:T(8,128)} %bitcast.252), calls=%async_computation.1 | async-start | bytes 4194304 | tf_op jit(solution)/shard_map/all_to_all | solution.py:260
  (44 other events, 471.6 us)
Sparse Core Ops, SparseCore 0:
  14.4 163.4 all-gather.1

commit v2 on v1

v2 whole, which is shorter than its diff:
```python
import functools

import jax
import jax.numpy as jnp
from jax import lax
from jax.experimental import pallas as pl
from jax.experimental.pallas import tpu as pltpu
from jax.sharding import PartitionSpec as P

SMALL = pl.CostEstimate(flops=0, bytes_accessed=0, transcendentals=0)


def assign_pairs(n_col, fronts):
    work = []
    for low in range(n_col):
        for high in range(low + 1, n_col):
            for front in range(fronts):
                middle = low + high - (n_col - 1)
                if high - low == 1:
                    middle = 0
                at_high = middle < 0 or (middle == 0 and front < fronts // 2)
                work.append((high, low, front) if at_high else (low, high, front))
    return work


def line_schedule(n_col, work, fronts, up):
    def fold(plane):
        return plane if up else n_col - 1 - plane

    wanted = {("z", src): n_col - 1 for src in range(n_col - 1)}
    for plane, partner, front in work:
        plane, partner = fold(plane), fold(partner)
        if partner < plane:
            wanted[(front, partner)] = max(wanted.get((front, partner), 0), plane)
    arrived = {key: {key[1]: 0} for key in wanted}
    rank = {"z": 0}
    for order, front in enumerate(range(fronts) if up else reversed(range(fronts))):
        rank[front] = 1 + order
    steps = []
    while True:
        sends = {}
        for plane in range(n_col - 1):
            ready = [
                key for key, last in wanted.items()
                if plane < last and plane in arrived[key] and plane + 1 not in arrived[key]
            ]
            if ready:
                sends[plane] = min(ready, key=lambda k: (k[0] != "z", -k[1] if k[0] == "z" else k[1], rank[k[0]]))
        if not sends:
            break
        steps.append(sends)
        for plane, key in sends.items():
            arrived[key][plane + 1] = len(steps)
    folded = [{fold(p): (k[0], fold(k[1])) for p, k in sends.items()} for sends in steps]
    where_at = {(k[0], fold(k[1])): {fold(p): s for p, s in at.items()} for k, at in arrived.items()}
    return folded, where_at


def color_slots(work, ready):
    slots = []
    load = [sum(it[0] == plane for it in work) for plane in range(1 + max(it[0] for it in work))]
    for item in sorted(work, key=lambda it: (ready[it], -load[it[0]], it)):
        for slot in slots:
            if all(other[0] != item[0] and other[1] != item[1] for other in slot):
                slot.append(item)
                break
        else:
            slots.append([item])
    return sorted(slots, key=lambda slot: max(ready[it] for it in slot))


def choose(index, options):
    groups = []
    for plane, array in options.items():
        for entry in groups:
            if entry[0] is array:
                entry[1].append(plane)
                break
        else:
            groups.append((array, [plane]))
    result = groups[0][0]
    for array, planes in groups[1:]:
        hit = index == planes[0]
        for plane in planes[1:]:
            hit = jnp.logical_or(hit, index == plane)
        result = jnp.where(hit, array, result)
    return result


def tie(value, after):
    return lax.optimization_barrier((value, after))[0]


def swap(part, axis, bit, n_row):
    mine = (lax.axis_index("row") >> bit) & 1
    send = lax.dynamic_index_in_dim(part, 1 - mine, axis, keepdims=False)
    keep = lax.dynamic_index_in_dim(part, mine, axis, keepdims=False)
    return keep + lax.ppermute(send, "row", [(i, i ^ (1 << bit)) for i in range(n_row)])


def reduce_scatter(halves, n_row, bits, after=None):
    other = [(i, i ^ 1) for i in range(n_row)]
    first = jnp.stack([kept + lax.ppermute(sent, "row", other) for kept, sent in halves])
    parts, groups, left_rows, rows, width = first.shape
    first = first.reshape((parts, groups) + (2,) * (bits - 1) + (rows, width))

    def run(piece, order):
        left = sorted(order, reverse=True)
        for bit in order:
            if after is not None and bit == order[-1]:
                piece = tie(piece, after)
            piece = swap(piece, 2 + left.index(bit), bit, n_row)
            left.remove(bit)
        return piece

    half = width // 2
    rest = list(range(1, bits))
    return first, jnp.concatenate([run(first[..., :half], rest), run(first[..., half:], rest[::-1])], axis=-1)


def split(value):
    upper = value.astype(jnp.bfloat16)
    return upper, (value - upper.astype(jnp.float32)).astype(jnp.bfloat16)


def three_pass(left, right, dims):
    (left_up, left_low), (right_up, right_low) = left, right
    dot = functools.partial(lax.dot_general, dimension_numbers=(dims, ((), ())), preferred_element_type=jnp.float32)
    return dot(left_up, right_up) + (dot(left_up, right_low) + dot(left_low, right_up))


def off_block(own, lower_blocks, upper_blocks, where, columns, factor):
    anc_rows, block = own.shape
    depth, width = columns.shape
    n_col = depth // block
    tile = min(256, width)

    def kernel(where, own_ref, *refs):
        lows, highs = refs[:n_col - 1], refs[n_col - 1:2 * n_col - 2]
        cols_ref, factor_ref, out_ref, sum_ref, diag_ref, upper, lower = refs[2 * n_col - 2:]
        hold, first = where[1], where[2]

        def take(shift, ref):
            upper[shift], lower[shift] = split(ref[...])

            @pl.when(lax.rem(where[0] - shift + n_col, n_col) == hold)
            def _():
                place = lax.broadcasted_iota(jnp.int32, ref.shape, 1) - lax.broadcasted_iota(jnp.int32, ref.shape, 0)
                diag_ref[...] = jnp.sum(jnp.where(place == first, ref[...], 0.0), axis=0, keepdims=True)

        @pl.when(pl.program_id(0) == 0)
        def _():
            take(0, own_ref)
            for shift in range(1, n_col):
                pl.when(where[0] >= shift)(functools.partial(take, shift, lows[shift - 1]))
                pl.when(where[0] < shift)(functools.partial(take, shift, highs[n_col - shift - 1]))

        total = jnp.zeros((anc_rows, tile), jnp.float32)
        for shift in range(n_col):
            at = lax.rem(where[0] - shift + n_col, n_col) * block
            right = split(cols_ref[pl.ds(pl.multiple_of(at, block), block), :])
            total -= three_pass((upper[shift], lower[shift]), right, ((1,), (0,)))
        out_ref[...] = total
        sum_ref[...] = -jnp.sum(total * factor_ref[...], axis=0, keepdims=True)

    whole = pl.BlockSpec((anc_rows, block), lambda n, where: (0, 0), pipeline_mode=pl.Buffered(1))
    return pl.pallas_call(
        kernel,
        grid_spec=pltpu.PrefetchScalarGridSpec(
            num_scalar_prefetch=1,
            grid=(width // tile,),
            in_specs=[whole] * (2 * n_col - 1) + [
                pl.BlockSpec((depth, tile), lambda n, where: (0, n)),
                pl.BlockSpec((anc_rows, tile), lambda n, where: (0, n)),
            ],
            out_specs=[
                pl.BlockSpec((anc_rows, tile), lambda n, where: (0, n)),
                pl.BlockSpec((1, tile), lambda n, where: (0, n)),
                pl.BlockSpec((1, block), lambda n, where: (0, 0)),
            ],
            scratch_shapes=[pltpu.VMEM((n_col, anc_rows, block), jnp.bfloat16)] * 2,
        ),
        out_shape=[
            jax.ShapeDtypeStruct((anc_rows, width), jnp.float32),
            jax.ShapeDtypeStruct((1, width), jnp.float32),
            jax.ShapeDtypeStruct((1, block), jnp.float32),
        ],
        compiler_params=pltpu.CompilerParams(vmem_limit_bytes=52 * 1024 * 1024),
        cost_estimate=pl.CostEstimate(
            flops=6 * anc_rows * depth * width, bytes_accessed=4 * (depth + 2 * anc_rows) * width, transcendentals=0
        ),
    )(where, own, *lower_blocks, *upper_blocks, columns, factor)


def partial_block(sides, which, off, front, mine, groups, bits):
    anc_rows, width = sides[0].shape
    tall = width // groups
    rows = tall >> bits

    def kernel(where, *refs):
        side_refs = refs[:len(sides)]
        off_ref, kept_ref, sent_ref, upper, lower, side_up, side_low = refs[len(sides):]

        @pl.when(pl.program_id(0) == 0)
        def _():
            upper[...], lower[...] = split(off_ref[...])

        def take(ref):
            side_up[...], side_low[...] = split(ref[...])

        for number, ref in enumerate(side_refs):
            pl.when(where[2] == number)(functools.partial(take, ref))
        found = three_pass((side_up[...], side_low[...]), (upper[...], lower[...]), ((0,), (0,)))
        found = found.reshape(1 << (bits - 1), 2, rows, width)
        zero = where[1] == 0
        kept_ref[0] = jnp.where(zero, found[:, 0], found[:, 1])
        sent_ref[0] = jnp.where(zero, found[:, 1], found[:, 0])

    out = jax.ShapeDtypeStruct((groups, 1 << (bits - 1), rows, width), jnp.float32)
    out_spec = pl.BlockSpec((1,) + out.shape[1:], lambda h, where: (h, 0, 0, 0))
    return pl.pallas_call(
        kernel,
        grid_spec=pltpu.PrefetchScalarGridSpec(
            num_scalar_prefetch=1,
            grid=(groups,),
            in_specs=[pl.BlockSpec((anc_rows, tall), lambda h, where: (0, h)) for _ in sides] + [
                pl.BlockSpec((anc_rows, width), lambda h, where: (0, where[0])),
            ],
            out_specs=[out_spec, out_spec],
            scratch_shapes=[pltpu.VMEM((anc_rows, width), jnp.bfloat16)] * 2
            + [pltpu.VMEM((anc_rows, tall), jnp.bfloat16)] * 2,
        ),
        out_shape=[out, out],
        compiler_params=pltpu.CompilerParams(vmem_limit_bytes=48 * 1024 * 1024),
        cost_estimate=SMALL,
    )(jnp.stack([front, mine, which]).astype(jnp.int32), *sides, off)


def subtract_blocks(base, found, straight):
    fronts, tall, width = base.shape
    n_row, _, rows, _ = found.shape

    def kernel(flag, base_ref, found_ref, out_ref):
        block = found_ref[...].reshape(tall, tall)

        @pl.when(flag[pl.program_id(0)] == 1)
        def _():
            out_ref[0] = base_ref[0] - block

        @pl.when(flag[pl.program_id(0)] == 0)
        def _():
            out_ref[0] = base_ref[0] - block.T

    spec = pl.BlockSpec((1, tall, tall), lambda k, h, flag: (k, 0, h))
    return pl.pallas_call(
        kernel,
        grid_spec=pltpu.PrefetchScalarGridSpec(
            num_scalar_prefetch=1,
            grid=(fronts, width // tall),
            in_specs=[spec, pl.BlockSpec((n_row, 1, rows, tall), lambda k, h, flag: (0, k, 0, h))],
            out_specs=spec,
        ),
        out_shape=jax.ShapeDtypeStruct(base.shape, base.dtype),
        compiler_params=pltpu.CompilerParams(vmem_limit_bytes=32 * 1024 * 1024),
    )(straight, base, found)


def per_device(anc_inverse, off_factor, diag_inverse, block_mask, edge_child, edge_other):
    fronts, anc_rows, col_width = off_factor.shape
    diag_rows = diag_inverse.shape[1]
    anc_cols = anc_inverse.shape[1]
    row_id = lax.axis_index("row")
    col_id = lax.axis_index("col")
    n_row, n_col = lax.axis_size("row"), lax.axis_size("col")
    groups = col_width // diag_rows
    supercols, ancestor = col_width * n_col, anc_cols * n_col

    keep = jnp.repeat(block_mask, anc_rows // block_mask.shape[1], axis=1).astype(jnp.float32)
    factor = [off_factor[k] * keep[k][:, None] for k in range(fronts)]
    side_by_side = jnp.concatenate(factor, axis=1)
    columns = lax.all_gather(side_by_side, "row", axis=0, tiled=True)

    work = assign_pairs(n_col, fronts)
    plans = {up: line_schedule(n_col, work, fronts, up) for up in (True, False)}
    got = {up: {} for up in plans}
    spots = {up: plans[up][1] for up in plans}
    ready = {
        (plane, partner, front): spots[partner < plane][(front, partner)][plane] for plane, partner, front in work
    }

    def hop(number, after=()):
        earlier = tuple(got[up][number - 1] for up in got if number - 1 in got[up]) or (side_by_side,)
        operands = {}
        for up, (steps, where_at) in plans.items():
            if number > len(steps):
                continue
            options = {}
            for plane, (kind, src) in steps[number - 1].items():
                if src == plane:
                    options[plane] = anc_inverse if kind == "z" else factor[kind]
                else:
                    options[plane] = got[up][where_at[(kind, src)][plane]]
            operands[up] = choose(col_id, options)
        operands = tie(operands, earlier + tuple(after))
        for up, operand in operands.items():
            step = 1 if up else -1
            sends = sorted(plans[up][0][number - 1])
            got[up][number] = lax.ppermute(operand, "col", [(p, p + step) for p in sends])

    for number in range(1, n_col):
        hop(number)
    hop(n_col)
    steps_of = {up: [got[up][step] for step in range(1, n_col)] for up in got}
    owner = row_id * anc_rows // anc_cols
    place = row_id * anc_rows - owner * anc_cols
    off, minus_sums, z_diag = off_block(
        anc_inverse, steps_of[True], steps_of[False], jnp.stack([col_id, owner, place]), columns, side_by_side
    )
    z_far = lax.dynamic_slice_in_dim(z_diag[0], place, anc_rows, 0)
    last = max(len(steps) for steps, where_at in plans.values())
    for number in range(n_col + 1, last + 1):
        hop(number, (off,))

    row_global = row_id * diag_rows + jnp.arange(diag_rows, dtype=jnp.int32)
    col_global = col_id * col_width + jnp.arange(col_width, dtype=jnp.int32)
    hit = row_global[:, None] == col_global[None, :]
    base_diag = jnp.sum(jnp.where(hit, diag_inverse, 0.0), axis=1)
    cc_part = base_diag + minus_sums.reshape(fronts, col_width)
    cc_near = cc_part
    bit = 1
    while bit < n_row:
        cc_near = cc_near + lax.ppermute(cc_near, "row", [(i, i ^ bit) for i in range(n_row)])
        bit *= 2
    cc_rows = lax.dynamic_slice_in_dim(cc_near, row_id % groups * diag_rows, diag_rows, 1)
    cc_far = cc_rows
    for shift in range(1, n_col):
        pairs = []
        for row in range(n_row):
            owner = row // groups
            pairs.append((row * n_col + owner, row * n_col + (owner + shift) % n_col))
        came = lax.ppermute(cc_rows, ("row", "col"), pairs)
        cc_far = jnp.where((col_id - row_id // groups) % n_col == shift, came, cc_far)
    is_child = edge_other < supercols
    at_col = edge_child[:, :, None] == col_global
    at_row = edge_other[:, :, None] == row_global
    at_anc = edge_other[:, :, None] == supercols + row_id * anc_rows + jnp.arange(anc_rows, dtype=jnp.int32)

    def picked(at, values):
        return jnp.sum(jnp.where(at, values, 0.0), axis=-1)

    def mixed_of(at, block):
        rows = jnp.einsum("ker,krc->kec", at.astype(jnp.float32), block, precision=lax.Precision.HIGHEST)
        return picked(at_col, rows)

    off_inverse = jnp.stack([off[:, k * col_width:(k + 1) * col_width] for k in range(fronts)])
    ends = picked(at_col, cc_near[:, None, :]) + picked(at_row, cc_far[:, None, :]) + picked(at_anc, z_far)
    ends = ends - 2.0 * mixed_of(at_anc, off_inverse)

    bits = n_row.bit_length() - 1
    low_bit = row_id & 1
    slots = color_slots(work, ready)
    no = jnp.int32(0)
    if n_col in got[True]:
        off = tie(off, (got[True][n_col], got[False][n_col]))
    halves = [partial_block([factor[k]], no, off, jnp.int32(k), low_bit, groups, bits) for k in range(fronts)]
    first, pieces = reduce_scatter(halves, n_row, bits)
    diag_piece = list(pieces)
    for up in got:
        for step in got[up]:
            if step > n_col:
                got[up][step] = tie(got[up][step], pieces)
    direct, turned = {}, {}
    came = None
    for start in range(0, len(slots), 2):
        halves = []
        for slot in slots[start:start + 2]:
            sides, which, fronts_of = [], {}, {}
            for plane, partner, front in slot:
                side = got[partner < plane][spots[partner < plane][(front, partner)][plane]]
                if not any(side is known for known in sides):
                    sides.append(side)
                which[plane] = [side is known for known in sides].index(True)
                fronts_of[plane] = front
            if slot is slots[1]:
                sides = list(tie(tuple(sides), first))
            table = [jnp.array([of.get(plane, 0) for plane in range(n_col)], jnp.int32)[col_id] for of in (which, fronts_of)]
            halves.append(partial_block(sides, table[0], off, table[1], low_bit, groups, bits))
        pieces = reduce_scatter(halves, n_row, bits, came)[1]
        moved = []
        for slot, piece in zip(slots[start:start + 2], pieces):
            sent = lax.ppermute(piece, "col", [(plane, partner) for plane, partner, front in slot])
            moved.append(sent)
            sent = jnp.stack([
                jnp.concatenate([sent[h][:, g * diag_rows:(g + 1) * diag_rows] for h in range(groups)], axis=1)
                for g in range(groups)
            ])
            for plane, partner, front in slot:
                direct[(plane, partner, front)] = piece
                turned[(partner, plane, front)] = sent
        came = tuple(moved)

    block_id = row_id // groups
    chunks = []
    straight = []
    for k in range(fronts):
        blocks = []
        for block in range(n_col):
            options = {}
            for plane in range(n_col):
                if plane == block:
                    options[plane] = diag_piece[k]
                elif (plane, block, k) in direct:
                    options[plane] = direct[(plane, block, k)]
                else:
                    options[plane] = turned[(plane, block, k)]
            blocks.append(choose(col_id, options))
        chunks.append(jnp.stack(blocks).reshape(n_row, -1, col_width))
        flag = jnp.zeros((), jnp.bool_)
        for plane in range(n_col):
            for block in range(n_col):
                if plane == block or (plane, block, k) in direct:
                    flag = jnp.logical_or(flag, jnp.logical_and(col_id == plane, block_id == block))
        straight.append(flag)
    chunks = tie(jnp.stack(chunks, axis=1), ends)
    found = lax.all_to_all(chunks, "row", 0, 0, tiled=True)
    diag_part = subtract_blocks(diag_inverse, found, jnp.stack(straight).astype(jnp.int32))
    resist = ends - 2.0 * mixed_of(at_row, diag_part)
    return (off_inverse, diag_part, resist)


def solution(mesh):
    placed = (
        P("row", "col"),
        P(None, "row", "col"),
        P(None, "row", "col"),
        P(None, "row"),
        P(None, ("row", "col")),
        P(None, ("row", "col")),
    )
    return jax.shard_map(
        per_device,
        mesh=mesh,
        in_specs=placed,
        out_specs=(P(None, "row", "col"), P(None, "row", "col"), P(None, ("row", "col"))),
        check_vma=False,
    )
```

time: 572 us -> 541 us (0.946); the launches traced: 561 us -> 537 us
  Pallas kernels: 2.65 us -> 90.3 us
  matrix products: 65.1 us -> 7.14 us
  starting transfers between devices: 86.4 us -> 58.5 us
  local copies, waits for them, and re-layouts: 34.8 us -> 14.1 us
    pallas_call x2 -> x8, Pallas kernels: 2.65 us -> 90.3 us  [the longest x6 47.1 us: partial_block(): pl.pallas_call(kernel, grid_spec=pltpu.PrefetchScalarGridSpec(num_scalar_...]
    dot_general x7 -> x0, matrix products: 60.1 us -> none  [the longest x1 33 us: per_device(): off_cat = -jnp.dot(whole_rows, columns, precision=high)]
    ppermute x40 -> x28, waiting for transfers between devices: 243 us -> 203 us  [the longest x10 148 us: hop(): lax.ppermute(operand, 'col', [(p, p + step) for p in sends])]
    ppermute x40 -> x28, starting transfers between devices: 57.2 us -> 36.1 us  [the longest x10 24.7 us: hop(): lax.ppermute(operand, 'col', [(p, p + step) for p in sends])]
    ppermute x3, waiting for transfers between devices: 2.32 us -> 19.7 us  [per_device(): lax.ppermute(cc_near, 'row', [(i, i ^ bit) for i in range(n_row)])]
    ppermute x4, waiting for transfers between devices: 26.9 us -> 40.8 us  [per_device(): lax.ppermute(piece, 'col', [(plane, partner) for plane, partner, front in...]
    squeeze x23 -> x9, local copies, waits for them, and re-layouts: 10.4 us -> 1.47 us  [swap(): send = lax.dynamic_index_in_dim(part, 1 - mine, axis, keepdims=False)]
    all_to_all x2 -> x1, waiting for transfers between devices: 44.3 us -> 49 us  [per_device(): found = lax.all_to_all(chunks, 'row', 0, 0, tiled=True)]
  transfers between devices with their start and end apart: 53 -> 40, of which waited for: 33 -> 23; matrix products, arithmetic and copies ran while one was open for 20% -> 7% of each run, Pallas kernels for 0% -> 14%
where the time goes in v2:
time: 541 us; the launch traced here: 537 us
  waiting for transfers between devices  313 us (58%)
  Pallas kernels  90.3 us (17%)
  starting transfers between devices  58.5 us (11%)
  other arithmetic  38.3 us (7%)
  between operations  15.3 us (3%)
  local copies, waits for them, and re-layouts  14.1 us (3%)
  matrix products  7.14 us (1%)
    ppermute x10, waiting for transfers between devices, hop(): lax.ppermute(operand, 'col', [(p, p + step) for p in sends])  148 us
    ppermute x12, waiting for transfers between devices, swap(): lax.ppermute(send, 'row', [(i, i ^ 1 << bit) for i in range(n_row)])  55 us
    all_to_all x1, waiting for transfers between devices, per_device(): found = lax.all_to_all(chunks, 'row', 0, 0, tiled=True)  49 us
    pallas_call x6, Pallas kernels, partial_block(): pl.pallas_call(kernel, grid_spec=pltpu.PrefetchScalarGridSpec(num_scalar_...  47.1 us
    ppermute x4, waiting for transfers between devices, per_device(): lax.ppermute(piece, 'col', [(plane, partner) for plane, partner, front in...  40.8 us
    pallas_call x1, Pallas kernels, off_block(): pl.pallas_call(kernel, grid_spec=pltpu.PrefetchScalarGridSpec(num_scalar_...  37.6 us
    ppermute x10, starting transfers between devices, hop(): lax.ppermute(operand, 'col', [(p, p + step) for p in sends])  24.7 us
    ppermute x3, waiting for transfers between devices, per_device(): lax.ppermute(cc_near, 'row', [(i, i ^ bit) for i in range(n_row)])  19.7 us
  transfers between devices with their start and end apart: 40, of which 23 were waited for; matrix products, arithmetic and copies ran while one was open for 7% of the time, Pallas kernels for 14%

profile of v2, /device:TPU:0, one launch (start us, length us, event | category | flops | bytes accessed | tf_op | source)
XLA Modules:
  0.0 536.9 jit_solution(7255016110405661975)
XLA Ops:
  14.3 6.3 %collective-permute-start = (f32[512,1024]{1,0:T(8,128)}, f32[512,1024]{1,0:T(8,128)}, u32[]{:S(2)}, u32[]{:S(2)}) collective-permute-start(f32[512,1024]{1,0:T(8,128)} %own_ref.1), channel_id=1, source_target_pairs={{0,1},{1,2},{2,3},{4,5},{5,6},{6,7},{8,9},{9,10},{10,11},{12,13},{... | collective-permute-start | bytes 6291464 | tf_op jit(solution)/shard_map/ppermute | solution.py:308
  21.8 42.6 %collective-permute-done.refs_0_ = f32[512,1024]{1,0:T(8,128)} collective-permute-done((f32[512,1024]{1,0:T(8,128)}, f32[512,1024]{1,0:T(8,128)}, u32[]{:S(2)}, u32[]{:S(2)}) %collective-permute-start) | collective-permute-done | bytes 2097184 | tf_op jit(solution)/shard_map/ppermute | solution.py:308
  66.4 3.4 collective-permute-done.1.refs_3_
  70.2 4.0 collective-permute-start.2
  75.6 42.2 %collective-permute-done.2.refs_1_.refs_0_ = f32[512,1024]{1,0:T(8,128)S(1)} collective-permute-done((f32[512,1024]{1,0:T(8,128)S(1)}, f32[512,1024]{1,0:T(8,128)S(1)}, u32[]{:S(2)}, u32[]{:S(2)}) %collective-permute-start.2) | collective-permute-done | bytes 2097184 | tf_op jit(solution)/shard_map/ppermute | solution.py:308
  123.4 4.7 collective-permute-start.4
  129.5 40.1 %collective-permute-done.4.refs_2_.refs_1_ = f32[512,1024]{1,0:T(8,128)} collective-permute-done((f32[512,1024]{1,0:T(8,128)}, f32[512,1024]{1,0:T(8,128)}, u32[]{:S(2)}, u32[]{:S(2)}) %collective-permute-start.4) | collective-permute-done | bytes 2097184 | tf_op jit(solution)/shard_map/ppermute | solution.py:308
  169.7 5.2 collective-permute-done.5.refs_5_.refs_0_
  178.3 37.6 %shard_map.157 = (f32[512,2048]{1,0:T(8,128)}, f32[1,2048]{1,0:T(1,128)S(1)}, f32[1,1024]{1,0:T(1,128)S(1)}) custom-call(s32[3]{0:T(128)S(1)} %pad_add_fusion.2.where, f32[512,1024]{1,0:T(8,128)} %own_ref.1, f32[512,1024]{1,0:T(8,128)} %collective-permute-done.refs_0_, f32[512,1024]{1,0:T(8,128)} %copy-done.13, ...), custom_call_target="tpu_custom_call" | custom-call | flops 25769803776 | bytes 41943040 | tf_op jit(solution)/shard_map/pallas_call | solution.py:167
  216.0 7.0 %collective-permute-done.7.refs_0_ = f32[512,1024]{1,0:T(8,128)} collective-permute-done((f32[512,1024]{1,0:T(8,128)}, f32[512,1024]{1,0:T(8,128)}, u32[]{:S(2)}, u32[]{:S(2)}) %collective-permute-start.7) | collective-permute-done | bytes 2097184 | tf_op jit(solution)/shard_map/ppermute | solution.py:308
  222.9 7.7 %shard_map.158 = (f32[2,4,64,1024]{3,2,1,0:T(8,128)S(1)}, f32[2,4,64,1024]{3,2,1,0:T(8,128)}) custom-call(s32[3]{0:T(128)S(1)} %get-tuple-element.120.where, f32[512,1024]{1,0:T(8,128)} %copy-done.9, f32[512,2048]{1,0:T(8,128)} %get-tuple-element.46.refs_1_.refs_4_.refs_2_), custom_call_target="tpu_custom_call" | custom-call | tf_op jit(solution)/shard_map/pallas_call | solution.py:221
  230.7 7.9 %shard_map.159 = (f32[2,4,64,1024]{3,2,1,0:T(8,128)S(1)}, f32[2,4,64,1024]{3,2,1,0:T(8,128)}) custom-call(s32[3]{0:T(128)S(1)} %get-tuple-element.119.where, f32[512,1024]{1,0:T(8,128)} %copy-done.7, f32[512,2048]{1,0:T(8,128)} %get-tuple-element.46.refs_1_.refs_4_.refs_2_), custom_call_target="tpu_custom_call" | custom-call | tf_op jit(solution)/shard_map/pallas_call | solution.py:221
  247.7 8.3 %shard_map.162 = (f32[2,4,64,1024]{3,2,1,0:T(8,128)S(1)}, f32[2,4,64,1024]{3,2,1,0:T(8,128)}) custom-call(s32[3]{0:T(128)S(1)} %add_add_fusion.where, f32[512,1024]{1,0:T(8,128)} %collective-permute-done.5.refs_5_.refs_0_, f32[512,1024]{1,0:T(8,128)} %collective-permute-done.4.refs_2_.refs_1_, f32[512,2048]{1,0:T(8,128)} %get-tuple-element.46.refs_1_.refs_4_.refs_2_), custom_call_target="tpu_custom_call" | custom-call | tf_op jit(solution)/shard_map/pallas_call | solution.py:221
  264.0 7.1 %shard_map.163 = (f32[2,4,64,1024]{3,2,1,0:T(8,128)S(1)}, f32[2,4,64,1024]{3,2,1,0:T(8,128)S(1)}) custom-call(s32[3]{0:T(128)S(1)} %add_add_fusion.1.where, f32[512,1024]{1,0:T(8,128)} %collective-permute-done.7.refs_0_, f32[512,1024]{1,0:T(8,128)} %collective-permute-done.6.refs_1_, f32[512,2048]{1,0:T(8,128)} %get-tuple-element.46.refs_1_.refs_4_.refs_2_), custom_call_target="tpu_custom_call" | custom-call | tf_op jit(solution)/shard_map/pallas_call | solution.py:221
  277.7 19.7 %collective-permute-done.33 = f32[2,1024]{1,0:T(2,128)S(1)} collective-permute-done((f32[2,1024]{1,0:T(2,128)S(1)}, f32[2,1024]{1,0:T(2,128)S(1)}, u32[]{:S(2)}, u32[]{:S(2)}) %collective-permute-start.33) | collective-permute-done | bytes 8224 | tf_op jit(solution)/shard_map/ppermute | solution.py:332
  313.4 6.6 %collective-permute-done.12 = f32[2,2,64,512]{3,2,1,0:T(8,128)S(1)} collective-permute-done((f32[2,2,64,512]{3,2,1,0:T(8,128)S(1)}, f32[2,2,64,512]{3,2,1,0:T(8,128)S(1)}, u32[]{:S(2)}, u32[]{:S(2)}) %collective-permute-start.12) | collective-permute-done | bytes 524320 | tf_op jit(solution)/shard_map/ppermute | solution.py:98
  321.1 24.3 %collective-permute-done.14 = f32[2,2,64,512]{3,2,1,0:T(8,128)S(1)} collective-permute-done((f32[2,2,64,512]{3,2,1,0:T(8,128)S(1)}, f32[2,2,64,512]{3,2,1,0:T(8,128)S(1)}, u32[]{:S(2)}, u32[]{:S(2)}) %collective-permute-start.14) | collective-permute-done | bytes 524320 | tf_op jit(solution)/shard_map/ppermute | solution.py:98
  346.8 4.9 collective-permute-done.8.refs_2_
  351.7 8.1 %shard_map.161 = (f32[2,4,64,1024]{3,2,1,0:T(8,128)S(1)}, f32[2,4,64,1024]{3,2,1,0:T(8,128)S(1)}) custom-call(s32[3]{0:T(128)S(1)} %pad_add_fusion.4.where, f32[512,1024]{1,0:T(8,128)} %collective-permute-done.7.refs_0_, f32[512,1024]{1,0:T(8,128)} %collective-permute-done.6.refs_1_, f32[512,1024]{1,0:T(8,128)} %collective-permute-done.8.refs_2_, ...), custom_call_target="tpu_custom_call" | custom-call | tf_op jit(solution)/shard_map/pallas_call | solution.py:221
  359.9 8.1 %shard_map.160 = (f32[2,4,64,1024]{3,2,1,0:T(8,128)S(1)}, f32[2,4,64,1024]{3,2,1,0:T(8,128)S(1)}) custom-call(s32[3]{0:T(128)S(1)} %pad_add_fusion.3.where, f32[512,1024]{1,0:T(8,128)} %copy-done.13, f32[512,1024]{1,0:T(8,128)} %copy-done.14, f32[512,1024]{1,0:T(8,128)} %collective-permute-done.8.refs_2_, f32[512,1024]{1,0:T(8,128)} %copy-done.15, ...), custom_call_target="tpu_custom_call" | custom-call | tf_op jit(solution)/shard_map/pallas_call | solution.py:221
  375.0 3.2 collective-permute-start.37
  380.0 7.2 %collective-permute-done.22 = f32[2,2,64,512]{3,2,1,0:T(8,128)S(1)} collective-permute-done((f32[2,2,64,512]{3,2,1,0:T(8,128)S(1)}, f32[2,2,64,512]{3,2,1,0:T(8,128)S(1)}, u32[]{:S(2)}, u32[]{:S(2)}) %collective-permute-start.22) | collective-permute-done | bytes 524320 | tf_op jit(solution)/shard_map/ppermute | solution.py:98
  387.3 4.5 collective-permute-done.24
  398.1 11.4 %collective-permute-done.26 = f32[2,64,1024]{2,1,0:T(8,128)S(1)} collective-permute-done((f32[2,64,1024]{2,1,0:T(8,128)S(1)}, f32[2,64,1024]{2,1,0:T(8,128)S(1)}, u32[]{:S(2)}, u32[]{:S(2)}) %collective-permute-start.26) | collective-permute-done | bytes 524320 | tf_op jit(solution)/shard_map/ppermute | solution.py:391
  409.6 8.7 %collective-permute-done.25 = f32[2,64,1024]{2,1,0:T(8,128)S(1)} collective-permute-done((f32[2,64,1024]{2,1,0:T(8,128)S(1)}, f32[2,64,1024]{2,1,0:T(8,128)S(1)}, u32[]{:S(2)}, u32[]{:S(2)}) %collective-permute-start.25) | collective-permute-done | bytes 524320 | tf_op jit(solution)/shard_map/ppermute | solution.py:391
  425.3 7.6 %collective-permute-done.27 = f32[2,2,64,512]{3,2,1,0:T(8,128)S(1)} collective-permute-done((f32[2,2,64,512]{3,2,1,0:T(8,128)S(1)}, f32[2,2,64,512]{3,2,1,0:T(8,128)S(1)}, u32[]{:S(2)}, u32[]{:S(2)}) %collective-permute-start.27) | collective-permute-done | bytes 524320 | tf_op jit(solution)/shard_map/ppermute | solution.py:98
  438.6 10.7 %collective-permute-done.30 = f32[2,64,1024]{2,1,0:T(8,128)S(1)} collective-permute-done((f32[2,64,1024]{2,1,0:T(8,128)S(1)}, f32[2,64,1024]{2,1,0:T(8,128)S(1)}, u32[]{:S(2)}, u32[]{:S(2)}) %collective-permute-start.30) | collective-permute-done | bytes 524320 | tf_op jit(solution)/shard_map/ppermute | solution.py:391
  449.4 10.0 %collective-permute-done.31 = f32[2,64,1024]{2,1,0:T(8,128)S(1)} collective-permute-done((f32[2,64,1024]{2,1,0:T(8,128)S(1)}, f32[2,64,1024]{2,1,0:T(8,128)S(1)}, u32[]{:S(2)}, u32[]{:S(2)}) %collective-permute-start.31) | collective-permute-done | bytes 524320 | tf_op jit(solution)/shard_map/ppermute | solution.py:391
  463.2 4.6 all-to-all-start
  467.9 49.0 %all-to-all-done.found_ref = f32[8,2,64,1024]{3,2,1,0:T(8,128)} async-done(((f32[8,2,64,1024]{3,2,1,0:T(8,128)}), f32[8,2,64,1024]{3,2,1,0:T(8,128)}, u32[]{:S(2)}, u32[]{:S(2)}) %all-to-all-start) | async-done | bytes 4194336 | tf_op jit(solution)/shard_map/all_to_all | solution.py:425
  519.1 5.5 %shard_map.164 = f32[2,512,1024]{2,1,0:T(8,128)} custom-call(s32[2]{0:T(128)S(1)} %add_convert_fusion.flag, f32[2,512,1024]{2,1,0:T(8,128)S(1)} %copy-done.1, f32[8,2,64,1024]{3,2,1,0:T(8,128)} %all-to-all-done.found_ref), custom_call_target="tpu_custom_call" | custom-call | tf_op jit(solution)/shard_map/pallas_call | solution.py:255
  524.7 4.6 fusion.2
  (212 shorter events, 98.8 us)
Async XLA Ops:
  7.2 171.2 %all-gather.2.cloned.1.call-start = ((), (), s32[]{:S(2)}) async-start(), calls=%async_computation.1 | async-start | bytes 37748736 | tf_op jit(solution)/shard_map/all_gather | solution.py:281
  14.3 50.1 %collective-permute-start = (f32[512,1024]{1,0:T(8,128)}, f32[512,1024]{1,0:T(8,128)}, u32[]{:S(2)}, u32[]{:S(2)}) collective-permute-start(f32[512,1024]{1,0:T(8,128)} %own_ref.1), channel_id=1, source_target_pairs={{0,1},{1,2},{2,3},{4,5},{5,6},{6,7},{8,9},{9,10},{10,11},{12,13},{... | collective-permute-start | bytes 6291464 | tf_op jit(solution)/shard_map/ppermute | solution.py:308
  20.5 49.3 %collective-permute-start.1 = (f32[512,1024]{1,0:T(8,128)}, f32[512,1024]{1,0:T(8,128)}, u32[]{:S(2)}, u32[]{:S(2)}) collective-permute-start(f32[512,1024]{1,0:T(8,128)} %own_ref.1), channel_id=1, source_target_pairs={{1,0},{2,1},{3,2},{5,4},{6,5},{7,6},{9,8},{10,9},{11,10},{13,12},{... | collective-permute-start | bytes 6291464 | tf_op jit(solution)/shard_map/ppermute | solution.py:308
  70.2 47.6 %collective-permute-start.2 = (f32[512,1024]{1,0:T(8,128)S(1)}, f32[512,1024]{1,0:T(8,128)S(1)}, u32[]{:S(2)}, u32[]{:S(2)}) collective-permute-start(f32[512,1024]{1,0:T(8,128)S(1)} %broadcast_select_fusion.2), channel_id=1, source_target_pairs={{0,1},{1,2},{2,3},{4,5},{5,6},{6,7},{8,9},{9,10},{10,11},{12,13},{... | collective-permute-start | bytes 6291464 | tf_op jit(solution)/shard_map/ppermute | solution.py:308
  74.3 47.8 %collective-permute-start.3 = (f32[512,1024]{1,0:T(8,128)S(1)}, f32[512,1024]{1,0:T(8,128)S(1)}, u32[]{:S(2)}, u32[]{:S(2)}) collective-permute-start(f32[512,1024]{1,0:T(8,128)S(1)} %broadcast_select_fusion.3), channel_id=1, source_target_pairs={{1,0},{2,1},{3,2},{5,4},{6,5},{7,6},{9,8},{10,9},{11,10},{13,12},{... | collective-permute-start | bytes 6291464 | tf_op jit(solution)/shard_map/ppermute | solution.py:308
  123.4 46.2 %collective-permute-start.4 = (f32[512,1024]{1,0:T(8,128)}, f32[512,1024]{1,0:T(8,128)}, u32[]{:S(2)}, u32[]{:S(2)}) collective-permute-start(f32[512,1024]{1,0:T(8,128)} %broadcast_select_fusion), channel_id=1, source_target_pairs={{0,1},{1,2},{2,3},{4,5},{5,6},{6,7},{8,9},{9,10},{10,11},{12,13},{... | collective-permute-start | bytes 6291464 | tf_op jit(solution)/shard_map/ppermute | solution.py:308
  128.1 46.8 %collective-permute-start.5 = (f32[512,1024]{1,0:T(8,128)S(1)}, f32[512,1024]{1,0:T(8,128)}, u32[]{:S(2)}, u32[]{:S(2)}) collective-permute-start(f32[512,1024]{1,0:T(8,128)S(1)} %broadcast_select_fusion.1), channel_id=1, source_target_pairs={{1,0},{2,1},{3,2},{5,4},{6,5},{7,6},{9,8},{10,9},{11,10},{13,12},{... | collective-permute-start | bytes 6291464 | tf_op jit(solution)/shard_map/ppermute | solution.py:308
  174.9 41.1 %collective-permute-start.6 = (f32[512,1024]{1,0:T(8,128)}, f32[512,1024]{1,0:T(8,128)}, u32[]{:S(2)}, u32[]{:S(2)}) collective-permute-start(f32[512,1024]{1,0:T(8,128)} %collective-permute-done.4.refs_2_.refs_1_), channel_id=1, source_target_pairs={{1,2},{2,3},{5,6},{6,7},{9,10},{10,11},{13,14},{14,15},{17,18},{18... | collective-permute-start | bytes 6291464 | tf_op jit(solution)/shard_map/ppermute | solution.py:308
  176.8 46.1 %collective-permute-start.7 = (f32[512,1024]{1,0:T(8,128)}, f32[512,1024]{1,0:T(8,128)}, u32[]{:S(2)}, u32[]{:S(2)}) collective-permute-start(f32[512,1024]{1,0:T(8,128)} %collective-permute-done.5.refs_5_.refs_0_), channel_id=1, source_target_pairs={{1,0},{2,1},{5,4},{6,5},{9,8},{10,9},{13,12},{14,13},{17,16},{18,1... | collective-permute-start | bytes 6291464 | tf_op jit(solution)/shard_map/ppermute | solution.py:308
  230.6 29.1 %collective-permute-start.9 = (f32[2,4,64,1024]{3,2,1,0:T(8,128)}, f32[2,4,64,1024]{3,2,1,0:T(8,128)}, u32[]{:S(2)}, u32[]{:S(2)}) collective-permute-start(f32[2,4,64,1024]{3,2,1,0:T(8,128)} %get-tuple-element.48), channel_id=1, source_target_pairs={{0,4},{4,0},{8,12},{12,8},{16,20},{20,16},{24,28},{28,24},{1,5},{5... | collective-permute-start | bytes 6291464 | tf_op jit(solution)/shard_map/ppermute | solution.py:103
  239.9 22.0 %collective-permute-start.10 = (f32[2,4,64,1024]{3,2,1,0:T(8,128)}, f32[2,4,64,1024]{3,2,1,0:T(8,128)}, u32[]{:S(2)}, u32[]{:S(2)}) collective-permute-start(f32[2,4,64,1024]{3,2,1,0:T(8,128)} %get-tuple-element.50), channel_id=1, source_target_pairs={{0,4},{4,0},{8,12},{12,8},{16,20},{20,16},{24,28},{28,24},{1,5},{5... | collective-permute-start | bytes 6291464 | tf_op jit(solution)/shard_map/ppermute | solution.py:103
  256.0 46.4 %collective-permute-start.19 = (f32[2,4,64,1024]{3,2,1,0:T(8,128)}, f32[2,4,64,1024]{3,2,1,0:T(8,128)}, u32[]{:S(2)}, u32[]{:S(2)}) collective-permute-start(f32[2,4,64,1024]{3,2,1,0:T(8,128)} %get-tuple-element.59), channel_id=1, source_target_pairs={{0,4},{4,0},{8,12},{12,8},{16,20},{20,16},{24,28},{28,24},{1,5},{5... | collective-permute-start | bytes 6291464 | tf_op jit(solution)/shard_map/ppermute | solution.py:103
  259.2 14.6 %collective-permute-start.32 = (f32[2,1024]{1,0:T(2,128)S(1)}, f32[2,1024]{1,0:T(2,128)S(1)}, u32[]{:S(2)}, u32[]{:S(2)}) collective-permute-start(f32[2,1024]{1,0:T(2,128)S(1)} %add.201), channel_id=1, source_target_pairs={{0,4},{4,0},{8,12},{12,8},{16,20},{20,16},{24,28},{28,24},{1,5},{5... | collective-permute-start | bytes 24584 | tf_op jit(solution)/shard_map/ppermute | solution.py:332
  271.0 37.1 %collective-permute-start.20 = (f32[2,4,64,1024]{3,2,1,0:T(8,128)S(1)}, f32[2,4,64,1024]{3,2,1,0:T(8,128)S(1)}, u32[]{:S(2)}, u32[]{:S(2)}) collective-permute-start(f32[2,4,64,1024]{3,2,1,0:T(8,128)S(1)} %get-tuple-element.63), channel_id=1, source_target_pairs={{0,4},{4,0},{8,12},{12,8},{16,20},{20,16},{24,28},{28,24},{1,5},{5... | collective-permute-start | bytes 6291464 | tf_op jit(solution)/shard_map/ppermute | solution.py:103
  271.7 34.6 %collective-permute-start.11 = (f32[2,2,2,64,512]{4,3,2,1,0:T(8,128)S(1)}, f32[2,2,2,64,512]{4,3,2,1,0:T(8,128)S(1)}, u32[]{:S(2)}, u32[]{:S(2)}) collective-permute-start(f32[2,2,2,64,512]{4,3,2,1,0:T(8,128)S(1)} %dynamic-slice_bitcast_fusion.2), channel_id=1, source_target_pairs={{0,8},{4,12},{8,0},{12,4},{16,24},{20,28},{24,16},{28,20},{1,9},{5... | collective-permute-start | bytes 3145736 | tf_op jit(solution)/shard_map/ppermute | solution.py:98
  273.8 23.7 %collective-permute-start.33 = (f32[2,1024]{1,0:T(2,128)S(1)}, f32[2,1024]{1,0:T(2,128)S(1)}, u32[]{:S(2)}, u32[]{:S(2)}) collective-permute-start(f32[2,1024]{1,0:T(2,128)S(1)} %add.202), channel_id=1, source_target_pairs={{0,8},{4,12},{8,0},{12,4},{16,24},{20,28},{24,16},{28,20},{1,9},{5... | collective-permute-start | bytes 24584 | tf_op jit(solution)/shard_map/ppermute | solution.py:332
  275.7 32.1 %collective-permute-start.13 = (f32[2,2,2,64,512]{4,3,2,1,0:T(8,128)S(1)}, f32[2,2,2,64,512]{4,3,2,1,0:T(8,128)S(1)}, u32[]{:S(2)}, u32[]{:S(2)}) collective-permute-start(f32[2,2,2,64,512]{4,3,2,1,0:T(8,128)S(1)} %bitcast.158), channel_id=1, source_target_pairs={{0,16},{4,20},{8,24},{12,28},{16,0},{20,4},{24,8},{28,12},{1,17},{... | collective-permute-start | bytes 3145736 | tf_op jit(solution)/shard_map/ppermute | solution.py:98
  301.6 43.9 %collective-permute-start.15 = (f32[512,1024]{1,0:T(8,128)S(1)}, f32[512,1024]{1,0:T(8,128)S(1)}, u32[]{:S(2)}, u32[]{:S(2)}) collective-permute-start(f32[512,1024]{1,0:T(8,128)S(1)} %copy-done.11), channel_id=1, source_target_pairs={{1,2},{2,3},{5,6},{6,7},{9,10},{10,11},{13,14},{14,15},{17,18},{18... | collective-permute-start | bytes 6291464 | tf_op jit(solution)/shard_map/ppermute | solution.py:308
  302.4 49.3 %collective-permute-start.8 = (f32[512,1024]{1,0:T(8,128)S(1)}, f32[512,1024]{1,0:T(8,128)}, u32[]{:S(2)}, u32[]{:S(2)}) collective-permute-start(f32[512,1024]{1,0:T(8,128)S(1)} %copy-done.8), channel_id=1, source_target_pairs={{1,0},{2,1},{5,4},{6,5},{9,8},{10,9},{13,12},{14,13},{17,16},{18,1... | collective-permute-start | bytes 6291464 | tf_op jit(solution)/shard_map/ppermute | solution.py:308
  309.8 60.8 %collective-permute-start.21 = (f32[2,2,2,64,512]{4,3,2,1,0:T(8,128)}, f32[2,2,2,64,512]{4,3,2,1,0:T(8,128)}, u32[]{:S(2)}, u32[]{:S(2)}) collective-permute-start(f32[2,2,2,64,512]{4,3,2,1,0:T(8,128)} %dynamic-slice_bitcast_fusion), channel_id=1, source_target_pairs={{0,8},{4,12},{8,0},{12,4},{16,24},{20,28},{24,16},{28,20},{1,9},{5... | collective-permute-start | bytes 3145736 | tf_op jit(solution)/shard_map/ppermute | solution.py:98
  311.4 34.1 %collective-permute-start.14 = (f32[2,2,64,512]{3,2,1,0:T(8,128)S(1)}, f32[2,2,64,512]{3,2,1,0:T(8,128)S(1)}, u32[]{:S(2)}, u32[]{:S(2)}) collective-permute-start(f32[2,2,64,512]{3,2,1,0:T(8,128)S(1)} %dynamic-slice_bitcast_fusion.7), channel_id=1, source_target_pairs={{0,8},{4,12},{8,0},{12,4},{16,24},{20,28},{24,16},{28,20},{1,9},{5... | collective-permute-start | bytes 1572872 | tf_op jit(solution)/shard_map/ppermute | solution.py:98
  320.0 53.5 %collective-permute-start.23 = (f32[2,2,2,64,512]{4,3,2,1,0:T(8,128)}, f32[2,2,2,64,512]{4,3,2,1,0:T(8,128)}, u32[]{:S(2)}, u32[]{:S(2)}) collective-permute-start(f32[2,2,2,64,512]{4,3,2,1,0:T(8,128)} %fusion.10), channel_id=1, source_target_pairs={{0,16},{4,20},{8,24},{12,28},{16,0},{20,4},{24,8},{28,12},{1,17},{... | collective-permute-start | bytes 3145736 | tf_op jit(solution)/shard_map/ppermute | solution.py:98
  359.8 33.4 %collective-permute-start.17 = (f32[2,4,64,1024]{3,2,1,0:T(8,128)S(1)}, f32[2,4,64,1024]{3,2,1,0:T(8,128)}, u32[]{:S(2)}, u32[]{:S(2)}) collective-permute-start(f32[2,4,64,1024]{3,2,1,0:T(8,128)S(1)} %get-tuple-element.57), channel_id=1, source_target_pairs={{0,4},{4,0},{8,12},{12,8},{16,20},{20,16},{24,28},{28,24},{1,5},{5... | collective-permute-start | bytes 6291464 | tf_op jit(solution)/shard_map/ppermute | solution.py:103
  368.0 27.4 %collective-permute-start.16 = (f32[2,4,64,1024]{3,2,1,0:T(8,128)S(1)}, f32[2,4,64,1024]{3,2,1,0:T(8,128)S(1)}, u32[]{:S(2)}, u32[]{:S(2)}) collective-permute-start(f32[2,4,64,1024]{3,2,1,0:T(8,128)S(1)} %get-tuple-element.55), channel_id=1, source_target_pairs={{0,4},{4,0},{8,12},{12,8},{16,20},{20,16},{24,28},{28,24},{1,5},{5... | collective-permute-start | bytes 6291464 | tf_op jit(solution)/shard_map/ppermute | solution.py:103
  373.5 13.7 %collective-permute-start.22 = (f32[2,2,64,512]{3,2,1,0:T(8,128)S(1)}, f32[2,2,64,512]{3,2,1,0:T(8,128)S(1)}, u32[]{:S(2)}, u32[]{:S(2)}) collective-permute-start(f32[2,2,64,512]{3,2,1,0:T(8,128)S(1)} %dynamic-slice_bitcast_fusion.6), channel_id=1, source_target_pairs={{0,16},{4,20},{8,24},{12,28},{16,0},{20,4},{24,8},{28,12},{1,17},{... | collective-permute-start | bytes 1572872 | tf_op jit(solution)/shard_map/ppermute | solution.py:98
  391.9 17.7 %collective-permute-start.26 = (f32[2,64,1024]{2,1,0:T(8,128)S(1)}, f32[2,64,1024]{2,1,0:T(8,128)S(1)}, u32[]{:S(2)}, u32[]{:S(2)}) collective-permute-start(f32[2,64,1024]{2,1,0:T(8,128)S(1)} %get-tuple-element.91), channel_id=1, source_target_pairs={{1,3},{2,0},{5,7},{6,4},{9,11},{10,8},{13,15},{14,12},{17,19},{18,... | collective-permute-start | bytes 1572872 | tf_op jit(solution)/shard_map/ppermute | solution.py:391
  396.1 23.7 %collective-permute-start.18 = (f32[2,2,2,64,512]{4,3,2,1,0:T(8,128)S(1)}, f32[2,2,2,64,512]{4,3,2,1,0:T(8,128)S(1)}, u32[]{:S(2)}, u32[]{:S(2)}) collective-permute-start(f32[2,2,2,64,512]{4,3,2,1,0:T(8,128)S(1)} %dynamic-slice_bitcast_fusion.1), channel_id=1, source_target_pairs={{0,8},{4,12},{8,0},{12,4},{16,24},{20,28},{24,16},{28,20},{1,9},{5... | collective-permute-start | bytes 3145736 | tf_op jit(solution)/shard_map/ppermute | solution.py:98
  396.4 21.9 %collective-permute-start.25 = (f32[2,64,1024]{2,1,0:T(8,128)S(1)}, f32[2,64,1024]{2,1,0:T(8,128)S(1)}, u32[]{:S(2)}, u32[]{:S(2)}) collective-permute-start(f32[2,64,1024]{2,1,0:T(8,128)S(1)} %get-tuple-element.92), channel_id=1, source_target_pairs={{1,3},{2,0},{5,7},{6,4},{9,11},{10,8},{13,15},{14,12},{17,19},{18,... | collective-permute-start | bytes 1572872 | tf_op jit(solution)/shard_map/ppermute | solution.py:391
  398.0 25.0 %collective-permute-start.28 = (f32[2,2,2,64,512]{4,3,2,1,0:T(8,128)S(1)}, f32[2,2,2,64,512]{4,3,2,1,0:T(8,128)S(1)}, u32[]{:S(2)}, u32[]{:S(2)}) collective-permute-start(f32[2,2,2,64,512]{4,3,2,1,0:T(8,128)S(1)} %fusion.15), channel_id=1, source_target_pairs={{0,16},{4,20},{8,24},{12,28},{16,0},{20,4},{24,8},{28,12},{1,17},{... | collective-permute-start | bytes 3145736 | tf_op jit(solution)/shard_map/ppermute | solution.py:98
  433.8 15.5 %collective-permute-start.30 = (f32[2,64,1024]{2,1,0:T(8,128)S(1)}, f32[2,64,1024]{2,1,0:T(8,128)S(1)}, u32[]{:S(2)}, u32[]{:S(2)}) collective-permute-start(f32[2,64,1024]{2,1,0:T(8,128)S(1)} %bitcast.157), channel_id=1, source_target_pairs={{1,0},{2,3},{0,1},{3,2},{5,4},{6,7},{4,5},{7,6},{9,8},{10,11},{8,9... | collective-permute-start | bytes 1572872 | tf_op jit(solution)/shard_map/ppermute | solution.py:391
  437.0 22.3 %collective-permute-start.31 = (f32[2,64,1024]{2,1,0:T(8,128)S(1)}, f32[2,64,1024]{2,1,0:T(8,128)S(1)}, u32[]{:S(2)}, u32[]{:S(2)}) collective-permute-start(f32[2,64,1024]{2,1,0:T(8,128)S(1)} %bitcast.156), channel_id=1, source_target_pairs={{0,3},{3,0},{1,2},{2,1},{4,7},{7,4},{5,6},{6,5},{8,11},{11,8},{9,1... | collective-permute-start | bytes 1572872 | tf_op jit(solution)/shard_map/ppermute | solution.py:391
  463.2 53.7 %all-to-all-start = ((f32[8,2,64,1024]{3,2,1,0:T(8,128)}), f32[8,2,64,1024]{3,2,1,0:T(8,128)}, u32[]{:S(2)}, u32[]{:S(2)}) async-start(f32[8,2,64,1024]{3,2,1,0:T(8,128)} %pad_maximum_fusion.3), calls=%async_computation | async-start | bytes 8388608 | tf_op jit(solution)/shard_map/all_to_all | solution.py:425
  (32 other events, 427.9 us)
Sparse Core Ops, SparseCore 0:
  14.4 163.4 all-gather.1

commit v3 on v2

v3 whole, which is shorter than its diff:
```python
import functools

import jax
import jax.numpy as jnp
from jax import lax
from jax.experimental import pallas as pl
from jax.experimental.pallas import tpu as pltpu
from jax.sharding import PartitionSpec as P

SMALL = pl.CostEstimate(flops=1, bytes_accessed=1, transcendentals=0)


def assign_pairs(n_col, fronts):
    work = []
    for low in range(n_col):
        for high in range(low + 1, n_col):
            for front in range(fronts):
                middle = low + high - (n_col - 1)
                if high - low == 1:
                    middle = 0
                at_high = middle < 0 or (middle == 0 and front < fronts // 2)
                work.append((high, low, front) if at_high else (low, high, front))
    return work


def line_schedule(n_col, work, fronts, up):
    def fold(plane):
        return plane if up else n_col - 1 - plane

    wanted = {("z", src): n_col - 1 for src in range(n_col - 1)}
    for plane, partner, front in work:
        plane, partner = fold(plane), fold(partner)
        if partner < plane:
            wanted[(front, partner)] = max(wanted.get((front, partner), 0), plane)
    arrived = {key: {key[1]: 0} for key in wanted}
    rank = {"z": 0}
    for front in range(fronts):
        rank[front] = 1 + front
    steps = []
    while True:
        sends = {}
        for plane in range(n_col - 1):
            ready = [
                key for key, last in wanted.items()
                if plane < last and plane in arrived[key] and plane + 1 not in arrived[key]
            ]
            if ready:
                sends[plane] = min(ready, key=lambda k: (k[0] != "z", -k[1] if k[0] == "z" else k[1], rank[k[0]]))
        if not sends:
            break
        steps.append(sends)
        for plane, key in sends.items():
            arrived[key][plane + 1] = len(steps)
    folded = [{fold(p): (k[0], fold(k[1])) for p, k in sends.items()} for sends in steps]
    where_at = {(k[0], fold(k[1])): {fold(p): s for p, s in at.items()} for k, at in arrived.items()}
    return folded, where_at


def color_slots(work, ready):
    slots = []
    load = [sum(it[0] == plane for it in work) for plane in range(1 + max(it[0] for it in work))]
    for item in sorted(work, key=lambda it: (ready[it], -load[it[0]], it)):
        for slot in slots:
            if all(other[0] != item[0] and other[1] != item[1] for other in slot):
                slot.append(item)
                break
        else:
            slots.append([item])
    return sorted(slots, key=lambda slot: max(ready[it] for it in slot))


def choose(index, options):
    groups = []
    for plane, array in options.items():
        for entry in groups:
            if entry[0] is array:
                entry[1].append(plane)
                break
        else:
            groups.append((array, [plane]))
    result = groups[0][0]
    for array, planes in groups[1:]:
        hit = index == planes[0]
        for plane in planes[1:]:
            hit = jnp.logical_or(hit, index == plane)
        result = jnp.where(hit, array, result)
    return result


ANYWHERE = pl.BlockSpec(memory_space=pl.ANY)


def tie(values, after):
    values, after = tuple(values), tuple(after)

    def kernel(*refs):
        del refs

    return pl.pallas_call(
        kernel,
        in_specs=[ANYWHERE] * (len(values) + len(after)),
        out_specs=[ANYWHERE] * len(values),
        out_shape=[jax.ShapeDtypeStruct(value.shape, value.dtype) for value in values],
        input_output_aliases={at: at for at in range(len(values))},
        cost_estimate=SMALL,
    )(*values, *after)


def pick(index, options, after=()):
    arrays, number = [], {}
    for plane, array in options.items():
        if not any(array is other for other in arrays):
            arrays.append(array)
        number[plane] = [array is other for other in arrays].index(True)
    table = jnp.array([number.get(plane, 0) for plane in range(1 + max(number))], jnp.int32)
    which = table[jnp.minimum(index, max(number))]

    rows, width = arrays[0].shape
    parts = 4

    def kernel(which, *refs):
        out_ref = refs[-1]
        for at in range(len(arrays)):
            @pl.when(which[0] == at)
            def _():
                out_ref[...] = refs[at][...]

    spec = pl.BlockSpec((rows // parts, width), lambda n, which: (n, 0))
    return pl.pallas_call(
        kernel,
        grid_spec=pltpu.PrefetchScalarGridSpec(
            num_scalar_prefetch=1,
            grid=(parts,),
            in_specs=[spec] * len(arrays) + [ANYWHERE] * len(after),
            out_specs=spec,
        ),
        out_shape=jax.ShapeDtypeStruct(arrays[0].shape, arrays[0].dtype),
        cost_estimate=pl.CostEstimate(flops=0, bytes_accessed=2 * 4 * arrays[0].size, transcendentals=0),
    )(which.astype(jnp.int32).reshape(1), *arrays, *after)


def split(value):
    upper = value.astype(jnp.bfloat16)
    return upper, (value - upper.astype(jnp.float32)).astype(jnp.bfloat16)


def three_pass(left, right, dims):
    (left_up, left_low), (right_up, right_low) = left, right
    dot = functools.partial(lax.dot_general, dimension_numbers=(dims, ((), ())), preferred_element_type=jnp.float32)
    return dot(left_up, right_up) + (dot(left_up, right_low) + dot(left_low, right_up))


def off_block(blocks, where, columns, begun=None, factor=None, after=()):
    shifts = sorted(blocks)
    refs_of = {shift: len(blocks[shift]) for shift in shifts}
    anc_rows, block = blocks[shifts[0]][0].shape
    depth, width = columns.shape
    n_col = depth // block
    tile = min(256, width)
    last = factor is not None

    def kernel(where, *refs):
        refs = list(refs)
        held = {shift: [refs.pop(0) for _ in range(refs_of[shift])] for shift in shifts}
        cols_ref = refs.pop(0)
        begun_ref = refs.pop(0) if begun is not None else None
        factor_ref = refs.pop(0) if last else None
        del refs[:len(after)]
        out_ref = refs.pop(0)
        sum_ref, diag_ref = (refs.pop(0), refs.pop(0)) if last else (None, None)
        upper, lower = refs
        hold, first = where[1], where[2]

        def take(at, shift, ref):
            upper[at], lower[at] = split(ref[...])
            if last:
                @pl.when(lax.rem(where[0] - shift + n_col, n_col) == hold)
                def _():
                    place = lax.broadcasted_iota(jnp.int32, ref.shape, 1) - lax.broadcasted_iota(jnp.int32, ref.shape, 0)
                    diag_ref[...] = jnp.sum(jnp.where(place == first, ref[...], 0.0), axis=0, keepdims=True)

        @pl.when(pl.program_id(0) == 0)
        def _():
            if last:
                diag_ref[...] = jnp.zeros_like(diag_ref)
            for at, shift in enumerate(shifts):
                if shift == 0:
                    take(at, shift, held[shift][0])
                else:
                    pl.when(where[0] >= shift)(functools.partial(take, at, shift, held[shift][0]))
                    pl.when(where[0] < shift)(functools.partial(take, at, shift, held[shift][1]))

        total = jnp.zeros((anc_rows, tile), jnp.float32) if begun is None else begun_ref[...]
        for at, shift in enumerate(shifts):
            start = lax.rem(where[0] - shift + n_col, n_col) * block
            right = split(cols_ref[pl.ds(pl.multiple_of(start, block), block), :])
            total -= three_pass((upper[at], lower[at]), right, ((1,), (0,)))
        out_ref[...] = total
        if last:
            sum_ref[...] = -jnp.sum(total * factor_ref[...], axis=0, keepdims=True)

    whole = pl.BlockSpec((anc_rows, block), lambda n, where: (0, 0), pipeline_mode=pl.Buffered(1))
    tall = pl.BlockSpec((anc_rows, tile), lambda n, where: (0, n))
    args = [array for shift in shifts for array in blocks[shift]] + [columns]
    in_specs = [whole] * (len(args) - 1) + [pl.BlockSpec((depth, tile), lambda n, where: (0, n))]
    for extra in (begun, factor):
        if extra is not None:
            args.append(extra)
            in_specs.append(tall)
    args += after
    in_specs += [ANYWHERE] * len(after)
    out_specs, out_shape = [tall], [jax.ShapeDtypeStruct((anc_rows, width), jnp.float32)]
    if last:
        out_specs += [
            pl.BlockSpec((1, tile), lambda n, where: (0, n)), pl.BlockSpec((1, block), lambda n, where: (0, 0))
        ]
        out_shape += [
            jax.ShapeDtypeStruct((1, width), jnp.float32), jax.ShapeDtypeStruct((1, block), jnp.float32)
        ]
    return pl.pallas_call(
        kernel,
        grid_spec=pltpu.PrefetchScalarGridSpec(
            num_scalar_prefetch=1,
            grid=(width // tile,),
            in_specs=in_specs,
            out_specs=out_specs,
            scratch_shapes=[pltpu.VMEM((len(shifts), anc_rows, block), jnp.bfloat16)] * 2,
        ),
        out_shape=out_shape,
        compiler_params=pltpu.CompilerParams(vmem_limit_bytes=52 * 1024 * 1024),
        cost_estimate=pl.CostEstimate(
            flops=6 * anc_rows * len(shifts) * block * width, bytes_accessed=4 * depth * width, transcendentals=0
        ),
    )(where, *args)


def halves_of(block, low, high, a_refs, b_refs):
    many, rows, width = block.shape
    half = width // 2
    left = block[..., :half].reshape(many // 2, 2, rows, half)
    right = block[..., half:].reshape(2, many // 2, rows, half)
    a_refs[0][0, 0] = jnp.where(low == 0, left[:, 0], left[:, 1])
    a_refs[1][0, 0] = jnp.where(low == 0, left[:, 1], left[:, 0])
    b_refs[0][0, 0] = jnp.where(high == 0, right[0], right[1])
    b_refs[1][0, 0] = jnp.where(high == 0, right[1], right[0])


def partial_blocks(sides, mates, which, row_id, width, groups, bits, after=()):
    anc_rows = mates[0][0].shape[0]
    part = width // groups // 2
    many = 1 << (bits - 1)
    rows = part // many
    count = len(sides)

    def kernel(where, *refs):
        side_refs = [refs[2 * at:2 * at + 2] for at in range(count)]
        refs = refs[2 * count:]
        mate_refs = [refs[2 * at:2 * at + 2] for at in range(len(mates))]
        keep_a, send_a, keep_b, send_b, upper, lower, side_up, side_low = refs[2 * len(mates) + len(after):]
        this = pl.program_id(0)

        def take_side(pair):
            for core in range(2):
                side_up[core], side_low[core] = split(pair[core][...])

        def take_mate(pair):
            for core in range(2):
                upper[core], lower[core] = split(pair[core][...])

        for at in range(count):
            pl.when(this == at)(functools.partial(take_side, side_refs[at]))

        @pl.when(pl.program_id(1) == 0)
        def _():
            for at in range(count):
                for number in range(len(mates)):
                    pl.when(jnp.logical_and(this == at, where[3 + 2 * count + at] == number))(
                        functools.partial(take_mate, mate_refs[number])
                    )

        found = jnp.zeros((part, width), jnp.float32)
        for core in range(2):
            found += three_pass((side_up[core], side_low[core]), (upper[core], lower[core]), ((0,), (0,)))
        halves_of(found.reshape(many, rows, width), where[1], where[2], (keep_a, send_a), (keep_b, send_b))

    def side_spec(at):
        first = 2 * groups * sides[at // 2][4]
        return pl.BlockSpec((anc_rows, part), lambda n, h, where: (where[3 + at], first + 2 * h + where[0]))

    def mate_spec(front):
        return pl.BlockSpec((anc_rows, width), lambda n, h, where: (0, front), pipeline_mode=pl.Buffered(1))

    out = jax.ShapeDtypeStruct((count, groups, many // 2, rows, width // 2), jnp.float32)
    out_spec = pl.BlockSpec((1, 1) + out.shape[2:], lambda n, h, where: (n, h, 0, 0, 0))
    scalars = [row_id & 1, (row_id >> 1) & 1, (row_id >> (bits - 1)) & 1]
    for own, own_at, other, other_at, front in sides:
        scalars += [own_at, other_at]
    return pl.pallas_call(
        kernel,
        grid_spec=pltpu.PrefetchScalarGridSpec(
            num_scalar_prefetch=1,
            grid=(count, groups),
            in_specs=[side_spec(at) for at in range(2 * count)]
            + [mate_spec(front) for own, other, front in mates for core in range(2)]
            + [ANYWHERE] * len(after),
            out_specs=[out_spec] * 4,
            scratch_shapes=[pltpu.VMEM((2, anc_rows, width), jnp.bfloat16)] * 2
            + [pltpu.VMEM((2, anc_rows, part), jnp.bfloat16)] * 2,
        ),
        out_shape=[out] * 4,
        compiler_params=pltpu.CompilerParams(vmem_limit_bytes=48 * 1024 * 1024),
        cost_estimate=pl.CostEstimate(
            flops=2 * count * anc_rows * width * width, bytes_accessed=count * width * width, transcendentals=0
        ),
    )(
        jnp.stack(scalars + which).astype(jnp.int32),
        *[array for own, own_at, other, other_at, front in sides for array in (own, other)],
        *[array for own, other, front in mates for array in (own, other)],
        *after,
    )


def add_split(keep_a, came_a, keep_b, came_b, low, high):
    count, groups, many, rows, half = keep_a.shape

    def kernel(where, ka, ca, kb, cb, keep_a, send_a, keep_b, send_b):
        block = jnp.concatenate([ka[0, 0] + ca[0, 0], kb[0, 0] + cb[0, 0]], axis=-1)
        halves_of(block, where[0], where[1], (keep_a, send_a), (keep_b, send_b))

    spec = pl.BlockSpec((1, 1, many, rows, half), lambda n, h, where: (n, h, 0, 0, 0))
    out = jax.ShapeDtypeStruct((count, groups, many // 2, rows, half), jnp.float32)
    out_spec = pl.BlockSpec((1, 1) + out.shape[2:], lambda n, h, where: (n, h, 0, 0, 0))
    return pl.pallas_call(
        kernel,
        grid_spec=pltpu.PrefetchScalarGridSpec(
            num_scalar_prefetch=1, grid=(count, groups), in_specs=[spec] * 4, out_specs=[out_spec] * 4
        ),
        out_shape=[out] * 4,
        cost_estimate=pl.CostEstimate(flops=keep_a.size, bytes_accessed=4 * keep_a.size, transcendentals=0),
    )(jnp.stack([low, high]).astype(jnp.int32), keep_a, came_a, keep_b, came_b)


def add_chips(halves, row_id, n_row, bits):
    for step in range(1, bits):
        keep_a, send_a, keep_b, send_b = halves
        low, high = step, bits - step
        came_a = lax.ppermute(send_a, "row", [(i, i ^ (1 << low)) for i in range(n_row)])
        came_b = lax.ppermute(send_b, "row", [(i, i ^ (1 << high)) for i in range(n_row)])
        if step < bits - 1:
            halves = add_split(keep_a, came_a, keep_b, came_b, (row_id >> (low + 1)) & 1, (row_id >> (high - 1)) & 1)
    found = jnp.concatenate([keep_a + came_a, keep_b + came_b], axis=-1)
    return found.reshape(found.shape[:2] + found.shape[3:])


def subtract_blocks(base, found, straight):
    fronts, tall, width = base.shape
    n_row, _, rows, _ = found.shape

    def kernel(flag, base_ref, found_ref, out_ref):
        cores = found_ref[...].reshape(n_row // 2, 2, rows, tall)
        block = jnp.concatenate([cores[:, core].reshape(tall // 2, tall) for core in range(2)], axis=0)

        @pl.when(flag[pl.program_id(0)] == 1)
        def _():
            out_ref[0] = base_ref[0] - block

        @pl.when(flag[pl.program_id(0)] == 0)
        def _():
            out_ref[0] = base_ref[0] - block.T

    spec = pl.BlockSpec((1, tall, tall), lambda k, h, flag: (k, 0, h))
    return pl.pallas_call(
        kernel,
        grid_spec=pltpu.PrefetchScalarGridSpec(
            num_scalar_prefetch=1,
            grid=(fronts, width // tall),
            in_specs=[spec, pl.BlockSpec((n_row, 1, rows, tall), lambda k, h, flag: (0, k, 0, h))],
            out_specs=spec,
        ),
        out_shape=jax.ShapeDtypeStruct(base.shape, base.dtype),
        compiler_params=pltpu.CompilerParams(vmem_limit_bytes=32 * 1024 * 1024),
    )(straight, base, found)


def per_device(anc_inverse, off_factor, diag_inverse, block_mask, edge_child, edge_other):
    fronts, anc_rows, col_width = off_factor.shape
    diag_rows = diag_inverse.shape[1]
    anc_cols = anc_inverse.shape[1]
    row_id = lax.axis_index("row")
    col_id = lax.axis_index("col")
    n_row, n_col = lax.axis_size("row"), lax.axis_size("col")
    groups = col_width // diag_rows
    supercols, ancestor = col_width * n_col, anc_cols * n_col

    keep = jnp.repeat(block_mask, anc_rows // block_mask.shape[1], axis=1).astype(jnp.float32)
    factor = [off_factor[k] * keep[k][:, None] for k in range(fronts)]
    side_by_side = jnp.concatenate(factor, axis=1)
    columns = lax.all_gather(side_by_side, "row", axis=0, tiled=True)

    work = assign_pairs(n_col, fronts)
    plans = {up: line_schedule(n_col, work, fronts, up) for up in (True, False)}
    got = {up: {} for up in plans}
    spots = {up: plans[up][1] for up in plans}
    ready = {
        (plane, partner, front): spots[partner < plane][(front, partner)][plane] for plane, partner, front in work
    }

    def hop(number, after=()):
        operands = {}
        for up, (steps, where_at) in plans.items():
            if number > len(steps):
                continue
            options = {}
            for plane, (kind, src) in steps[number - 1].items():
                if src == plane:
                    options[plane] = anc_inverse if kind == "z" else factor[kind]
                else:
                    options[plane] = got[up][where_at[(kind, src)][plane]]
            operands[up] = choose(col_id, options)
        earlier = tuple(got[up][number - 1] for up in got if number - 1 in got[up]) or tuple(factor)
        operands = dict(zip(operands, tie(operands.values(), earlier + after)))
        for up, operand in operands.items():
            step = 1 if up else -1
            sends = sorted(plans[up][0][number - 1])
            got[up][number] = lax.ppermute(operand, "col", [(p, p + step) for p in sends])

    owner = row_id * anc_rows // anc_cols
    place = row_id * anc_rows - owner * anc_cols
    where = jnp.stack([col_id, owner, place])
    for number in range(1, n_col + 1):
        hop(number)
    blocks = {0: [anc_inverse]}
    for shift in range(1, n_col):
        blocks[shift] = [got[True][shift], got[False][n_col - shift]]
    off, sums, z_diag = off_block(blocks, where, columns, None, side_by_side)
    bits = n_row.bit_length() - 1
    to_core = [(i, i ^ 1) for i in range(n_row)]
    off_other = lax.ppermute(off, "row", to_core)
    last = max(len(steps) for steps, where_at in plans.values())
    for step in range(n_col + 1, last + 1):
        hop(step)
    slots = color_slots(work, ready)
    slot_jobs = [("slot", number) for number in range(len(slots))]
    early = slot_jobs[:1] if all(front == 0 for plane, partner, front in slots[0]) else []
    later = slot_jobs[len(early):]
    jobs = [[("diag", 0)] + early, [("diag", k) for k in range(1, fronts)] + later[:1]]
    jobs += [later[start:start + 2] for start in range(1, len(later), 2)]

    row_global = row_id * diag_rows + jnp.arange(diag_rows, dtype=jnp.int32)
    col_global = col_id * col_width + jnp.arange(col_width, dtype=jnp.int32)
    hit = row_global[:, None] == col_global[None, :]
    def diagonals(sums):
        base_diag = jnp.sum(jnp.where(hit, diag_inverse, 0.0), axis=1)
        cc_part = base_diag + sums.reshape(fronts, col_width)
        cc_near = cc_part
        bit = 1
        while bit < n_row:
            cc_near = cc_near + lax.ppermute(cc_near, "row", [(i, i ^ bit) for i in range(n_row)])
            bit *= 2
        cc_rows = lax.dynamic_slice_in_dim(cc_near, row_id % groups * diag_rows, diag_rows, 1)
        cc_far = cc_rows
        for shift in range(1, n_col):
            pairs = []
            for row in range(n_row):
                owner = row // groups
                pairs.append((row * n_col + owner, row * n_col + (owner + shift) % n_col))
            came = lax.ppermute(cc_rows, ("row", "col"), pairs)
            cc_far = jnp.where((col_id - row_id // groups) % n_col == shift, came, cc_far)
        return cc_near, cc_far

    diag_piece, direct, turned = {}, {}, {}
    cc_near, cc_far = diagonals(sums)
    picked = {}

    def side_of(at, after):
        if at not in picked:
            side = pick(col_id, {
                plane: got[partner < plane][spots[partner < plane][(front, partner)][plane]]
                for plane, partner, front in slots[at]
            }, after)
            picked[at] = (side, jnp.int32(0), lax.ppermute(side, "row", to_core), jnp.int32(0), 0)
        return picked[at]

    for number, job in enumerate(jobs):
        sides, which, used = [], [], []
        for kind, at in job:
            used += [at] if kind == "diag" else [front for plane, partner, front in slots[at]]
        used = sorted(set(used))
        for kind, at in job:
            if kind == "diag":
                sides.append((columns, row_id, columns, row_id ^ 1, at))
                which.append(jnp.int32(used.index(at)))
                continue
            sides.append(side_of(at, (halves[0],) if number > 1 else ()))
            front_of = {plane: used.index(front) for plane, partner, front in slots[at]}
            which.append(jnp.array([front_of.get(plane, 0) for plane in range(n_col)], jnp.int32)[col_id])
        after = (off,) + tuple(got[up][n_col] for up in got) if number == 0 else (cc_near, cc_far) if number == len(jobs) - 1 else ()
        halves = partial_blocks(sides, [(off, off_other, k) for k in used], which, row_id, col_width, groups, bits, after)
        for (kind, at), piece in zip(job, add_chips(halves, row_id, n_row, bits)):
            if kind == "diag":
                diag_piece[at] = piece
                continue
            sent = lax.ppermute(piece, "col", [(plane, partner) for plane, partner, front in slots[at]])
            sent = jnp.stack([
                jnp.concatenate([sent[h][:, g * diag_rows:(g + 1) * diag_rows] for h in range(groups)], axis=1)
                for g in range(groups)
            ])
            for plane, partner, front in slots[at]:
                direct[(plane, partner, front)] = piece
                turned[(partner, plane, front)] = sent
    z_far = lax.dynamic_slice_in_dim(z_diag[0], place, anc_rows, 0)

    is_child = edge_other < supercols
    at_col = edge_child[:, :, None] == col_global
    at_row = edge_other[:, :, None] == row_global
    at_anc = edge_other[:, :, None] == supercols + row_id * anc_rows + jnp.arange(anc_rows, dtype=jnp.int32)

    def picked(at, values):
        return jnp.sum(jnp.where(at, values, 0.0), axis=-1)

    def mixed_of(at, block):
        rows = jnp.einsum("ker,krc->kec", at.astype(jnp.float32), block, precision=lax.Precision.HIGHEST)
        return picked(at_col, rows)

    off_inverse = jnp.stack([off[:, k * col_width:(k + 1) * col_width] for k in range(fronts)])
    ends = picked(at_col, cc_near[:, None, :]) + picked(at_row, cc_far[:, None, :]) + picked(at_anc, z_far)
    ends = ends - 2.0 * mixed_of(at_anc, off_inverse)

    block_id = row_id // groups
    chunks = []
    straight = []
    for k in range(fronts):
        blocks = []
        for block in range(n_col):
            options = {}
            for plane in range(n_col):
                if plane == block:
                    options[plane] = diag_piece[k]
                elif (plane, block, k) in direct:
                    options[plane] = direct[(plane, block, k)]
                else:
                    options[plane] = turned[(plane, block, k)]
            blocks.append(choose(col_id, options))
        chunks.append(jnp.stack(blocks).reshape(n_row, -1, col_width))
        flag = jnp.zeros((), jnp.bool_)
        for plane in range(n_col):
            for block in range(n_col):
                if plane == block or (plane, block, k) in direct:
                    flag = jnp.logical_or(flag, jnp.logical_and(col_id == plane, block_id == block))
        straight.append(flag)
    chunks = jnp.stack(chunks, axis=1)
    found = lax.all_to_all(chunks, "row", 0, 0, tiled=True)
    diag_part = subtract_blocks(diag_inverse, found, jnp.stack(straight).astype(jnp.int32))
    resist = ends - 2.0 * mixed_of(at_row, diag_part)
    return (off_inverse, diag_part, resist)


def solution(mesh):
    placed = (
        P("row", "col"),
        P(None, "row", "col"),
        P(None, "row", "col"),
        P(None, "row"),
        P(None, ("row", "col")),
        P(None, ("row", "col")),
    )
    return jax.shard_map(
        per_device,
        mesh=mesh,
        in_specs=placed,
        out_specs=(P(None, "row", "col"), P(None, "row", "col"), P(None, ("row", "col"))),
        check_vma=False,
    )
```

time: 541 us -> 567 us (1.048)
  Pallas kernels: 90.3 us -> 119 us
  waiting for transfers between devices: 313 us -> 288 us
  local copies, waits for them, and re-layouts: 14.1 us -> 30.9 us
  starting transfers between devices: 58.5 us -> 72 us
  other arithmetic: 38.3 us -> 30 us
    ppermute x24 -> x23, waiting for transfers between devices: 75.9 us -> 31.4 us  [the longest x6 23.2 us: add_chips(): lax.ppermute(send_a, 'row', [(i, i ^ 1 << low) for i in range(n_row)])]
    ppermute x10, waiting for transfers between devices: 148 us -> 189 us  [hop(): lax.ppermute(operand, 'col', [(p, p + step) for p in sends])]
    pallas_call x6 -> x15, Pallas kernels: 47.1 us -> 76.2 us  [the longest x3 40.9 us: partial_blocks(): pl.pallas_call(kernel, grid_spec=pltpu.PrefetchScalarGridSpec(num_scalar_...]
    ppermute x4, waiting for transfers between devices: 40.8 us -> 24.7 us  [per_device(): lax.ppermute(piece, 'col', [(plane, partner) for plane, partner, front in...]
    ppermute x24 -> x23, starting transfers between devices: 21.7 us -> 32.5 us  [the longest x3 14.9 us: diagonals(): came = lax.ppermute(cc_rows, ('row', 'col'), pairs)]
    unnamed x48 -> x81, local copies, waits for them, and re-layouts: 7.27 us -> 17.9 us
    add x22 -> x10, other arithmetic: 13.6 us -> 3.74 us  [the longest x6 3.72 us: add_chips(): found = jnp.concatenate([keep_a + came_a, keep_b + came_b], axis=-1)]
    all_to_all x1, waiting for transfers between devices: 49 us -> 42.5 us  [per_device(): found = lax.all_to_all(chunks, 'row', 0, 0, tiled=True)]
  transfers between devices with their start and end apart: 40 -> 39, of which waited for: 23 -> 25; matrix products, arithmetic and copies ran while one was open for 7% -> 7% of each run, Pallas kernels for 14% -> 13%
where the time goes in v3:
time: 567 us; the launch traced here: 562 us
  waiting for transfers between devices  288 us (51%)
  Pallas kernels  119 us (21%)
  starting transfers between devices  72 us (13%)
  local copies, waits for them, and re-layouts  30.9 us (5%)
  other arithmetic  30 us (5%)
  between operations  15.2 us (3%)
  matrix products  7.14 us (1%)
    ppermute x10, waiting for transfers between devices, hop(): lax.ppermute(operand, 'col', [(p, p + step) for p in sends])  189 us
    all_to_all x1, waiting for transfers between devices, per_device(): found = lax.all_to_all(chunks, 'row', 0, 0, tiled=True)  42.5 us
    pallas_call x3, Pallas kernels, partial_blocks(): pl.pallas_call(kernel, grid_spec=pltpu.PrefetchScalarGridSpec(num_scalar_...  40.9 us
    pallas_call x1, Pallas kernels, off_block(): pl.pallas_call(kernel, grid_spec=pltpu.PrefetchScalarGridSpec(num_scalar_...  37.6 us
    ppermute x10, starting transfers between devices, hop(): lax.ppermute(operand, 'col', [(p, p + step) for p in sends])  28 us
    ppermute x4, waiting for transfers between devices, per_device(): lax.ppermute(piece, 'col', [(plane, partner) for plane, partner, front in...  24.7 us
    ppermute x6, waiting for transfers between devices, add_chips(): lax.ppermute(send_a, 'row', [(i, i ^ 1 << low) for i in range(n_row)])  23.2 us
    pallas_call x4, Pallas kernels, pick(): pl.pallas_call(kernel, grid_spec=pltpu.PrefetchScalarGridSpec(num_scalar_...  20.3 us
  transfers between devices with their start and end apart: 39, of which 25 were waited for; matrix products, arithmetic and copies ran while one was open for 7% of the time, Pallas kernels for 13%

profile of v3, /device:TPU:0, one launch (start us, length us, event | category | flops | bytes accessed | tf_op | source)
XLA Modules:
  0.0 562.4 jit_solution(11027469472606477703)
XLA Ops:
  18.4 6.4 %collective-permute-start = (f32[512,1024]{1,0:T(8,128)}, f32[512,1024]{1,0:T(8,128)}, u32[]{:S(2)}, u32[]{:S(2)}) collective-permute-start(f32[512,1024]{1,0:T(8,128)} %get-tuple-element.40), channel_id=1, source_target_pairs={{0,1},{1,2},{2,3},{4,5},{5,6},{6,7},{8,9},{9,10},{10,11},{12,13},{... | collective-permute-start | bytes 6291464 | tf_op jit(solution)/shard_map/ppermute | solution.py:425
  26.1 42.6 %collective-permute-done.refs_2_.refs_1_ = f32[512,1024]{1,0:T(8,128)} collective-permute-done((f32[512,1024]{1,0:T(8,128)}, f32[512,1024]{1,0:T(8,128)}, u32[]{:S(2)}, u32[]{:S(2)}) %collective-permute-start) | collective-permute-done | bytes 2097184 | tf_op jit(solution)/shard_map/ppermute | solution.py:425
  68.7 5.4 collective-permute-done.1.refs_3_.refs_6_
  76.9 4.7 collective-permute-start.2
  82.9 42.6 %collective-permute-done.2.refs_2_.refs_3_.refs_0_ = f32[512,1024]{1,0:T(8,128)S(1)} collective-permute-done((f32[512,1024]{1,0:T(8,128)}, f32[512,1024]{1,0:T(8,128)S(1)}, u32[]{:S(2)}, u32[]{:S(2)}) %collective-permute-start.2) | collective-permute-done | bytes 2097184 | tf_op jit(solution)/shard_map/ppermute | solution.py:425
  125.5 4.1 collective-permute-done.3.refs_3_.refs_4_
  133.6 6.4 %collective-permute-start.5 = (f32[512,1024]{1,0:T(8,128)}, f32[512,1024]{1,0:T(8,128)}, u32[]{:S(2)}, u32[]{:S(2)}) collective-permute-start(f32[512,1024]{1,0:T(8,128)} %get-tuple-element.45), channel_id=1, source_target_pairs={{0,1},{1,2},{2,3},{4,5},{5,6},{6,7},{8,9},{9,10},{10,11},{12,13},{... | collective-permute-start | bytes 6291464 | tf_op jit(solution)/shard_map/ppermute | solution.py:425
  140.1 39.5 %collective-permute-done.4.refs_2_.refs_3_.refs_1_.refs_0_ = f32[512,1024]{1,0:T(8,128)} collective-permute-done((f32[512,1024]{1,0:T(8,128)}, f32[512,1024]{1,0:T(8,128)}, u32[]{:S(2)}, u32[]{:S(2)}) %collective-permute-start.4) | collective-permute-done | bytes 2097184 | tf_op jit(solution)/shard_map/ppermute | solution.py:425
  180.8 37.6 %shard_map.160 = (f32[512,2048]{1,0:T(8,128)}, f32[1,2048]{1,0:T(1,128)S(1)}, f32[1,1024]{1,0:T(1,128)S(1)}) custom-call(s32[3]{0:T(128)S(1)} %pad_add_fusion.where, f32[512,1024]{1,0:T(8,128)} %refs_0_.2, f32[512,1024]{1,0:T(8,128)} %collective-permute-done.refs_2_.refs_1_, f32[512,1024]{1,0:T(8,128)} %collective-permute-done.4.refs_2_.refs_3_.refs_1_.refs_0_, ...), custom_call_target="tpu_custom_call" | custom-call | flops 25769803776 | bytes 33554432 | tf_op jit(solution)/shard_map/pallas_call | solution.py:220
  228.9 4.8 shard_map.169.refs_2_
  234.1 41.1 %collective-permute-done.6.refs_3_.refs_0_.refs_2_.refs_8_ = f32[512,1024]{1,0:T(8,128)} collective-permute-done((f32[512,1024]{1,0:T(8,128)}, f32[512,1024]{1,0:T(8,128)}, u32[]{:S(2)}, u32[]{:S(2)}) %collective-permute-start.6) | collective-permute-done | bytes 2097184 | tf_op jit(solution)/shard_map/ppermute | solution.py:425
  275.2 4.8 shard_map.163.refs_2_
  285.3 13.4 %shard_map.170 = (f32[2,2,2,64,512]{4,3,2,1,0:T(8,128)S(1)}, f32[2,2,2,64,512]{4,3,2,1,0:T(8,128)S(1)}, f32[2,2,2,64,512]{4,3,2,1,0:T(8,128)S(1)}, f32[2,2,2,64,512]{4,3,2,1,0:T(8,128)S(1)}) custom-call(s32[9]{0:T(128)S(1)} %stack.143.where, f32[4096,2048]{1,0:T(8,128)} %all-gather.2.cloned.1.call-done.refs_7_.refs_0_.refs_1_, ...), custom_call_target="tpu_custom_call" | custom-call | flops 2147483648 | bytes 2097152 | tf_op jit(solution)/shard_map/pallas_call | solution.py:298
  307.1 13.1 %shard_map.164 = (f32[2,2,2,64,512]{4,3,2,1,0:T(8,128)S(1)}, f32[2,2,2,64,512]{4,3,2,1,0:T(8,128)S(1)}, f32[2,2,2,64,512]{4,3,2,1,0:T(8,128)S(1)}, f32[2,2,2,64,512]{4,3,2,1,0:T(8,128)S(1)}) custom-call(s32[9]{0:T(128)S(1)} %stack.143.where, f32[4096,2048]{1,0:T(8,128)} %all-gather.2.cloned.1.call-done.refs_7_.refs_0_.refs_1_, ...), custom_call_target="tpu_custom_call" | custom-call | flops 2147483648 | bytes 2097152 | tf_op jit(solution)/shard_map/pallas_call | solution.py:298
  323.3 12.5 %collective-permute-done.12.refs_1_ = f32[512,1024]{1,0:T(8,128)} collective-permute-done((f32[512,1024]{1,0:T(8,128)}, f32[512,1024]{1,0:T(8,128)}, u32[]{:S(2)}, u32[]{:S(2)}) %collective-permute-start.12) | collective-permute-done | bytes 2097184 | tf_op jit(solution)/shard_map/ppermute | solution.py:425
  335.9 5.1 shard_map.166.refs_2_
  341.0 5.7 %shard_map.165.refs_0_ = f32[512,1024]{1,0:T(8,128)} custom-call(s32[1]{0:T(128)} %dynamic_slice.34.which, f32[512,1024]{1,0:T(8,128)} %copy-done.13, f32[512,1024]{1,0:T(8,128)} %collective-permute-done.4.refs_2_.refs_3_.refs_1_.refs_0_, f32[512,1024]{1,0:T(8,128)} %collective-permute-done.6.refs_3_.refs_0_.refs_2_.refs_8_, ...), custom_call_target="tpu_custom_call" | custom-call | bytes 4194304 | tf_op jit(solution)/shard_map/pallas_call | solution.py:129
  350.9 7.7 %collective-permute-start.17 = (f32[2,512]{1,0:T(2,128)S(1)}, f32[2,512]{1,0:T(2,128)S(1)}, u32[]{:S(2)}, u32[]{:S(2)}) collective-permute-start(f32[2,512]{1,0:T(2,128)S(1)} %constant_dynamic-slice_fusion), channel_id=1, source_target_pairs={{0,3},{4,7},{9,8},{13,12},{18,17},{22,21},{27,26},{31,30}} | collective-permute-start | bytes 12296 | tf_op jit(solution)/shard_map/ppermute | solution.py:467
  364.2 5.8 %collective-permute-start.19 = (f32[2,512]{1,0:T(2,128)S(1)}, f32[2,512]{1,0:T(2,128)S(1)}, u32[]{:S(2)}, u32[]{:S(2)}) collective-permute-start(f32[2,512]{1,0:T(2,128)S(1)} %constant_dynamic-slice_fusion), channel_id=1, source_target_pairs={{0,1},{4,5},{9,10},{13,14},{18,19},{22,23},{27,24},{31,28}} | collective-permute-start | bytes 12296 | tf_op jit(solution)/shard_map/ppermute | solution.py:467
  370.6 5.0 shard_map.171
  375.7 10.1 %collective-permute-done.32.ca = f32[2,2,2,64,512]{4,3,2,1,0:T(8,128)} collective-permute-done((f32[2,2,2,64,512]{4,3,2,1,0:T(8,128)}, f32[2,2,2,64,512]{4,3,2,1,0:T(8,128)}, u32[]{:S(2)}, u32[]{:S(2)}) %collective-permute-start.32) | collective-permute-done | bytes 1048608 | tf_op jit(solution)/shard_map/ppermute | solution.py:347
  389.6 5.0 shard_map.172
  408.6 14.4 %shard_map.167 = (f32[2,2,2,64,512]{4,3,2,1,0:T(8,128)S(1)}, f32[2,2,2,64,512]{4,3,2,1,0:T(8,128)S(1)}, f32[2,2,2,64,512]{4,3,2,1,0:T(8,128)S(1)}, f32[2,2,2,64,512]{4,3,2,1,0:T(8,128)S(1)}) custom-call(s32[9]{0:T(128)S(1)} %stack.140.where, f32[512,1024]{1,0:T(8,128)} %shard_map.165.refs_0_, f32[512,1024]{1,0:T(8,128)} %collective-permute-done.11.refs_1_, ...), custom_call_target="tpu_custom_call" | custom-call | flops 2147483648 | bytes 2097152 | tf_op jit(solution)/shard_map/pallas_call | solution.py:298
  434.3 8.5 %collective-permute-done.36 = f32[2,64,1024]{2,1,0:T(8,128)} collective-permute-done((f32[2,64,1024]{2,1,0:T(8,128)}, f32[2,64,1024]{2,1,0:T(8,128)}, u32[]{:S(2)}, u32[]{:S(2)}) %collective-permute-start.36) | collective-permute-done | bytes 524320 | tf_op jit(solution)/shard_map/ppermute | solution.py:503
  447.8 5.0 shard_map.168
  455.8 6.5 %collective-permute-done.22 = f32[2,2,1,64,512]{4,3,1,2,0:T(8,128)S(1)} collective-permute-done((f32[2,2,1,64,512]{4,3,1,2,0:T(8,128)}, f32[2,2,1,64,512]{4,3,1,2,0:T(8,128)S(1)}, u32[]{:S(2)}, u32[]{:S(2)}) %collective-permute-start.22) | collective-permute-done | bytes 524320 | tf_op jit(solution)/shard_map/ppermute | solution.py:347
  468.0 10.7 %collective-permute-done.30 = f32[2,64,1024]{2,1,0:T(8,128)S(1)} collective-permute-done((f32[2,64,1024]{2,1,0:T(8,128)S(1)}, f32[2,64,1024]{2,1,0:T(8,128)S(1)}, u32[]{:S(2)}, u32[]{:S(2)}) %collective-permute-start.30) | collective-permute-done | bytes 524320 | tf_op jit(solution)/shard_map/ppermute | solution.py:503
  478.8 5.5 collective-permute-done.31
  488.4 4.8 all-to-all-start
  499.8 42.5 %all-to-all-done.found_ref = f32[8,2,64,1024]{3,2,1,0:T(8,128)} async-done(((f32[8,2,64,1024]{3,2,1,0:T(8,128)}), f32[8,2,64,1024]{3,2,1,0:T(8,128)}, u32[]{:S(2)}, u32[]{:S(2)}) %all-to-all-start) | async-done | bytes 4194336 | tf_op jit(solution)/shard_map/all_to_all | solution.py:552
  544.5 5.5 shard_map.173
  550.1 4.6 fusion.2
  (224 shorter events, 115.7 us)
Async XLA Ops:
  7.2 173.6 %all-gather.2.cloned.1.call-start = ((), (), s32[]{:S(2)}) async-start(), calls=%async_computation.1 | async-start | bytes 37748736 | tf_op jit(solution)/shard_map/all_gather | solution.py:398
  18.4 50.2 %collective-permute-start = (f32[512,1024]{1,0:T(8,128)}, f32[512,1024]{1,0:T(8,128)}, u32[]{:S(2)}, u32[]{:S(2)}) collective-permute-start(f32[512,1024]{1,0:T(8,128)} %get-tuple-element.40), channel_id=1, source_target_pairs={{0,1},{1,2},{2,3},{4,5},{5,6},{6,7},{8,9},{9,10},{10,11},{12,13},{... | collective-permute-start | bytes 6291464 | tf_op jit(solution)/shard_map/ppermute | solution.py:425
  24.8 49.3 %collective-permute-start.1 = (f32[512,1024]{1,0:T(8,128)}, f32[512,1024]{1,0:T(8,128)}, u32[]{:S(2)}, u32[]{:S(2)}) collective-permute-start(f32[512,1024]{1,0:T(8,128)} %get-tuple-element.41), channel_id=1, source_target_pairs={{1,0},{2,1},{3,2},{5,4},{6,5},{7,6},{9,8},{10,9},{11,10},{13,12},{... | collective-permute-start | bytes 6291464 | tf_op jit(solution)/shard_map/ppermute | solution.py:425
  76.9 48.5 %collective-permute-start.2 = (f32[512,1024]{1,0:T(8,128)}, f32[512,1024]{1,0:T(8,128)S(1)}, u32[]{:S(2)}, u32[]{:S(2)}) collective-permute-start(f32[512,1024]{1,0:T(8,128)} %get-tuple-element.42), channel_id=1, source_target_pairs={{0,1},{1,2},{2,3},{4,5},{5,6},{6,7},{8,9},{9,10},{10,11},{12,13},{... | collective-permute-start | bytes 6291464 | tf_op jit(solution)/shard_map/ppermute | solution.py:425
  81.6 48.0 %collective-permute-start.3 = (f32[512,1024]{1,0:T(8,128)}, f32[512,1024]{1,0:T(8,128)S(1)}, u32[]{:S(2)}, u32[]{:S(2)}) collective-permute-start(f32[512,1024]{1,0:T(8,128)} %get-tuple-element.43), channel_id=1, source_target_pairs={{1,0},{2,1},{3,2},{5,4},{6,5},{7,6},{9,8},{10,9},{11,10},{13,12},{... | collective-permute-start | bytes 6291464 | tf_op jit(solution)/shard_map/ppermute | solution.py:425
  132.3 47.3 %collective-permute-start.4 = (f32[512,1024]{1,0:T(8,128)}, f32[512,1024]{1,0:T(8,128)}, u32[]{:S(2)}, u32[]{:S(2)}) collective-permute-start(f32[512,1024]{1,0:T(8,128)} %get-tuple-element.44), channel_id=1, source_target_pairs={{1,0},{2,1},{3,2},{5,4},{6,5},{7,6},{9,8},{10,9},{11,10},{13,12},{... | collective-permute-start | bytes 6291464 | tf_op jit(solution)/shard_map/ppermute | solution.py:425
  133.6 47.2 %collective-permute-start.5 = (f32[512,1024]{1,0:T(8,128)}, f32[512,1024]{1,0:T(8,128)}, u32[]{:S(2)}, u32[]{:S(2)}) collective-permute-start(f32[512,1024]{1,0:T(8,128)} %get-tuple-element.45), channel_id=1, source_target_pairs={{0,1},{1,2},{2,3},{4,5},{5,6},{6,7},{8,9},{9,10},{10,11},{12,13},{... | collective-permute-start | bytes 6291464 | tf_op jit(solution)/shard_map/ppermute | solution.py:425
  218.4 66.8 %collective-permute-start.10 = (f32[512,2048]{1,0:T(8,128)}, f32[512,2048]{1,0:T(8,128)}, u32[]{:S(2)}, u32[]{:S(2)}) collective-permute-start(f32[512,2048]{1,0:T(8,128)} %get-tuple-element.46.refs_4_.refs_6_), channel_id=1, source_target_pairs={{0,4},{4,0},{8,12},{12,8},{16,20},{20,16},{24,28},{28,24},{1,5},{5... | collective-permute-start | bytes 12582920 | tf_op jit(solution)/shard_map/ppermute | solution.py:438
  224.9 50.4 %collective-permute-start.6 = (f32[512,1024]{1,0:T(8,128)}, f32[512,1024]{1,0:T(8,128)}, u32[]{:S(2)}, u32[]{:S(2)}) collective-permute-start(f32[512,1024]{1,0:T(8,128)} %get-tuple-element.47), channel_id=1, source_target_pairs={{1,0},{2,1},{5,4},{6,5},{9,8},{10,9},{13,12},{14,13},{17,16},{18,1... | collective-permute-start | bytes 6291464 | tf_op jit(solution)/shard_map/ppermute | solution.py:425
  226.3 49.0 %collective-permute-start.7 = (f32[512,1024]{1,0:T(8,128)}, f32[512,1024]{1,0:T(8,128)}, u32[]{:S(2)}, u32[]{:S(2)}) collective-permute-start(f32[512,1024]{1,0:T(8,128)} %get-tuple-element.48), channel_id=1, source_target_pairs={{1,2},{2,3},{5,6},{6,7},{9,10},{10,11},{13,14},{14,15},{17,18},{18... | collective-permute-start | bytes 6291464 | tf_op jit(solution)/shard_map/ppermute | solution.py:425
  233.6 51.6 %collective-permute-start.24 = (f32[512,1024]{1,0:T(8,128)}, f32[512,1024]{1,0:T(8,128)}, u32[]{:S(2)}, u32[]{:S(2)}) collective-permute-start(f32[512,1024]{1,0:T(8,128)} %shard_map.169.refs_2_), channel_id=1, source_target_pairs={{0,4},{4,0},{8,12},{12,8},{16,20},{20,16},{24,28},{28,24},{1,5},{5... | collective-permute-start | bytes 6291464 | tf_op jit(solution)/shard_map/ppermute | solution.py:481
  280.0 26.5 %collective-permute-start.9 = (f32[512,1024]{1,0:T(8,128)}, f32[512,1024]{1,0:T(8,128)}, u32[]{:S(2)}, u32[]{:S(2)}) collective-permute-start(f32[512,1024]{1,0:T(8,128)} %shard_map.163.refs_2_), channel_id=1, source_target_pairs={{0,4},{4,0},{8,12},{12,8},{16,20},{20,16},{24,28},{28,24},{1,5},{5... | collective-permute-start | bytes 6291464 | tf_op jit(solution)/shard_map/ppermute | solution.py:481
  281.7 54.2 %collective-permute-start.12 = (f32[512,1024]{1,0:T(8,128)}, f32[512,1024]{1,0:T(8,128)}, u32[]{:S(2)}, u32[]{:S(2)}) collective-permute-start(f32[512,1024]{1,0:T(8,128)} %get-tuple-element.51), channel_id=1, source_target_pairs={{1,0},{2,1},{5,4},{6,5},{9,8},{10,9},{13,12},{14,13},{17,16},{18,1... | collective-permute-start | bytes 6291464 | tf_op jit(solution)/shard_map/ppermute | solution.py:425
  283.0 52.9 %collective-permute-start.8 = (f32[512,1024]{1,0:T(8,128)}, f32[512,1024]{1,0:T(8,128)}, u32[]{:S(2)}, u32[]{:S(2)}) collective-permute-start(f32[512,1024]{1,0:T(8,128)} %get-tuple-element.49), channel_id=1, source_target_pairs={{1,2},{2,3},{5,6},{6,7},{9,10},{10,11},{13,14},{14,15},{17,18},{18... | collective-permute-start | bytes 6291464 | tf_op jit(solution)/shard_map/ppermute | solution.py:425
  298.7 63.9 %collective-permute-start.25 = (f32[2,2,2,64,512]{4,3,2,1,0:T(8,128)S(1)}, f32[2,2,2,64,512]{4,3,2,1,0:T(8,128)}, u32[]{:S(2)}, u32[]{:S(2)}) collective-permute-start(f32[2,2,2,64,512]{4,3,2,1,0:T(8,128)S(1)} %get-tuple-element.62), channel_id=1, source_target_pairs={{0,8},{4,12},{8,0},{12,4},{16,24},{20,28},{24,16},{28,20},{1,9},{5... | collective-permute-start | bytes 3145736 | tf_op jit(solution)/shard_map/ppermute | solution.py:347
  303.7 60.4 %collective-permute-start.26 = (f32[2,2,2,64,512]{4,3,2,1,0:T(8,128)S(1)}, f32[2,2,2,64,512]{4,3,2,1,0:T(8,128)}, u32[]{:S(2)}, u32[]{:S(2)}) collective-permute-start(f32[2,2,2,64,512]{4,3,2,1,0:T(8,128)S(1)} %get-tuple-element.64), channel_id=1, source_target_pairs={{0,16},{4,20},{8,24},{12,28},{16,0},{20,4},{24,8},{28,12},{1,17},{... | collective-permute-start | bytes 3145736 | tf_op jit(solution)/shard_map/ppermute | solution.py:348
  306.5 40.6 %collective-permute-start.15 = (f32[2,1024]{1,0:T(2,128)S(1)}, f32[2,1024]{1,0:T(2,128)S(1)}, u32[]{:S(2)}, u32[]{:S(2)}) collective-permute-start(f32[2,1024]{1,0:T(2,128)S(1)} %add.113), channel_id=1, source_target_pairs={{0,8},{4,12},{8,0},{12,4},{16,24},{20,28},{24,16},{28,20},{1,9},{5... | collective-permute-start | bytes 24584 | tf_op jit(solution)/shard_map/ppermute | solution.py:458
  341.0 67.6 %collective-permute-start.13 = (f32[512,1024]{1,0:T(8,128)}, f32[512,1024]{1,0:T(8,128)}, u32[]{:S(2)}, u32[]{:S(2)}) collective-permute-start(f32[512,1024]{1,0:T(8,128)} %shard_map.166.refs_2_), channel_id=1, source_target_pairs={{0,4},{4,0},{8,12},{12,8},{16,20},{20,16},{24,28},{28,24},{1,5},{5... | collective-permute-start | bytes 6291464 | tf_op jit(solution)/shard_map/ppermute | solution.py:481
  346.6 62.0 %collective-permute-start.11 = (f32[512,1024]{1,0:T(8,128)}, f32[512,1024]{1,0:T(8,128)}, u32[]{:S(2)}, u32[]{:S(2)}) collective-permute-start(f32[512,1024]{1,0:T(8,128)} %shard_map.165.refs_0_), channel_id=1, source_target_pairs={{0,4},{4,0},{8,12},{12,8},{16,20},{20,16},{24,28},{28,24},{1,5},{5... | collective-permute-start | bytes 6291464 | tf_op jit(solution)/shard_map/ppermute | solution.py:481
  362.5 23.3 %collective-permute-start.32 = (f32[2,2,2,64,512]{4,3,2,1,0:T(8,128)}, f32[2,2,2,64,512]{4,3,2,1,0:T(8,128)}, u32[]{:S(2)}, u32[]{:S(2)}) collective-permute-start(f32[2,2,2,64,512]{4,3,2,1,0:T(8,128)} %copy-done.8), channel_id=1, source_target_pairs={{0,8},{4,12},{8,0},{12,4},{16,24},{20,28},{24,16},{28,20},{1,9},{5... | collective-permute-start | bytes 3145736 | tf_op jit(solution)/shard_map/ppermute | solution.py:347
  362.5 26.1 %collective-permute-start.33 = (f32[2,2,2,64,512]{4,3,2,1,0:T(8,128)S(1)}, f32[2,2,2,64,512]{4,3,2,1,0:T(8,128)S(1)}, u32[]{:S(2)}, u32[]{:S(2)}) collective-permute-start(f32[2,2,2,64,512]{4,3,2,1,0:T(8,128)S(1)} %get-tuple-element.71), channel_id=1, source_target_pairs={{0,16},{4,20},{8,24},{12,28},{16,0},{20,4},{24,8},{28,12},{1,17},{... | collective-permute-start | bytes 3145736 | tf_op jit(solution)/shard_map/ppermute | solution.py:348
  364.2 11.4 %collective-permute-start.19 = (f32[2,512]{1,0:T(2,128)S(1)}, f32[2,512]{1,0:T(2,128)S(1)}, u32[]{:S(2)}, u32[]{:S(2)}) collective-permute-start(f32[2,512]{1,0:T(2,128)S(1)} %constant_dynamic-slice_fusion), channel_id=1, source_target_pairs={{0,1},{4,5},{9,10},{13,14},{18,19},{22,23},{27,24},{31,28}} | collective-permute-start | bytes 12296 | tf_op jit(solution)/shard_map/ppermute | solution.py:467
  375.6 23.5 %collective-permute-start.27 = (f32[2,2,1,64,512]{4,3,1,2,0:T(8,128)}, f32[2,2,1,64,512]{4,3,1,2,0:T(8,128)}, u32[]{:S(2)}, u32[]{:S(2)}) collective-permute-start(f32[2,2,1,64,512]{4,3,1,2,0:T(8,128)} %bitcast.135), channel_id=1, source_target_pairs={{0,16},{4,20},{8,24},{12,28},{16,0},{20,4},{24,8},{28,12},{1,17},{... | collective-permute-start | bytes 1572872 | tf_op jit(solution)/shard_map/ppermute | solution.py:347
  385.9 16.4 %collective-permute-start.28 = (f32[2,2,1,64,512]{4,3,1,2,0:T(8,128)}, f32[2,2,1,64,512]{4,3,1,2,0:T(8,128)}, u32[]{:S(2)}, u32[]{:S(2)}) collective-permute-start(f32[2,2,1,64,512]{4,3,1,2,0:T(8,128)} %bitcast.134), channel_id=1, source_target_pairs={{0,8},{4,12},{8,0},{12,4},{16,24},{20,28},{24,16},{28,20},{1,9},{5... | collective-permute-start | bytes 1572872 | tf_op jit(solution)/shard_map/ppermute | solution.py:348
  394.6 12.9 %collective-permute-start.34 = (f32[2,2,1,64,512]{4,3,2,1,0:T(8,128)}, f32[2,2,1,64,512]{4,3,2,1,0:T(8,128)S(1)}, u32[]{:S(2)}, u32[]{:S(2)}) collective-permute-start(f32[2,2,1,64,512]{4,3,2,1,0:T(8,128)} %get-tuple-element.73), channel_id=1, source_target_pairs={{0,16},{4,20},{8,24},{12,28},{16,0},{20,4},{24,8},{28,12},{1,17},{... | collective-permute-start | bytes 1572872 | tf_op jit(solution)/shard_map/ppermute | solution.py:347
  404.4 27.5 %collective-permute-start.29 = (f32[2,64,1024]{2,1,0:T(8,128)}, f32[2,64,1024]{2,1,0:T(8,128)}, u32[]{:S(2)}, u32[]{:S(2)}) collective-permute-start(f32[2,64,1024]{2,1,0:T(8,128)} %fusion.29), channel_id=1, source_target_pairs={{1,3},{2,0},{5,7},{6,4},{9,11},{10,8},{13,15},{14,12},{17,19},{18,... | collective-permute-start | bytes 1572872 | tf_op jit(solution)/shard_map/ppermute | solution.py:503
  424.9 21.7 %collective-permute-start.20 = (f32[2,2,2,64,512]{4,3,2,1,0:T(8,128)S(1)}, f32[2,2,2,64,512]{4,3,2,1,0:T(8,128)}, u32[]{:S(2)}, u32[]{:S(2)}) collective-permute-start(f32[2,2,2,64,512]{4,3,2,1,0:T(8,128)S(1)} %get-tuple-element.54), channel_id=1, source_target_pairs={{0,8},{4,12},{8,0},{12,4},{16,24},{20,28},{24,16},{28,20},{1,9},{5... | collective-permute-start | bytes 3145736 | tf_op jit(solution)/shard_map/ppermute | solution.py:347
  427.0 20.9 %collective-permute-start.21 = (f32[2,2,2,64,512]{4,3,2,1,0:T(8,128)S(1)}, f32[2,2,2,64,512]{4,3,2,1,0:T(8,128)}, u32[]{:S(2)}, u32[]{:S(2)}) collective-permute-start(f32[2,2,2,64,512]{4,3,2,1,0:T(8,128)S(1)} %get-tuple-element.56), channel_id=1, source_target_pairs={{0,16},{4,20},{8,24},{12,28},{16,0},{20,4},{24,8},{28,12},{1,17},{... | collective-permute-start | bytes 3145736 | tf_op jit(solution)/shard_map/ppermute | solution.py:348
  430.5 12.3 %collective-permute-start.36 = (f32[2,64,1024]{2,1,0:T(8,128)}, f32[2,64,1024]{2,1,0:T(8,128)}, u32[]{:S(2)}, u32[]{:S(2)}) collective-permute-start(f32[2,64,1024]{2,1,0:T(8,128)} %slice_bitcast_fusion.2), channel_id=1, source_target_pairs={{1,3},{2,0},{5,7},{6,4},{9,11},{10,8},{13,15},{14,12},{17,19},{18,... | collective-permute-start | bytes 1572872 | tf_op jit(solution)/shard_map/ppermute | solution.py:503
  463.9 14.8 %collective-permute-start.30 = (f32[2,64,1024]{2,1,0:T(8,128)S(1)}, f32[2,64,1024]{2,1,0:T(8,128)S(1)}, u32[]{:S(2)}, u32[]{:S(2)}) collective-permute-start(f32[2,64,1024]{2,1,0:T(8,128)S(1)} %bitcast.132), channel_id=1, source_target_pairs={{1,0},{2,3},{0,1},{3,2},{5,4},{6,7},{4,5},{7,6},{9,8},{10,11},{8,9... | collective-permute-start | bytes 1572872 | tf_op jit(solution)/shard_map/ppermute | solution.py:503
  466.3 18.0 %collective-permute-start.31 = (f32[2,64,1024]{2,1,0:T(8,128)S(1)}, f32[2,64,1024]{2,1,0:T(8,128)S(1)}, u32[]{:S(2)}, u32[]{:S(2)}) collective-permute-start(f32[2,64,1024]{2,1,0:T(8,128)S(1)} %bitcast.131), channel_id=1, source_target_pairs={{3,0},{1,2},{2,1},{0,3},{7,4},{5,6},{6,5},{4,7},{11,8},{9,10},{10,... | collective-permute-start | bytes 1572872 | tf_op jit(solution)/shard_map/ppermute | solution.py:503
  488.4 54.0 %all-to-all-start = ((f32[8,2,64,1024]{3,2,1,0:T(8,128)}), f32[8,2,64,1024]{3,2,1,0:T(8,128)}, u32[]{:S(2)}, u32[]{:S(2)}) async-start(f32[8,2,64,1024]{3,2,1,0:T(8,128)} %pad_maximum_fusion.2), calls=%async_computation | async-start | bytes 8388608 | tf_op jit(solution)/shard_map/all_to_all | solution.py:552
  (46 other events, 369.9 us)
Sparse Core Ops, SparseCore 0:
  14.4 163.4 all-gather.1

commit v4 on v2

--- a/solution.py
+++ b/solution.py
@@ -192,14 +192,15 @@
     )(where, own, *lower_blocks, *upper_blocks, columns, factor)
 
 
-def partial_block(sides, which, off, front, mine, groups, bits):
+def partial_block(sides, which, off, front, mine, groups, bits, after=()):
     anc_rows, width = sides[0].shape
     tall = width // groups
     rows = tall >> bits
 
     def kernel(where, *refs):
         side_refs = refs[:len(sides)]
-        off_ref, kept_ref, sent_ref, upper, lower, side_up, side_low = refs[len(sides):]
+        off_ref = refs[len(sides)]
+        kept_ref, sent_ref, upper, lower, side_up, side_low = refs[len(sides) + 1 + len(after):]
 
         @pl.when(pl.program_id(0) == 0)
         def _():
@@ -225,7 +226,7 @@
             grid=(groups,),
             in_specs=[pl.BlockSpec((anc_rows, tall), lambda h, where: (0, h)) for _ in sides] + [
                 pl.BlockSpec((anc_rows, width), lambda h, where: (0, where[0])),
-            ],
+            ] + [pl.BlockSpec(memory_space=pl.ANY) for _ in after],
             out_specs=[out_spec, out_spec],
             scratch_shapes=[pltpu.VMEM((anc_rows, width), jnp.bfloat16)] * 2
             + [pltpu.VMEM((anc_rows, tall), jnp.bfloat16)] * 2,
@@ -233,7 +234,7 @@
         out_shape=[out, out],
         compiler_params=pltpu.CompilerParams(vmem_limit_bytes=48 * 1024 * 1024),
         cost_estimate=SMALL,
-    )(jnp.stack([front, mine, which]).astype(jnp.int32), *sides, off)
+    )(jnp.stack([front, mine, which]).astype(jnp.int32), *sides, off, *after)
 
 
 def subtract_blocks(base, found, straight):
@@ -384,7 +385,8 @@
             if slot is slots[1]:
                 sides = list(tie(tuple(sides), first))
             table = [jnp.array([of.get(plane, 0) for plane in range(n_col)], jnp.int32)[col_id] for of in (which, fronts_of)]
-            halves.append(partial_block(sides, table[0], off, table[1], low_bit, groups, bits))
+            newest = tuple(got[up][max(got[up])] for up in got)
+            halves.append(partial_block(sides, table[0], off, table[1], low_bit, groups, bits, newest))
         pieces = reduce_scatter(halves, n_row, bits, came)[1]
         moved = []
         for slot, piece in zip(slots[start:start + 2], pieces):

time: 541 us -> 570 us (1.054)
  waiting for transfers between devices: 313 us -> 329 us
  other arithmetic: 38.3 us -> 53.7 us
    ppermute x12, waiting for transfers between devices: 55 us -> 82.5 us  [swap(): lax.ppermute(send, 'row', [(i, i ^ 1 << bit) for i in range(n_row)])]
    ppermute x3, waiting for transfers between devices: 19.7 us -> 3.74 us  [per_device(): lax.ppermute(cc_near, 'row', [(i, i ^ bit) for i in range(n_row)])]
    select_n x8, other arithmetic: 5.92 us -> 14.1 us  [choose(): result = jnp.where(hit, array, result)]
    ppermute x10, waiting for transfers between devices: 148 us -> 155 us  [hop(): lax.ppermute(operand, 'col', [(p, p + step) for p in sends])]
  transfers between devices with their start and end apart: 40 -> 40, of which waited for: 23 -> 27; matrix products, arithmetic and copies ran while one was open for 7% -> 8% of each run, Pallas kernels for 14% -> 12%
where the time goes in v4:
time: 570 us; the launch traced here: 566 us
  waiting for transfers between devices  329 us (58%)
  Pallas kernels  91.7 us (16%)
  other arithmetic  53.7 us (9%)
  starting transfers between devices  53.6 us (9%)
  local copies, waits for them, and re-layouts  15.2 us (3%)
  between operations  15.1 us (3%)
  matrix products  7.15 us (1%)
    ppermute x10, waiting for transfers between devices, hop(): lax.ppermute(operand, 'col', [(p, p + step) for p in sends])  155 us
    ppermute x12, waiting for transfers between devices, swap(): lax.ppermute(send, 'row', [(i, i ^ 1 << bit) for i in range(n_row)])  82.5 us
    all_to_all x1, waiting for transfers between devices, per_device(): found = lax.all_to_all(chunks, 'row', 0, 0, tiled=True)  49 us
    pallas_call x6, Pallas kernels, partial_block(): pl.pallas_call(kernel, grid_spec=pltpu.PrefetchScalarGridSpec(num_scalar_...  48.5 us
    pallas_call x1, Pallas kernels, off_block(): pl.pallas_call(kernel, grid_spec=pltpu.PrefetchScalarGridSpec(num_scalar_...  37.7 us
    ppermute x4, waiting for transfers between devices, per_device(): lax.ppermute(piece, 'col', [(plane, partner) for plane, partner, front in...  35.8 us
    ppermute x10, starting transfers between devices, hop(): lax.ppermute(operand, 'col', [(p, p + step) for p in sends])  21.8 us
    select_n x8, other arithmetic, choose(): result = jnp.where(hit, array, result)  14.1 us
  transfers between devices with their start and end apart: 40, of which 27 were waited for; matrix products, arithmetic and copies ran while one was open for 8% of the time, Pallas kernels for 12%

profile of v4, /device:TPU:0, one launch (start us, length us, event | category | flops | bytes accessed | tf_op | source)
XLA Modules:
  0.0 565.9 jit_solution(17674073103560109328)
XLA Ops:
  12.5 4.7 pad_maximum_fusion.refs_7_
  17.2 5.1 collective-permute-start
  23.6 43.7 %collective-permute-done.refs_0_ = f32[512,1024]{1,0:T(8,128)S(1)} collective-permute-done((f32[512,1024]{1,0:T(8,128)}, f32[512,1024]{1,0:T(8,128)S(1)}, u32[]{:S(2)}, u32[]{:S(2)}) %collective-permute-start) | collective-permute-done | bytes 2097184 | tf_op jit(solution)/shard_map/ppermute | solution.py:309
  78.4 42.2 %collective-permute-done.2.refs_1_.refs_0_ = f32[512,1024]{1,0:T(8,128)S(1)} collective-permute-done((f32[512,1024]{1,0:T(8,128)S(1)}, f32[512,1024]{1,0:T(8,128)S(1)}, u32[]{:S(2)}, u32[]{:S(2)}) %collective-permute-start.2) | collective-permute-done | bytes 2097184 | tf_op jit(solution)/shard_map/ppermute | solution.py:309
  133.1 40.4 %collective-permute-done.4.refs_2_.refs_1_ = f32[512,1024]{1,0:T(8,128)} collective-permute-done((f32[512,1024]{1,0:T(8,128)}, f32[512,1024]{1,0:T(8,128)}, u32[]{:S(2)}, u32[]{:S(2)}) %collective-permute-start.4) | collective-permute-done | bytes 2097184 | tf_op jit(solution)/shard_map/ppermute | solution.py:309
  173.4 5.4 collective-permute-done.5.refs_5_.refs_0_
  182.4 37.7 %shard_map.157 = (f32[512,2048]{1,0:T(8,128)}, f32[1,2048]{1,0:T(1,128)S(1)}, f32[1,1024]{1,0:T(1,128)S(1)}) custom-call(s32[3]{0:T(128)S(1)} %pad_add_fusion.2.where, f32[512,1024]{1,0:T(8,128)} %own_ref.1, f32[512,1024]{1,0:T(8,128)} %copy-done.11, f32[512,1024]{1,0:T(8,128)} %copy-done.8, f32[512,1024]{1,0:T(8,128)} %collective-permute-done.4.refs_2_.refs_1_, ...), custom_call_target="tpu_custom_call" | custom-call | flops 25769803776 | bytes 41943040 | tf_op jit(solution)/shard_map/pallas_call | solution.py:167
  220.1 11.9 %collective-permute-done.7.refs_0_ = f32[512,1024]{1,0:T(8,128)} collective-permute-done((f32[512,1024]{1,0:T(8,128)}, f32[512,1024]{1,0:T(8,128)}, u32[]{:S(2)}, u32[]{:S(2)}) %collective-permute-start.7) | collective-permute-done | bytes 2097184 | tf_op jit(solution)/shard_map/ppermute | solution.py:309
  232.0 7.7 %shard_map.158 = (f32[2,4,64,1024]{3,2,1,0:T(8,128)S(1)}, f32[2,4,64,1024]{3,2,1,0:T(8,128)}) custom-call(s32[3]{0:T(128)S(1)} %get-tuple-element.120.where, f32[512,1024]{1,0:T(8,128)} %get-tuple-element.52.refs_0_, f32[512,2048]{1,0:T(8,128)} %get-tuple-element.46.refs_1_.refs_4_.refs_2_), custom_call_target="tpu_custom_call" | custom-call | tf_op jit(solution)/shard_map/pallas_call | solution.py:222
  239.7 7.9 %shard_map.159 = (f32[2,4,64,1024]{3,2,1,0:T(8,128)S(1)}, f32[2,4,64,1024]{3,2,1,0:T(8,128)}) custom-call(s32[3]{0:T(128)S(1)} %get-tuple-element.119.where, f32[512,1024]{1,0:T(8,128)} %get-tuple-element.45.refs_0_, f32[512,2048]{1,0:T(8,128)} %get-tuple-element.46.refs_1_.refs_4_.refs_2_), custom_call_target="tpu_custom_call" | custom-call | tf_op jit(solution)/shard_map/pallas_call | solution.py:222
  268.1 16.2 %collective-permute-done.11 = f32[2,2,2,64,512]{4,3,2,1,0:T(8,128)} collective-permute-done((f32[2,2,2,64,512]{4,3,2,1,0:T(8,128)}, f32[2,2,2,64,512]{4,3,2,1,0:T(8,128)}, u32[]{:S(2)}, u32[]{:S(2)}) %collective-permute-start.11) | collective-permute-done | bytes 1048608 | tf_op jit(solution)/shard_map/ppermute | solution.py:98
  293.2 6.2 %collective-permute-done.12 = f32[2,2,64,512]{3,2,1,0:T(8,128)S(1)} collective-permute-done((f32[2,2,64,512]{3,2,1,0:T(8,128)S(1)}, f32[2,2,64,512]{3,2,1,0:T(8,128)S(1)}, u32[]{:S(2)}, u32[]{:S(2)}) %collective-permute-start.12) | collective-permute-done | bytes 524320 | tf_op jit(solution)/shard_map/ppermute | solution.py:98
  302.4 9.9 %collective-permute-done.8.refs_2_.refs_6_.refs_4_ = f32[512,1024]{1,0:T(8,128)S(1)} collective-permute-done((f32[512,1024]{1,0:T(8,128)}, f32[512,1024]{1,0:T(8,128)S(1)}, u32[]{:S(2)}, u32[]{:S(2)}) %collective-permute-start.8) | collective-permute-done | bytes 2097184 | tf_op jit(solution)/shard_map/ppermute | solution.py:309
  313.6 8.0 %shard_map.163 = (f32[2,4,64,1024]{3,2,1,0:T(8,128)S(1)}, f32[2,4,64,1024]{3,2,1,0:T(8,128)}) custom-call(s32[3]{0:T(128)S(1)} %add_add_fusion.1.where, f32[512,1024]{1,0:T(8,128)} %collective-permute-done.7.refs_0_, f32[512,1024]{1,0:T(8,128)} %collective-permute-done.6.refs_1_, f32[512,2048]{1,0:T(8,128)} %get-tuple-element.46.refs_1_.refs_4_.refs_2_, ...), custom_call_target="tpu_custom_call" | custom-call | tf_op jit(solution)/shard_map/pallas_call | solution.py:222
  321.7 8.1 %shard_map.162 = (f32[2,4,64,1024]{3,2,1,0:T(8,128)S(1)}, f32[2,4,64,1024]{3,2,1,0:T(8,128)}) custom-call(s32[3]{0:T(128)S(1)} %add_add_fusion.where, f32[512,1024]{1,0:T(8,128)} %collective-permute-done.5.refs_5_.refs_0_, f32[512,1024]{1,0:T(8,128)} %collective-permute-done.4.refs_2_.refs_1_, f32[512,2048]{1,0:T(8,128)} %get-tuple-element.46.refs_1_.refs_4_.refs_2_, ...), custom_call_target="tpu_custom_call" | custom-call | tf_op jit(solution)/shard_map/pallas_call | solution.py:222
  339.8 8.1 %shard_map.161 = (f32[2,4,64,1024]{3,2,1,0:T(8,128)S(1)}, f32[2,4,64,1024]{3,2,1,0:T(8,128)S(1)}) custom-call(s32[3]{0:T(128)S(1)} %pad_add_fusion.4.where, f32[512,1024]{1,0:T(8,128)} %collective-permute-done.7.refs_0_, f32[512,1024]{1,0:T(8,128)} %collective-permute-done.6.refs_1_, f32[512,1024]{1,0:T(8,128)} %copy-done.6, ...), custom_call_target="tpu_custom_call" | custom-call | tf_op jit(solution)/shard_map/pallas_call | solution.py:222
  348.5 8.7 %shard_map.160 = (f32[2,4,64,1024]{3,2,1,0:T(8,128)S(1)}, f32[2,4,64,1024]{3,2,1,0:T(8,128)S(1)}) custom-call(s32[3]{0:T(128)S(1)} %pad_add_fusion.3.where, f32[512,1024]{1,0:T(8,128)} %copy-done.8, f32[512,1024]{1,0:T(8,128)} %copy-done.9, f32[512,1024]{1,0:T(8,128)} %copy-done.6, f32[512,1024]{1,0:T(8,128)} %collective-permute-done.15.refs_3_.refs_5_, ...), custom_call_target="tpu_custom_call" | custom-call | tf_op jit(solution)/shard_map/pallas_call | solution.py:222
  370.9 5.4 collective-permute-start.35
  383.8 12.2 %collective-permute-done.21 = f32[2,2,2,64,512]{4,3,2,1,0:T(8,128)S(1)} collective-permute-done((f32[2,2,2,64,512]{4,3,2,1,0:T(8,128)S(1)}, f32[2,2,2,64,512]{4,3,2,1,0:T(8,128)S(1)}, u32[]{:S(2)}, u32[]{:S(2)}) %collective-permute-start.21) | collective-permute-done | bytes 1048608 | tf_op jit(solution)/shard_map/ppermute | solution.py:98
  396.9 8.6 %collective-permute-done.23 = f32[2,2,2,64,512]{4,3,2,1,0:T(8,128)S(1)} collective-permute-done((f32[2,2,2,64,512]{4,3,2,1,0:T(8,128)S(1)}, f32[2,2,2,64,512]{4,3,2,1,0:T(8,128)S(1)}, u32[]{:S(2)}, u32[]{:S(2)}) %collective-permute-start.23) | collective-permute-done | bytes 1048608 | tf_op jit(solution)/shard_map/ppermute | solution.py:98
  406.1 10.7 %collective-permute-done.22 = f32[2,2,64,512]{3,2,1,0:T(8,128)S(1)} collective-permute-done((f32[2,2,64,512]{3,2,1,0:T(8,128)S(1)}, f32[2,2,64,512]{3,2,1,0:T(8,128)S(1)}, u32[]{:S(2)}, u32[]{:S(2)}) %collective-permute-start.22) | collective-permute-done | bytes 524320 | tf_op jit(solution)/shard_map/ppermute | solution.py:98
  416.8 10.4 %collective-permute-done.24 = f32[2,2,64,512]{3,2,1,0:T(8,128)S(1)} collective-permute-done((f32[2,2,64,512]{3,2,1,0:T(8,128)S(1)}, f32[2,2,64,512]{3,2,1,0:T(8,128)S(1)}, u32[]{:S(2)}, u32[]{:S(2)}) %collective-permute-start.24) | collective-permute-done | bytes 524320 | tf_op jit(solution)/shard_map/ppermute | solution.py:98
  430.3 6.4 %collective-permute-done.28 = f32[2,2,2,64,512]{4,3,2,1,0:T(8,128)S(1)} collective-permute-done((f32[2,2,2,64,512]{4,3,2,1,0:T(8,128)S(1)}, f32[2,2,2,64,512]{4,3,2,1,0:T(8,128)S(1)}, u32[]{:S(2)}, u32[]{:S(2)}) %collective-permute-start.28) | collective-permute-done | bytes 1048608 | tf_op jit(solution)/shard_map/ppermute | solution.py:98
  436.9 8.4 %collective-permute-done.26 = f32[2,64,1024]{2,1,0:T(8,128)S(1)} collective-permute-done((f32[2,64,1024]{2,1,0:T(8,128)S(1)}, f32[2,64,1024]{2,1,0:T(8,128)S(1)}, u32[]{:S(2)}, u32[]{:S(2)}) %collective-permute-start.26) | collective-permute-done | bytes 524320 | tf_op jit(solution)/shard_map/ppermute | solution.py:393
  445.4 8.0 %collective-permute-done.25 = f32[2,64,1024]{2,1,0:T(8,128)S(1)} collective-permute-done((f32[2,64,1024]{2,1,0:T(8,128)S(1)}, f32[2,64,1024]{2,1,0:T(8,128)S(1)}, u32[]{:S(2)}, u32[]{:S(2)}) %collective-permute-start.25) | collective-permute-done | bytes 524320 | tf_op jit(solution)/shard_map/ppermute | solution.py:393
  456.2 8.0 %collective-permute-done.27 = f32[2,2,64,512]{3,2,1,0:T(8,128)S(1)} collective-permute-done((f32[2,2,64,512]{3,2,1,0:T(8,128)S(1)}, f32[2,2,64,512]{3,2,1,0:T(8,128)S(1)}, u32[]{:S(2)}, u32[]{:S(2)}) %collective-permute-start.27) | collective-permute-done | bytes 524320 | tf_op jit(solution)/shard_map/ppermute | solution.py:98
  468.6 11.3 %collective-permute-done.30 = f32[2,64,1024]{2,1,0:T(8,128)S(1)} collective-permute-done((f32[2,64,1024]{2,1,0:T(8,128)S(1)}, f32[2,64,1024]{2,1,0:T(8,128)S(1)}, u32[]{:S(2)}, u32[]{:S(2)}) %collective-permute-start.30) | collective-permute-done | bytes 524320 | tf_op jit(solution)/shard_map/ppermute | solution.py:393
  480.1 8.1 %collective-permute-done.31 = f32[2,64,1024]{2,1,0:T(8,128)S(1)} collective-permute-done((f32[2,64,1024]{2,1,0:T(8,128)S(1)}, f32[2,64,1024]{2,1,0:T(8,128)S(1)}, u32[]{:S(2)}, u32[]{:S(2)}) %collective-permute-start.31) | collective-permute-done | bytes 524320 | tf_op jit(solution)/shard_map/ppermute | solution.py:393
  492.0 4.8 all-to-all-start
  496.9 49.0 %all-to-all-done.found_ref = f32[8,2,64,1024]{3,2,1,0:T(8,128)} async-done(((f32[8,2,64,1024]{3,2,1,0:T(8,128)}), f32[8,2,64,1024]{3,2,1,0:T(8,128)}, u32[]{:S(2)}, u32[]{:S(2)}) %all-to-all-start) | async-done | bytes 4194336 | tf_op jit(solution)/shard_map/all_to_all | solution.py:427
  548.1 5.5 shard_map.164
  553.6 4.6 fusion.2
  (204 shorter events, 117.3 us)
Async XLA Ops:
  7.2 175.2 %all-gather.2.cloned.1.call-start = ((), (), s32[]{:S(2)}) async-start(), calls=%async_computation.1 | async-start | bytes 37748736 | tf_op jit(solution)/shard_map/all_gather | solution.py:282
  17.2 50.1 %collective-permute-start = (f32[512,1024]{1,0:T(8,128)}, f32[512,1024]{1,0:T(8,128)S(1)}, u32[]{:S(2)}, u32[]{:S(2)}) collective-permute-start(f32[512,1024]{1,0:T(8,128)} %own_ref.1), channel_id=1, source_target_pairs={{0,1},{1,2},{2,3},{4,5},{5,6},{6,7},{8,9},{9,10},{10,11},{12,13},{... | collective-permute-start | bytes 6291464 | tf_op jit(solution)/shard_map/ppermute | solution.py:309
  22.3 49.3 %collective-permute-start.1 = (f32[512,1024]{1,0:T(8,128)}, f32[512,1024]{1,0:T(8,128)}, u32[]{:S(2)}, u32[]{:S(2)}) collective-permute-start(f32[512,1024]{1,0:T(8,128)} %own_ref.1), channel_id=1, source_target_pairs={{1,0},{2,1},{3,2},{5,4},{6,5},{7,6},{9,8},{10,9},{11,10},{13,12},{... | collective-permute-start | bytes 6291464 | tf_op jit(solution)/shard_map/ppermute | solution.py:309
  73.6 47.0 %collective-permute-start.2 = (f32[512,1024]{1,0:T(8,128)S(1)}, f32[512,1024]{1,0:T(8,128)S(1)}, u32[]{:S(2)}, u32[]{:S(2)}) collective-permute-start(f32[512,1024]{1,0:T(8,128)S(1)} %broadcast_select_fusion.2), channel_id=1, source_target_pairs={{0,1},{1,2},{2,3},{4,5},{5,6},{6,7},{8,9},{9,10},{10,11},{12,13},{... | collective-permute-start | bytes 6291464 | tf_op jit(solution)/shard_map/ppermute | solution.py:309
  77.1 47.8 %collective-permute-start.3 = (f32[512,1024]{1,0:T(8,128)S(1)}, f32[512,1024]{1,0:T(8,128)S(1)}, u32[]{:S(2)}, u32[]{:S(2)}) collective-permute-start(f32[512,1024]{1,0:T(8,128)S(1)} %broadcast_select_fusion.3), channel_id=1, source_target_pairs={{1,0},{2,1},{3,2},{5,4},{6,5},{7,6},{9,8},{10,9},{11,10},{13,12},{... | collective-permute-start | bytes 6291464 | tf_op jit(solution)/shard_map/ppermute | solution.py:309
  129.0 44.5 %collective-permute-start.4 = (f32[512,1024]{1,0:T(8,128)}, f32[512,1024]{1,0:T(8,128)}, u32[]{:S(2)}, u32[]{:S(2)}) collective-permute-start(f32[512,1024]{1,0:T(8,128)} %broadcast_select_fusion), channel_id=1, source_target_pairs={{0,1},{1,2},{2,3},{4,5},{5,6},{6,7},{8,9},{9,10},{10,11},{12,13},{... | collective-permute-start | bytes 6291464 | tf_op jit(solution)/shard_map/ppermute | solution.py:309
  131.6 47.3 %collective-permute-start.5 = (f32[512,1024]{1,0:T(8,128)}, f32[512,1024]{1,0:T(8,128)}, u32[]{:S(2)}, u32[]{:S(2)}) collective-permute-start(f32[512,1024]{1,0:T(8,128)} %broadcast_select_fusion.1), channel_id=1, source_target_pairs={{1,0},{2,1},{3,2},{5,4},{6,5},{7,6},{9,8},{10,9},{11,10},{13,12},{... | collective-permute-start | bytes 6291464 | tf_op jit(solution)/shard_map/ppermute | solution.py:309
  178.9 41.2 %collective-permute-start.6 = (f32[512,1024]{1,0:T(8,128)}, f32[512,1024]{1,0:T(8,128)}, u32[]{:S(2)}, u32[]{:S(2)}) collective-permute-start(f32[512,1024]{1,0:T(8,128)} %collective-permute-done.4.refs_2_.refs_1_), channel_id=1, source_target_pairs={{1,2},{2,3},{5,6},{6,7},{9,10},{10,11},{13,14},{14,15},{17,18},{18... | collective-permute-start | bytes 6291464 | tf_op jit(solution)/shard_map/ppermute | solution.py:309
  180.9 51.1 %collective-permute-start.7 = (f32[512,1024]{1,0:T(8,128)}, f32[512,1024]{1,0:T(8,128)}, u32[]{:S(2)}, u32[]{:S(2)}) collective-permute-start(f32[512,1024]{1,0:T(8,128)} %collective-permute-done.5.refs_5_.refs_0_), channel_id=1, source_target_pairs={{1,0},{2,1},{5,4},{6,5},{9,8},{10,9},{13,12},{14,13},{17,16},{18,1... | collective-permute-start | bytes 6291464 | tf_op jit(solution)/shard_map/ppermute | solution.py:309
  258.5 25.8 %collective-permute-start.11 = (f32[2,2,2,64,512]{4,3,2,1,0:T(8,128)}, f32[2,2,2,64,512]{4,3,2,1,0:T(8,128)}, u32[]{:S(2)}, u32[]{:S(2)}) collective-permute-start(f32[2,2,2,64,512]{4,3,2,1,0:T(8,128)} %dynamic-slice_bitcast_fusion.2), channel_id=1, source_target_pairs={{0,8},{4,12},{8,0},{12,4},{16,24},{20,28},{24,16},{28,20},{1,9},{5... | collective-permute-start | bytes 3145736 | tf_op jit(solution)/shard_map/ppermute | solution.py:98
  261.4 26.2 %collective-permute-start.13 = (f32[2,2,2,64,512]{4,3,2,1,0:T(8,128)}, f32[2,2,2,64,512]{4,3,2,1,0:T(8,128)}, u32[]{:S(2)}, u32[]{:S(2)}) collective-permute-start(f32[2,2,2,64,512]{4,3,2,1,0:T(8,128)} %bitcast.139), channel_id=1, source_target_pairs={{0,16},{4,20},{8,24},{12,28},{16,0},{20,4},{24,8},{28,12},{1,17},{... | collective-permute-start | bytes 3145736 | tf_op jit(solution)/shard_map/ppermute | solution.py:98
  262.9 49.4 %collective-permute-start.8 = (f32[512,1024]{1,0:T(8,128)}, f32[512,1024]{1,0:T(8,128)S(1)}, u32[]{:S(2)}, u32[]{:S(2)}) collective-permute-start(f32[512,1024]{1,0:T(8,128)} %get-tuple-element.45.refs_0_), channel_id=1, source_target_pairs={{1,0},{2,1},{5,4},{6,5},{9,8},{10,9},{13,12},{14,13},{17,16},{18,1... | collective-permute-start | bytes 6291464 | tf_op jit(solution)/shard_map/ppermute | solution.py:309
  264.2 49.5 %collective-permute-start.15 = (f32[512,1024]{1,0:T(8,128)}, f32[512,1024]{1,0:T(8,128)}, u32[]{:S(2)}, u32[]{:S(2)}) collective-permute-start(f32[512,1024]{1,0:T(8,128)} %get-tuple-element.52.refs_0_), channel_id=1, source_target_pairs={{1,2},{2,3},{5,6},{6,7},{9,10},{10,11},{13,14},{14,15},{17,18},{18... | collective-permute-start | bytes 6291464 | tf_op jit(solution)/shard_map/ppermute | solution.py:309
  286.0 13.4 %collective-permute-start.12 = (f32[2,2,64,512]{3,2,1,0:T(8,128)S(1)}, f32[2,2,64,512]{3,2,1,0:T(8,128)S(1)}, u32[]{:S(2)}, u32[]{:S(2)}) collective-permute-start(f32[2,2,64,512]{3,2,1,0:T(8,128)S(1)} %dynamic-slice_bitcast_fusion.8), channel_id=1, source_target_pairs={{0,16},{4,20},{8,24},{12,28},{16,0},{20,4},{24,8},{28,12},{1,17},{... | collective-permute-start | bytes 1572872 | tf_op jit(solution)/shard_map/ppermute | solution.py:98
  289.1 13.2 %collective-permute-start.14 = (f32[2,2,64,512]{3,2,1,0:T(8,128)S(1)}, f32[2,2,64,512]{3,2,1,0:T(8,128)S(1)}, u32[]{:S(2)}, u32[]{:S(2)}) collective-permute-start(f32[2,2,64,512]{3,2,1,0:T(8,128)S(1)} %dynamic-slice_bitcast_fusion.7), channel_id=1, source_target_pairs={{0,8},{4,12},{8,0},{12,4},{16,24},{20,28},{24,16},{28,20},{1,9},{5... | collective-permute-start | bytes 1572872 | tf_op jit(solution)/shard_map/ppermute | solution.py:98
  321.7 43.7 %collective-permute-start.20 = (f32[2,4,64,1024]{3,2,1,0:T(8,128)}, f32[2,4,64,1024]{3,2,1,0:T(8,128)}, u32[]{:S(2)}, u32[]{:S(2)}) collective-permute-start(f32[2,4,64,1024]{3,2,1,0:T(8,128)} %get-tuple-element.63), channel_id=1, source_target_pairs={{0,4},{4,0},{8,12},{12,8},{16,20},{20,16},{24,28},{28,24},{1,5},{5... | collective-permute-start | bytes 6291464 | tf_op jit(solution)/shard_map/ppermute | solution.py:103
  331.1 36.5 %collective-permute-start.19 = (f32[2,4,64,1024]{3,2,1,0:T(8,128)}, f32[2,4,64,1024]{3,2,1,0:T(8,128)}, u32[]{:S(2)}, u32[]{:S(2)}) collective-permute-start(f32[2,4,64,1024]{3,2,1,0:T(8,128)} %get-tuple-element.59), channel_id=1, source_target_pairs={{0,4},{4,0},{8,12},{12,8},{16,20},{20,16},{24,28},{28,24},{1,5},{5... | collective-permute-start | bytes 6291464 | tf_op jit(solution)/shard_map/ppermute | solution.py:103
  339.7 18.2 %collective-permute-start.32 = (f32[2,1024]{1,0:T(2,128)S(1)}, f32[2,1024]{1,0:T(2,128)S(1)}, u32[]{:S(2)}, u32[]{:S(2)}) collective-permute-start(f32[2,1024]{1,0:T(2,128)S(1)} %add.201), channel_id=1, source_target_pairs={{0,4},{4,0},{8,12},{12,8},{16,20},{20,16},{24,28},{28,24},{1,5},{5... | collective-permute-start | bytes 24584 | tf_op jit(solution)/shard_map/ppermute | solution.py:333
  347.9 33.0 %collective-permute-start.17 = (f32[2,4,64,1024]{3,2,1,0:T(8,128)S(1)}, f32[2,4,64,1024]{3,2,1,0:T(8,128)}, u32[]{:S(2)}, u32[]{:S(2)}) collective-permute-start(f32[2,4,64,1024]{3,2,1,0:T(8,128)S(1)} %get-tuple-element.57), channel_id=1, source_target_pairs={{0,4},{4,0},{8,12},{12,8},{16,20},{20,16},{24,28},{28,24},{1,5},{5... | collective-permute-start | bytes 6291464 | tf_op jit(solution)/shard_map/ppermute | solution.py:103
  357.2 25.9 %collective-permute-start.16 = (f32[2,4,64,1024]{3,2,1,0:T(8,128)S(1)}, f32[2,4,64,1024]{3,2,1,0:T(8,128)S(1)}, u32[]{:S(2)}, u32[]{:S(2)}) collective-permute-start(f32[2,4,64,1024]{3,2,1,0:T(8,128)S(1)} %get-tuple-element.55), channel_id=1, source_target_pairs={{0,4},{4,0},{8,12},{12,8},{16,20},{20,16},{24,28},{28,24},{1,5},{5... | collective-permute-start | bytes 6291464 | tf_op jit(solution)/shard_map/ppermute | solution.py:103
  369.9 26.2 %collective-permute-start.21 = (f32[2,2,2,64,512]{4,3,2,1,0:T(8,128)S(1)}, f32[2,2,2,64,512]{4,3,2,1,0:T(8,128)S(1)}, u32[]{:S(2)}, u32[]{:S(2)}) collective-permute-start(f32[2,2,2,64,512]{4,3,2,1,0:T(8,128)S(1)} %dynamic-slice_bitcast_fusion), channel_id=1, source_target_pairs={{0,8},{4,12},{8,0},{12,4},{16,24},{20,28},{24,16},{28,20},{1,9},{5... | collective-permute-start | bytes 3145736 | tf_op jit(solution)/shard_map/ppermute | solution.py:98
  379.4 26.2 %collective-permute-start.23 = (f32[2,2,2,64,512]{4,3,2,1,0:T(8,128)S(1)}, f32[2,2,2,64,512]{4,3,2,1,0:T(8,128)S(1)}, u32[]{:S(2)}, u32[]{:S(2)}) collective-permute-start(f32[2,2,2,64,512]{4,3,2,1,0:T(8,128)S(1)} %fusion.10), channel_id=1, source_target_pairs={{0,16},{4,20},{8,24},{12,28},{16,0},{20,4},{24,8},{28,12},{1,17},{... | collective-permute-start | bytes 3145736 | tf_op jit(solution)/shard_map/ppermute | solution.py:98
  383.8 45.0 %collective-permute-start.18 = (f32[2,2,2,64,512]{4,3,2,1,0:T(8,128)S(1)}, f32[2,2,2,64,512]{4,3,2,1,0:T(8,128)S(1)}, u32[]{:S(2)}, u32[]{:S(2)}) collective-permute-start(f32[2,2,2,64,512]{4,3,2,1,0:T(8,128)S(1)} %dynamic-slice_bitcast_fusion.1), channel_id=1, source_target_pairs={{0,8},{4,12},{8,0},{12,4},{16,24},{20,28},{24,16},{28,20},{1,9},{5... | collective-permute-start | bytes 3145736 | tf_op jit(solution)/shard_map/ppermute | solution.py:98
  396.3 20.4 %collective-permute-start.22 = (f32[2,2,64,512]{3,2,1,0:T(8,128)S(1)}, f32[2,2,64,512]{3,2,1,0:T(8,128)S(1)}, u32[]{:S(2)}, u32[]{:S(2)}) collective-permute-start(f32[2,2,64,512]{3,2,1,0:T(8,128)S(1)} %dynamic-slice_bitcast_fusion.6), channel_id=1, source_target_pairs={{0,16},{4,20},{8,24},{12,28},{16,0},{20,4},{24,8},{28,12},{1,17},{... | collective-permute-start | bytes 1572872 | tf_op jit(solution)/shard_map/ppermute | solution.py:98
  405.8 21.5 %collective-permute-start.24 = (f32[2,2,64,512]{3,2,1,0:T(8,128)S(1)}, f32[2,2,64,512]{3,2,1,0:T(8,128)S(1)}, u32[]{:S(2)}, u32[]{:S(2)}) collective-permute-start(f32[2,2,64,512]{3,2,1,0:T(8,128)S(1)} %dynamic-slice_bitcast_fusion.5), channel_id=1, source_target_pairs={{0,8},{4,12},{8,0},{12,4},{16,24},{20,28},{24,16},{28,20},{1,9},{5... | collective-permute-start | bytes 1572872 | tf_op jit(solution)/shard_map/ppermute | solution.py:98
  406.0 30.7 %collective-permute-start.28 = (f32[2,2,2,64,512]{4,3,2,1,0:T(8,128)S(1)}, f32[2,2,2,64,512]{4,3,2,1,0:T(8,128)S(1)}, u32[]{:S(2)}, u32[]{:S(2)}) collective-permute-start(f32[2,2,2,64,512]{4,3,2,1,0:T(8,128)S(1)} %fusion.15), channel_id=1, source_target_pairs={{0,16},{4,20},{8,24},{12,28},{16,0},{20,4},{24,8},{28,12},{1,17},{... | collective-permute-start | bytes 3145736 | tf_op jit(solution)/shard_map/ppermute | solution.py:98
  427.4 17.9 %collective-permute-start.26 = (f32[2,64,1024]{2,1,0:T(8,128)S(1)}, f32[2,64,1024]{2,1,0:T(8,128)S(1)}, u32[]{:S(2)}, u32[]{:S(2)}) collective-permute-start(f32[2,64,1024]{2,1,0:T(8,128)S(1)} %get-tuple-element.91), channel_id=1, source_target_pairs={{1,3},{2,0},{5,7},{6,4},{9,11},{10,8},{13,15},{14,12},{17,19},{18,... | collective-permute-start | bytes 1572872 | tf_op jit(solution)/shard_map/ppermute | solution.py:393
  429.0 24.4 %collective-permute-start.25 = (f32[2,64,1024]{2,1,0:T(8,128)S(1)}, f32[2,64,1024]{2,1,0:T(8,128)S(1)}, u32[]{:S(2)}, u32[]{:S(2)}) collective-permute-start(f32[2,64,1024]{2,1,0:T(8,128)S(1)} %get-tuple-element.92), channel_id=1, source_target_pairs={{1,3},{2,0},{5,7},{6,4},{9,11},{10,8},{13,15},{14,12},{17,19},{18,... | collective-permute-start | bytes 1572872 | tf_op jit(solution)/shard_map/ppermute | solution.py:393
  454.0 11.4 %collective-permute-start.29 = (f32[2,2,64,512]{3,2,1,0:T(8,128)S(1)}, f32[2,2,64,512]{3,2,1,0:T(8,128)S(1)}, u32[]{:S(2)}, u32[]{:S(2)}) collective-permute-start(f32[2,2,64,512]{3,2,1,0:T(8,128)S(1)} %dynamic-slice_bitcast_fusion.3), channel_id=1, source_target_pairs={{0,8},{4,12},{8,0},{12,4},{16,24},{20,28},{24,16},{28,20},{1,9},{5... | collective-permute-start | bytes 1572872 | tf_op jit(solution)/shard_map/ppermute | solution.py:98
  465.7 14.3 %collective-permute-start.30 = (f32[2,64,1024]{2,1,0:T(8,128)S(1)}, f32[2,64,1024]{2,1,0:T(8,128)S(1)}, u32[]{:S(2)}, u32[]{:S(2)}) collective-permute-start(f32[2,64,1024]{2,1,0:T(8,128)S(1)} %bitcast.157), channel_id=1, source_target_pairs={{1,0},{2,3},{0,1},{3,2},{5,4},{6,7},{4,5},{7,6},{9,8},{10,11},{8,9... | collective-permute-start | bytes 1572872 | tf_op jit(solution)/shard_map/ppermute | solution.py:393
  465.9 22.3 %collective-permute-start.31 = (f32[2,64,1024]{2,1,0:T(8,128)S(1)}, f32[2,64,1024]{2,1,0:T(8,128)S(1)}, u32[]{:S(2)}, u32[]{:S(2)}) collective-permute-start(f32[2,64,1024]{2,1,0:T(8,128)S(1)} %bitcast.156), channel_id=1, source_target_pairs={{0,3},{3,0},{1,2},{2,1},{4,7},{7,4},{5,6},{6,5},{8,11},{11,8},{9,1... | collective-permute-start | bytes 1572872 | tf_op jit(solution)/shard_map/ppermute | solution.py:393
  492.0 53.9 %all-to-all-start = ((f32[8,2,64,1024]{3,2,1,0:T(8,128)}), f32[8,2,64,1024]{3,2,1,0:T(8,128)}, u32[]{:S(2)}, u32[]{:S(2)}) async-start(f32[8,2,64,1024]{3,2,1,0:T(8,128)} %pad_maximum_fusion.3), calls=%async_computation | async-start | bytes 8388608 | tf_op jit(solution)/shard_map/all_to_all | solution.py:427
  (28 other events, 129.0 us)
Sparse Core Ops, SparseCore 0:
  17.4 163.4 all-gather.1
